TPU v7x, 32 devices: a whole 2x2x4 slice. The times are simulated.
32 devices in a mesh: row: 4 (over y, x), col: 8 (over z, core).
Axes of the slice: x: 2, y: 2, z: 4, core: 2. Of those that a mesh axis runs over, the one named last changes fastest.
Arguments:
- tokens_in: bfloat16 [4096, 5120], P('row', 'col'), may hold values from -6 to 6
- token_grad: bfloat16 [4096, 5120], P('row', 'col'), may hold values from -6 to 6
- gate_gain: float32 [5120], replicated, may hold values from -4 to 4
- inner_weight: bfloat16 [5120, 13824], P(None, 'col'), may hold values from -0.078125 to 0.078125
- inner_bias: float32 [13824], P('col'), may hold values from -4 to 4
- outer_weight: bfloat16 [5120, 13824], P(None, 'col'), may hold values from -0.0546875 to 0.0546875
- inner_down: bfloat16 [5120, 64], replicated, may hold values from -0.078125 to 0.078125
- inner_up: bfloat16 [64, 13824], P(None, 'col'), may hold values from -0.1796875 to 0.1796875
- outer_down: bfloat16 [13824, 64], P('col'), may hold values from -0.0546875 to 0.0546875
- outer_up: bfloat16 [64, 5120], replicated, may hold values from -0.1796875 to 0.1796875
Outputs:
- tokens_grad: bfloat16 [4096, 5120], P('row', 'col')
- inner_down_grad: float32 [5120, 64], P('col')
- inner_up_grad: float32 [64, 13824], P(None, 'col')
- outer_down_grad: float32 [13824, 64], P('col')
- outer_up_grad: float32 [64, 5120], P(None, 'col')
All inputs are finite; a program needn't handle non-finite values.
Results may differ from a plain program's by a relative error of at most 0.023.
Values may be sent and summed in bfloat16 or wider, within the bound.
No kernel may reach another device: no remote copies, remote signals or barrier semaphores. Data moves between devices by JAX's collectives and lax.ppermute only.
A program may use at most 128 MiB of HBM per device.

v0:
```python
import functools
import math

import jax
import jax.numpy as jnp
from jax import lax
from jax.experimental import pallas as pl
from jax.experimental.pallas import tpu as pltpu
from jax.sharding import PartitionSpec as P

SLOPE_SCALE = 0.7978845608028654
CUBIC = 0.044715
F32 = jnp.float32
BF16 = jnp.bfloat16
LANES = 128
COLS = 256
VMEM_BYTES = 52 * 1024 * 1024
COST = pl.CostEstimate(flops=20_000_000_000, bytes_accessed=36_000_000, transcendentals=0)
SPLIT = (512, 512)


def dot_nn(left, right):
    return jnp.dot(left, right, preferred_element_type=F32)


def dot_nt(left, right):
    return lax.dot_general(left, right, (((1,), (1,)), ((), ())), preferred_element_type=F32)


def dot_tn(left, right):
    return lax.dot_general(left, right, (((0,), (0,)), ((), ())), preferred_element_type=F32)


def hidden_kernel(
    ff, both_ref, inner_ref, outer_ref, bias_ref, up_ref, down_lo_ref, down_hi_ref,
    grad_ref, low_ref, grads_ref, pre_acc, hid_acc, hidden_ref,
):
    step = pl.program_id(0)
    _, _, tokens, width = both_ref.shape
    padded = pre_acc.shape[1]

    def product(which, weight_ref):
        first, second = both_ref[0, which], both_ref[1, which]
        if width % LANES == 0:
            return dot_nt(jnp.concatenate([first, second], axis=1), weight_ref[...])
        return dot_nt(first, weight_ref[:, :width]) + dot_nt(second, weight_ref[:, width:])

    @pl.when(step == 0)
    def _():
        pre_acc[...] = product(0, inner_ref)
        hid_acc[...] = product(1, outer_ref)

    @pl.when(step > 0)
    def _():
        pre_acc[...] += product(0, inner_ref)
        hid_acc[...] += product(1, outer_ref)

    @pl.when(step == pl.num_programs(0) - 1)
    def _():
        tail = slice(padded - LANES, padded)
        inner_low = pre_acc[:, tail].astype(BF16)
        grad_low = hid_acc[:, tail].astype(BF16)
        rank = LANES // 2
        low = jnp.zeros((tokens, LANES), F32)
        for start in range(0, padded, COLS):
            cols = slice(start, start + COLS)
            pre = pre_acc[:, cols] + dot_nn(inner_low, up_ref[:, cols]) + bias_ref[:, cols]
            square = pre * pre
            tangent = jnp.tanh(SLOPE_SCALE * pre * (1.0 + CUBIC * square))
            half = 0.5 + 0.5 * tangent
            hidden = (pre * half).astype(BF16)
            slope = half + 0.5 * pre * (1.0 - tangent * tangent) * (
                SLOPE_SCALE + 3.0 * CUBIC * SLOPE_SCALE * square
            )
            grad_hidden = hid_acc[:, cols] + dot_nn(grad_low, down_hi_ref[:, cols])
            grad_pre = (grad_hidden * slope).astype(BF16)
            hidden_ref[:, cols] = hidden
            grad_ref[:, cols] = grad_pre
        low = dot_nt(hidden_ref[...], down_lo_ref[...]) + dot_nt(grad_ref[...], up_ref[...])
        low = low.astype(BF16)
        low_ref[...] = low
        grads_ref[:rank] = dot_tn(inner_low, grad_ref[...])[rank:]
        grads_ref[rank:] = dot_tn(grad_low, hidden_ref[...])[rank:]
        lane = lax.broadcasted_iota(jnp.int32, (tokens, LANES), 1)
        keep = lane + (padded - LANES) < ff
        filled = jnp.where(lane >= rank, low, jnp.zeros_like(low))
        grad_ref[:, tail] = jnp.where(keep, grad_ref[:, tail], filled)
        for start in range(0, padded - LANES, LANES):
            if start + LANES > ff:
                here = slice(start, start + LANES)
                grad_ref[:, here] = jnp.where(lane + start < ff, grad_ref[:, here], jnp.zeros_like(low))


def hidden_call(both, inner_cat, outer_cat, bias, up, down_lo, down_hi, ff):
    devices, _, tokens, width = both.shape
    padded = inner_cat.shape[0]
    steps = devices // 2
    whole = lambda k: (0, 0)
    return pl.pallas_call(
        functools.partial(hidden_kernel, ff),
        grid=(steps,),
        in_specs=[
            pl.BlockSpec((2, 2, tokens, width), lambda k: (k, 0, 0, 0)),
            pl.BlockSpec((padded, 2 * width), lambda k: (0, k)),
            pl.BlockSpec((padded, 2 * width), lambda k: (0, k)),
            pl.BlockSpec((1, padded), whole),
            pl.BlockSpec((LANES, padded), whole),
            pl.BlockSpec((LANES, padded), whole),
            pl.BlockSpec((LANES, padded), whole),
        ],
        out_specs=[
            pl.BlockSpec((tokens, padded), whole),
            pl.BlockSpec((tokens, LANES), whole),
            pl.BlockSpec((LANES, padded), whole),
        ],
        out_shape=[
            jax.ShapeDtypeStruct((tokens, padded), BF16),
            jax.ShapeDtypeStruct((tokens, LANES), BF16),
            jax.ShapeDtypeStruct((LANES, padded), F32),
        ],
        scratch_shapes=[
            pltpu.VMEM((tokens, padded), F32),
            pltpu.VMEM((tokens, padded), F32),
            pltpu.VMEM((tokens, padded), BF16),
        ],
        compiler_params=pltpu.CompilerParams(vmem_limit_bytes=VMEM_BYTES),
        cost_estimate=COST,
    )(both, inner_cat, outer_cat, bias, up, down_lo, down_hi)


def share_kernel(grad_ref, weight_ref, share_ref):
    width = share_ref.shape[2]
    if width % LANES == 0:
        share = dot_nn(grad_ref[...], weight_ref[...]).astype(BF16)
        share_ref[0], share_ref[1] = share[:, :width], share[:, width:]
    else:
        for part in (0, 1):
            here = slice(part * width, (part + 1) * width)
            share_ref[part] = dot_nn(grad_ref[...], weight_ref[:, here]).astype(BF16)


def share_call(grad, weight, devices):
    tokens, padded = grad.shape
    width = weight.shape[1] // devices
    return pl.pallas_call(
        share_kernel,
        grid=(devices // 2,),
        in_specs=[
            pl.BlockSpec((tokens, padded), lambda j: (0, 0)),
            pl.BlockSpec((padded, 2 * width), lambda j: (0, j)),
        ],
        out_specs=pl.BlockSpec((2, tokens, width), lambda j: (j, 0, 0)),
        out_shape=jax.ShapeDtypeStruct((devices, tokens, width), BF16),
        compiler_params=pltpu.CompilerParams(vmem_limit_bytes=VMEM_BYTES),
        cost_estimate=COST,
    )(grad, weight)


def lane_pairs(pairs):
    return [(2 * a + core, 2 * b + core) for a, b in pairs for core in (0, 1)]


def send(value, pairs):
    return lax.ppermute(value, "col", lane_pairs(pairs))


def swap_cores(value, chips):
    return lax.ppermute(value, "col", [(i, i ^ 1) for i in range(2 * chips)])


def add(*terms):
    total = terms[0].astype(F32)
    for term in terms[1:]:
        total = total + term.astype(F32)
    return total


class LowSum:
    def __init__(self, low, chips):
        self.chips, self.low = chips, low
        self.other = swap_cores(low, chips)

    def spread(self):
        self.mine = add(self.low, self.other).astype(BF16)
        chips = self.chips
        self.got = [send(self.mine, [(z, (z + d) % chips) for z in range(chips)]) for d in range(1, chips)]
        return [self.mine]

    def result(self):
        return add(self.mine, *self.got).astype(BF16)


def sum_rows(value):
    rows = lax.axis_size("row")
    if rows & (rows - 1):
        return lax.psum(value, "row").astype(F32)
    bits = [1 << b for b in range(rows.bit_length() - 1)]
    half = value.shape[0] // 2
    pieces = [(value[:half], bits), (value[half:], bits[::-1])]
    sums = []
    for piece, order in pieces:
        for bit in order:
            got = lax.ppermute(piece.astype(BF16), "row", [(i, i ^ bit) for i in range(rows)])
            piece = piece.astype(BF16).astype(F32) + got.astype(F32)
        sums.append(piece)
    return jnp.concatenate(sums, axis=0)


def sum_rows_at_once(value):
    rows = lax.axis_size("row")
    if rows & (rows - 1):
        return lax.psum(value, "row").astype(F32)
    terms = [value] + [
        lax.ppermute(value, "row", [(i, i ^ other) for i in range(rows)]) for other in range(1, rows)
    ]
    terms = [term.astype(F32) for term in terms]
    while len(terms) > 1:
        terms = [terms[i] + terms[i + 1] for i in range(0, len(terms), 2)]
    return terms[0]


def local(
    tokens_in, token_grad, gate_gain, inner_weight, inner_bias, outer_weight,
    inner_down, inner_up, outer_down, outer_up,
):
    chips = lax.axis_size("col") // 2
    col_index = lax.axis_index("col")
    tok_rows, width = token_grad.shape
    features, ff = inner_weight.shape
    rank = inner_down.shape[1]
    padded = -(-(ff + rank) // COLS) * COLS
    scale = 1.0 / math.sqrt(tok_rows * lax.axis_size("row"))

    gain_local = lax.dynamic_slice_in_dim(gate_gain, col_index * width, width, 0)
    sizes = [tok_rows * part // sum(SPLIT) for part in SPLIT]
    starts = [sum(sizes[:i]) for i in range(len(sizes))]

    gathered, gated_parts = [], []
    for start, size in zip(starts, sizes):
        gated = (gain_local[None, :] * token_grad[start : start + size].astype(F32)).astype(BF16)
        both = jnp.stack([tokens_in[start : start + size], gated])
        gathered.append(lax.all_gather(both, "col", axis=0))
        gated_parts.append(gated)

    gap = padded - ff - rank
    blank = jnp.zeros((gap, features), BF16)
    inner_cat = jnp.concatenate([inner_weight.T, blank, inner_down.T], axis=0)
    outer_cat = jnp.concatenate([outer_weight.T, blank, outer_up], axis=0)
    bias = jnp.pad(inner_bias, (0, padded - ff))[None, :]
    up_hi = jnp.pad(inner_up, ((LANES - rank, 0), (0, padded - ff)))
    down_hi = jnp.pad(outer_down.T, ((LANES - rank, 0), (0, padded - ff)))
    down_lo = jnp.pad(outer_down.T, ((0, LANES - rank), (0, padded - ff)))

    outs, lows, grads = [], [], None
    for both in gathered:
        grad_pre, low, grad = hidden_call(both, inner_cat, outer_cat, bias, up_hi, down_lo, down_hi, ff)
        share = share_call(grad_pre, inner_cat, 2 * chips)
        outs.append(lax.psum_scatter(share, "col", scatter_dimension=0))
        lows.append(LowSum(low, chips))
        lows[-1].spread()
        grads = grad if grads is None else grads + grad
    tokens_grad = jnp.concatenate(outs, axis=0)

    hidden_sums = sum_rows((grads[:, :ff] * scale).astype(BF16))
    inner_up_grad = hidden_sums[:rank]
    outer_down_grad = hidden_sums[rank:].T

    feature_part = 0.0
    for start, size, gated, piece in zip(starts, sizes, gated_parts, lows):
        low, tokens = piece.result(), tokens_in[start : start + size]
        feature_part = feature_part + jnp.concatenate(
            [dot_tn(low[:, :rank], gated), dot_tn(low[:, rank:], tokens)], axis=0
        )
    feature_sums = sum_rows_at_once((feature_part * scale).astype(BF16))
    outer_up_grad = feature_sums[:rank]
    inner_down_grad = feature_sums[rank:].T
    return (tokens_grad, inner_down_grad, inner_up_grad, outer_down_grad, outer_up_grad)


def solution(mesh):
    placed = (
        P("row", "col"),
        P("row", "col"),
        P(),
        P(None, "col"),
        P("col"),
        P(None, "col"),
        P(),
        P(None, "col"),
        P("col", None),
        P(),
    )
    return jax.shard_map(
        local,
        mesh=mesh,
        in_specs=placed,
        out_specs=(P("row", "col"), P("col", None), P(None, "col"), P("col", None), P(None, "col")),
        check_vma=False,
    )
```

profile of v0, /device:TPU:8, one launch (start us, length us, event | category | flops | bytes accessed | tf_op | source)
XLA Modules:
  0.0 356.8 jit_solution(1090512817263584283)
XLA Ops:
  7.2 1.5 slice_bitcast_fusion.1
  8.7 0.8 dynamic_slice.3
  9.8 1.2 pad_maximum_fusion.3
  11.0 1.2 pad_maximum_fusion.2
  12.3 0.6 copy-done.7
  13.3 1.1 fusion.18
  14.4 26.1 %pad_maximum_fusion = (bf16[1792,5120]{1,0:T(8,128)(2,1)}, bf16[1792,5120]{1,0:T(8,128)(2,1)}) fusion(bf16[64,5120]{1,0:T(8,128)(2,1)S(1)} %bitcast.22, bf16[1728,5120]{1,0:T(8,128)(2,1)} %bitcast.20, bf16[64,5120]{1,0:T(8,128)(2,1)} %param.19, bf16[1728,5120]{1,0:T(8,128)(2,1)} %bitcast.21), kind=kLoop, calls=%fused_computation | loop fusion | flops 73400320 | bytes 73400320 | tf_op jit(solution)/shard_map/concatenate | solution.py:247
  40.5 68.4 %all-gather.7.cloned.1.call-done = bf16[16,512,640]{2,1,0:T(8,128)(2,1)} async-done(((bf16[2,512,640]{2,1,0:T(8,128)(2,1)}), bf16[16,512,640]{2,1,0:T(8,128)(2,1)}) %all-gather.7.cloned.1.call-update) | async-done | bytes 10485776 | tf_op jit(solution)/shard_map/all_gather | solution.py:242
  108.9 30.8 %shard_map.139 = (bf16[512,1792]{1,0:T(8,128)(2,1)}, bf16[512,128]{1,0:T(8,128)(2,1)S(1)}, f32[128,1792]{1,0:T(8,128)}) custom-call(bf16[8,2,512,640]{3,2,1,0:T(8,128)(2,1)} %bitcast.27, bf16[1792,5120]{1,0:T(8,128)(2,1)} %get-tuple-element.29.inner_ref.weight_ref, bf16[1792,5120]{1,0:T(8,128)(2,1)} %get-tuple-element.30.outer_ref, ...), custom_call_target="tpu_custom_call" | custom-call | flops 20000000000 | bytes 36000000 | tf_op jit(solution)/shard_map/pallas_call | solution.py:99
  139.6 1.5 copy-done.1
  141.1 14.0 %shard_map.140 = bf16[8,512,640]{2,1,0:T(8,128)(2,1)} custom-call(bf16[512,1792]{1,0:T(8,128)(2,1)S(1)} %copy-done.1, bf16[1792,5120]{1,0:T(8,128)(2,1)} %get-tuple-element.29.inner_ref.weight_ref), custom_call_target="tpu_custom_call" | custom-call | flops 20000000000 | bytes 36000000 | tf_op jit(solution)/shard_map/pallas_call | solution.py:145
  155.2 53.1 %all-gather.5.cloned.1.call-done = bf16[16,512,640]{2,1,0:T(8,128)(2,1)} async-done(((bf16[2,512,640]{2,1,0:T(8,128)(2,1)}), bf16[16,512,640]{2,1,0:T(8,128)(2,1)}) %all-gather.5.cloned.1.call-update) | async-done | bytes 10485776 | tf_op jit(solution)/shard_map/all_gather | solution.py:242
  208.3 29.8 %shard_map.137 = (bf16[512,1792]{1,0:T(8,128)(2,1)}, bf16[512,128]{1,0:T(8,128)(2,1)S(1)}, f32[128,1792]{1,0:T(8,128)}) custom-call(bf16[8,2,512,640]{3,2,1,0:T(8,128)(2,1)} %bitcast.26, bf16[1792,5120]{1,0:T(8,128)(2,1)} %get-tuple-element.29.inner_ref.weight_ref, bf16[1792,5120]{1,0:T(8,128)(2,1)} %get-tuple-element.30.outer_ref, ...), custom_call_target="tpu_custom_call" | custom-call | flops 20000000000 | bytes 36000000 | tf_op jit(solution)/shard_map/pallas_call | solution.py:99
  238.1 1.5 copy-done
  239.7 14.0 %shard_map.138 = bf16[8,512,640]{2,1,0:T(8,128)(2,1)} custom-call(bf16[512,1792]{1,0:T(8,128)(2,1)S(1)} %copy-done, bf16[1792,5120]{1,0:T(8,128)(2,1)} %get-tuple-element.29.inner_ref.weight_ref), custom_call_target="tpu_custom_call" | custom-call | flops 20000000000 | bytes 36000000 | tf_op jit(solution)/shard_map/pallas_call | solution.py:145
  253.6 0.3 collective-permute-start
  254.2 0.6 copy-done.4
  254.8 1.3 fusion.1
  256.1 1.8 collective-permute-start.13
  257.9 1.5 collective-permute-start.11
  259.4 3.2 collective-permute-start.3
  262.6 0.8 collective-permute-start.2
  263.4 1.3 collective-permute-start.1
  264.8 4.7 %collective-permute-done.3 = bf16[512,128]{1,0:T(8,128)(2,1)S(1)} collective-permute-done((bf16[512,128]{1,0:T(8,128)(2,1)S(1)}, bf16[512,128]{1,0:T(8,128)(2,1)S(1)}, u32[]{:S(2)}, u32[]{:S(2)}) %collective-permute-start.3) | collective-permute-done | bytes 131104 | tf_op jit(solution)/shard_map/ppermute | solution.py:164
  269.5 2.7 collective-permute-start.7
  272.2 3.8 %collective-permute-done.2 = bf16[512,128]{1,0:T(8,128)(2,1)S(1)} collective-permute-done((bf16[512,128]{1,0:T(8,128)(2,1)S(1)}, bf16[512,128]{1,0:T(8,128)(2,1)S(1)}, u32[]{:S(2)}, u32[]{:S(2)}) %collective-permute-start.2) | collective-permute-done | bytes 131104 | tf_op jit(solution)/shard_map/ppermute | solution.py:164
  275.9 2.9 collective-permute-start.6
  278.9 2.4 collective-permute-done.1
  281.3 2.5 collective-permute-start.5
  283.8 5.4 %collective-permute-done.7 = bf16[512,128]{1,0:T(8,128)(2,1)S(1)} collective-permute-done((bf16[512,128]{1,0:T(8,128)(2,1)S(1)}, bf16[512,128]{1,0:T(8,128)(2,1)S(1)}, u32[]{:S(2)}, u32[]{:S(2)}) %collective-permute-start.7) | collective-permute-done | bytes 131104 | tf_op jit(solution)/shard_map/ppermute | solution.py:164
  289.3 0.3 collective-permute-done.5
  289.7 0.3 fusion.4
  290.2 0.3 fusion.8
  290.5 0.3 fusion.2
  290.9 2.4 collective-permute-start.10
  293.3 0.5 collective-permute-start.9
  293.8 0.6 collective-permute-start.8
  294.5 1.5 collective-permute-start.12
  296.0 1.5 collective-permute-start.14
  297.6 1.4 collective-permute-done.10
  298.9 2.5 collective-permute-done.9
  301.5 1.0 collective-permute-done.8
  302.5 0.7 fusion.17
  303.3 3.0 collective-permute-done.12
  306.3 0.8 convert_add_fusion
  307.1 0.8 add_bitcast_fusion
  307.9 39.9 %reduce-scatter.3.cloned.1.call-done = bf16[1,512,640]{2,1,0:T(8,128)(2,1)} async-done(((bf16[8,512,640]{2,1,0:T(8,128)(2,1)}), bf16[1,512,640]{2,1,0:T(8,128)(2,1)}) %reduce-scatter.3.cloned.1.call-update) | async-done | bytes 655376 | tf_op jit(solution)/shard_map/reduce_scatter | solution.py:258
  347.8 2.5 pad_maximum_fusion.4
  (41 shorter events, 1.8 us)
Async XLA Ops:
  7.2 101.7 %all-gather.7.cloned.1.call-start = ((), (), s32[]{:S(2)}) async-start(), calls=%async_computation.5 | async-start | bytes 11796480 | tf_op jit(solution)/shard_map/all_gather | solution.py:242
  7.2 2.3 copy-start.3
  11.0 197.3 %all-gather.5.cloned.1.call-start = ((), (), s32[]{:S(2)}) async-start(), calls=%async_computation.4 | async-start | bytes 11796480 | tf_op jit(solution)/shard_map/all_gather | solution.py:242
  12.3 0.7 copy-start.7
  12.3 1.0 copy-start.6
  12.3 2.1 copy-start.5
  12.3 295.6 %reduce-scatter.5.cloned.1.call-start = ((), (), s32[]{:S(2)}) async-start(), calls=%async_computation.3 | async-start | bytes 5898240 | tf_op jit(solution)/shard_map/reduce_scatter | solution.py:258
  139.6 1.5 copy-start.1
  155.1 192.7 %reduce-scatter.3.cloned.1.call-start = ((), (), s32[]{:S(2)}) async-start(), calls=%async_computation.2 | async-start | bytes 5898240 | tf_op jit(solution)/shard_map/reduce_scatter | solution.py:258
  238.1 1.5 copy-start
  253.6 1.2 copy-start.4
  253.6 5.7 %collective-permute-start = (bf16[512,128]{1,0:T(8,128)(2,1)S(1)}, bf16[512,128]{1,0:T(8,128)(2,1)S(1)}, u32[]{:S(2)}, u32[]{:S(2)}) collective-permute-start(bf16[512,128]{1,0:T(8,128)(2,1)S(1)} %get-tuple-element.13), channel_id=1, source_target_pairs={{0,1},{1,0},{2,3},{3,2},{4,5},{5,4},{6,7},{7,6},{8,9},{9,8},{10,11... | collective-permute-start | bytes 393224 | tf_op jit(solution)/shard_map/ppermute | solution.py:168
  254.0 9.5 %collective-permute-start.4 = (bf16[512,128]{1,0:T(8,128)(2,1)S(1)}, bf16[512,128]{1,0:T(8,128)(2,1)S(1)}, u32[]{:S(2)}, u32[]{:S(2)}) collective-permute-start(bf16[512,128]{1,0:T(8,128)(2,1)S(1)} %get-tuple-element.14), channel_id=1, source_target_pairs={{0,1},{1,0},{2,3},{3,2},{4,5},{5,4},{6,7},{7,6},{8,9},{9,8},{10,11... | collective-permute-start | bytes 393224 | tf_op jit(solution)/shard_map/ppermute | solution.py:168
  256.1 33.6 %copy-start.2 = (bf16[1024,640]{1,0:T(8,128)(2,1)S(1)}, bf16[1024,640]{1,0:T(8,128)(2,1)}, u32[]{:S(2)}) copy-start(bf16[1024,640]{1,0:T(8,128)(2,1)} %param.10) | copy-start | bytes 3932164
  256.1 38.3 %collective-permute-start.13 = (bf16[64,1728]{1,0:T(8,128)(2,1)S(1)}, bf16[64,1728]{1,0:T(8,128)(2,1)S(1)}, u32[]{:S(2)}, u32[]{:S(2)}) collective-permute-start(bf16[64,1728]{1,0:T(8,128)(2,1)S(1)} %get-tuple-element.23), channel_id=1, source_target_pairs={{0,16},{8,24},{16,0},{24,8},{1,17},{9,25},{17,1},{25,9},{2,18},{10... | collective-permute-start | bytes 663560 | tf_op jit(solution)/shard_map/ppermute | solution.py:203
  257.9 36.5 %collective-permute-start.11 = (bf16[64,1728]{1,0:T(8,128)(2,1)S(1)}, bf16[64,1728]{1,0:T(8,128)(2,1)S(1)}, u32[]{:S(2)}, u32[]{:S(2)}) collective-permute-start(bf16[64,1728]{1,0:T(8,128)(2,1)S(1)} %get-tuple-element.24), channel_id=1, source_target_pairs={{0,8},{8,0},{16,24},{24,16},{1,9},{9,1},{17,25},{25,17},{2,10},{10... | collective-permute-start | bytes 663560 | tf_op jit(solution)/shard_map/ppermute | solution.py:203
  259.4 10.1 %collective-permute-start.3 = (bf16[512,128]{1,0:T(8,128)(2,1)S(1)}, bf16[512,128]{1,0:T(8,128)(2,1)S(1)}, u32[]{:S(2)}, u32[]{:S(2)}) collective-permute-start(bf16[512,128]{1,0:T(8,128)(2,1)S(1)} %add_convert_fusion.5), channel_id=1, source_target_pairs={{0,6},{1,7},{2,0},{3,1},{4,2},{5,3},{6,4},{7,5},{8,14},{9,15},{10,... | collective-permute-start | bytes 393224 | tf_op jit(solution)/shard_map/ppermute | solution.py:164
  262.6 13.3 %collective-permute-start.2 = (bf16[512,128]{1,0:T(8,128)(2,1)S(1)}, bf16[512,128]{1,0:T(8,128)(2,1)S(1)}, u32[]{:S(2)}, u32[]{:S(2)}) collective-permute-start(bf16[512,128]{1,0:T(8,128)(2,1)S(1)} %add_convert_fusion.5), channel_id=1, source_target_pairs={{0,4},{1,5},{2,6},{3,7},{4,0},{5,1},{6,2},{7,3},{8,12},{9,13},{10,... | collective-permute-start | bytes 393224 | tf_op jit(solution)/shard_map/ppermute | solution.py:164
  263.4 17.9 %collective-permute-start.1 = (bf16[512,128]{1,0:T(8,128)(2,1)S(1)}, bf16[512,128]{1,0:T(8,128)(2,1)S(1)}, u32[]{:S(2)}, u32[]{:S(2)}) collective-permute-start(bf16[512,128]{1,0:T(8,128)(2,1)S(1)} %add_convert_fusion.5), channel_id=1, source_target_pairs={{0,2},{1,3},{2,4},{3,5},{4,6},{5,7},{6,0},{7,1},{8,10},{9,11},{10,... | collective-permute-start | bytes 393224 | tf_op jit(solution)/shard_map/ppermute | solution.py:164
  269.5 19.8 %collective-permute-start.7 = (bf16[512,128]{1,0:T(8,128)(2,1)S(1)}, bf16[512,128]{1,0:T(8,128)(2,1)S(1)}, u32[]{:S(2)}, u32[]{:S(2)}) collective-permute-start(bf16[512,128]{1,0:T(8,128)(2,1)S(1)} %add_convert_fusion.3), channel_id=1, source_target_pairs={{0,6},{1,7},{2,0},{3,1},{4,2},{5,3},{6,4},{7,5},{8,14},{9,15},{10,... | collective-permute-start | bytes 393224 | tf_op jit(solution)/shard_map/ppermute | solution.py:164
  275.9 13.3 %collective-permute-start.6 = (bf16[512,128]{1,0:T(8,128)(2,1)S(1)}, bf16[512,128]{1,0:T(8,128)(2,1)S(1)}, u32[]{:S(2)}, u32[]{:S(2)}) collective-permute-start(bf16[512,128]{1,0:T(8,128)(2,1)S(1)} %add_convert_fusion.3), channel_id=1, source_target_pairs={{0,4},{1,5},{2,6},{3,7},{4,0},{5,1},{6,2},{7,3},{8,12},{9,13},{10,... | collective-permute-start | bytes 393224 | tf_op jit(solution)/shard_map/ppermute | solution.py:164
  281.3 8.3 %collective-permute-start.5 = (bf16[512,128]{1,0:T(8,128)(2,1)S(1)}, bf16[512,128]{1,0:T(8,128)(2,1)S(1)}, u32[]{:S(2)}, u32[]{:S(2)}) collective-permute-start(bf16[512,128]{1,0:T(8,128)(2,1)S(1)} %add_convert_fusion.3), channel_id=1, source_target_pairs={{0,2},{1,3},{2,4},{3,5},{4,6},{5,7},{6,0},{7,1},{8,10},{9,11},{10,... | collective-permute-start | bytes 393224 | tf_op jit(solution)/shard_map/ppermute | solution.py:164
  290.9 8.1 %collective-permute-start.10 = (bf16[128,640]{1,0:T(8,128)(2,1)S(1)}, bf16[128,640]{1,0:T(8,128)(2,1)S(1)}, u32[]{:S(2)}, u32[]{:S(2)}) collective-permute-start(bf16[128,640]{1,0:T(8,128)(2,1)S(1)} %fusion.11), channel_id=1, source_target_pairs={{0,24},{8,16},{16,8},{24,0},{1,25},{9,17},{17,9},{25,1},{2,26},{10... | collective-permute-start | bytes 491528 | tf_op jit(solution)/shard_map/ppermute | solution.py:214
  293.3 8.2 %collective-permute-start.9 = (bf16[128,640]{1,0:T(8,128)(2,1)S(1)}, bf16[128,640]{1,0:T(8,128)(2,1)S(1)}, u32[]{:S(2)}, u32[]{:S(2)}) collective-permute-start(bf16[128,640]{1,0:T(8,128)(2,1)S(1)} %fusion.11), channel_id=1, source_target_pairs={{0,16},{8,24},{16,0},{24,8},{1,17},{9,25},{17,1},{25,9},{2,18},{10... | collective-permute-start | bytes 491528 | tf_op jit(solution)/shard_map/ppermute | solution.py:214
  293.8 8.6 %collective-permute-start.8 = (bf16[128,640]{1,0:T(8,128)(2,1)S(1)}, bf16[128,640]{1,0:T(8,128)(2,1)S(1)}, u32[]{:S(2)}, u32[]{:S(2)}) collective-permute-start(bf16[128,640]{1,0:T(8,128)(2,1)S(1)} %fusion.11), channel_id=1, source_target_pairs={{0,8},{8,0},{16,24},{24,16},{1,9},{9,1},{17,25},{25,17},{2,10},{10... | collective-permute-start | bytes 491528 | tf_op jit(solution)/shard_map/ppermute | solution.py:214
  294.5 11.7 %collective-permute-start.12 = (bf16[64,1728]{1,0:T(8,128)(2,1)S(1)}, bf16[64,1728]{1,0:T(8,128)(2,1)S(1)}, u32[]{:S(2)}, u32[]{:S(2)}) collective-permute-start(bf16[64,1728]{1,0:T(8,128)(2,1)S(1)} %get-tuple-element.22), channel_id=1, source_target_pairs={{0,16},{8,24},{16,0},{24,8},{1,17},{9,25},{17,1},{25,9},{2,18},{10... | collective-permute-start | bytes 663560 | tf_op jit(solution)/shard_map/ppermute | solution.py:203
  296.0 11.1 %collective-permute-start.14 = (bf16[64,1728]{1,0:T(8,128)(2,1)S(1)}, bf16[64,1728]{1,0:T(8,128)(2,1)S(1)}, u32[]{:S(2)}, u32[]{:S(2)}) collective-permute-start(bf16[64,1728]{1,0:T(8,128)(2,1)S(1)} %get-tuple-element.21), channel_id=1, source_target_pairs={{0,8},{8,0},{16,24},{24,16},{1,9},{9,1},{17,25},{25,17},{2,10},{10... | collective-permute-start | bytes 663560 | tf_op jit(solution)/shard_map/ppermute | solution.py:203
Sparse Core Ops, SparseCore 0:
  11.1 97.7 all-gather.6
  110.5 97.7 all-gather.4
  210.6 61.8 reduce-scatter.4
  274.7 73.1 reduce-scatter.2
where the time goes:
time: 362 us; the launch traced here: 357 us
  waiting for transfers between devices  186 us (51%)
  Pallas kernels  88.5 us (24%)
  other arithmetic  34.6 us (10%)
  starting transfers between devices  24 us (7%)
  between operations  13.9 us (4%)
  local copies, waits for them, and re-layouts  8.69 us (2%)
    all_gather x2, waiting for transfers between devices, local(): gathered.append(lax.all_gather(both, 'col', axis=0))  122 us
    pallas_call x2, Pallas kernels, hidden_call(): pl.pallas_call(functools.partial(hidden_kernel, ff), grid=(steps,), in_sp...  60.6 us
    reduce_scatter x2, waiting for transfers between devices, local(): outs.append(lax.psum_scatter(share, 'col', scatter_dimension=0))  39.9 us
    pallas_call x2, Pallas kernels, share_call(): pl.pallas_call(share_kernel, grid=(devices // 2,), in_specs=[pl.BlockSpec...  27.9 us
    concatenate x1, other arithmetic, local(): inner_cat = jnp.concatenate([inner_weight.T, blank, inner_down.T], axis=0)  26.1 us
    ppermute x6, waiting for transfers between devices, send(): return lax.ppermute(value, 'col', lane_pairs(pairs))  16.6 us
    ppermute x6, starting transfers between devices, send(): return lax.ppermute(value, 'col', lane_pairs(pairs))  13.4 us
  transfers between devices with their start and end apart: 19, of which 12 were waited for; matrix products, arithmetic and copies ran while one was open for 9% of the time, Pallas kernels for 25%

commit v1 on v0

--- a/solution.py
+++ b/solution.py
@@ -16,7 +16,7 @@
 COLS = 256
 VMEM_BYTES = 52 * 1024 * 1024
 COST = pl.CostEstimate(flops=20_000_000_000, bytes_accessed=36_000_000, transcendentals=0)
-SPLIT = (512, 512)
+SPLIT = ((512, 384), (512, 288))
 
 
 def dot_nn(left, right):
@@ -31,10 +31,8 @@
     return lax.dot_general(left, right, (((0,), (0,)), ((), ())), preferred_element_type=F32)
 
 
-def hidden_kernel(
-    ff, both_ref, inner_ref, outer_ref, bias_ref, up_ref, down_lo_ref, down_hi_ref,
-    grad_ref, low_ref, grads_ref, pre_acc, hid_acc, hidden_ref,
-):
+def hidden_kernel(ff, both_ref, inner_ref, outer_ref, bias_ref, up_ref, down_lo_ref, down_hi_ref, *refs):
+    grad_ref, low_ref, grads_ref, pre_acc, hid_acc, hidden_ref = refs[-6:]
     step = pl.program_id(0)
     _, _, tokens, width = both_ref.shape
     padded = pre_acc.shape[1]
@@ -91,7 +89,7 @@
                 grad_ref[:, here] = jnp.where(lane + start < ff, grad_ref[:, here], jnp.zeros_like(low))
 
 
-def hidden_call(both, inner_cat, outer_cat, bias, up, down_lo, down_hi, ff):
+def hidden_call(both, inner_cat, outer_cat, bias, up, down_lo, down_hi, ff, after=()):
     devices, _, tokens, width = both.shape
     padded = inner_cat.shape[0]
     steps = devices // 2
@@ -107,7 +105,8 @@
             pl.BlockSpec((LANES, padded), whole),
             pl.BlockSpec((LANES, padded), whole),
             pl.BlockSpec((LANES, padded), whole),
-        ],
+        ]
+        + [pl.BlockSpec(memory_space=pl.ANY)] * len(after),
         out_specs=[
             pl.BlockSpec((tokens, padded), whole),
             pl.BlockSpec((tokens, LANES), whole),
@@ -125,35 +124,62 @@
         ],
         compiler_params=pltpu.CompilerParams(vmem_limit_bytes=VMEM_BYTES),
         cost_estimate=COST,
-    )(both, inner_cat, outer_cat, bias, up, down_lo, down_hi)
-
-
-def share_kernel(grad_ref, weight_ref, share_ref):
-    width = share_ref.shape[2]
+    )(both, inner_cat, outer_cat, bias, up, down_lo, down_hi, *after)
+
+
+def share_kernel(place_ref, grad_ref, weight_ref, *refs):
+    share_ref, own_ref, other_ref = refs[-3:]
+    first, width = own_ref.shape[1:]
     if width % LANES == 0:
         share = dot_nn(grad_ref[...], weight_ref[...]).astype(BF16)
-        share_ref[0], share_ref[1] = share[:, :width], share[:, width:]
+        shares = [share[:, :width], share[:, width:]]
     else:
-        for part in (0, 1):
-            here = slice(part * width, (part + 1) * width)
-            share_ref[part] = dot_nn(grad_ref[...], weight_ref[:, here]).astype(BF16)
-
-
-def share_call(grad, weight, devices):
+        shares = [
+            dot_nn(grad_ref[...], weight_ref[:, part * width : (part + 1) * width]).astype(BF16)
+            for part in (0, 1)
+        ]
+    for part in (0, 1):
+        share_ref[part] = shares[part][first:]
+
+    @pl.when(place_ref[1] == 0)
+    def _():
+        own_ref[0], other_ref[0] = shares[0][:first], shares[1][:first]
+
+    @pl.when(place_ref[1] != 0)
+    def _():
+        own_ref[0], other_ref[0] = shares[1][:first], shares[0][:first]
+
+
+def share_call(place, grad, weight, chips, first, after=()):
     tokens, padded = grad.shape
-    width = weight.shape[1] // devices
+    width = weight.shape[1] // (2 * chips)
+    there = lambda j, place: lax.rem(place[0] + j, chips)
+    near = pl.BlockSpec((1, first, width), lambda j, place: (j, 0, 0))
+    near_shape = jax.ShapeDtypeStruct((chips, first, width), BF16)
     return pl.pallas_call(
         share_kernel,
-        grid=(devices // 2,),
-        in_specs=[
-            pl.BlockSpec((tokens, padded), lambda j: (0, 0)),
-            pl.BlockSpec((padded, 2 * width), lambda j: (0, j)),
+        grid_spec=pltpu.PrefetchScalarGridSpec(
+            num_scalar_prefetch=1,
+            grid=(chips,),
+            in_specs=[
+                pl.BlockSpec((tokens, padded), lambda j, place: (0, 0)),
+                pl.BlockSpec((padded, 2 * width), lambda j, place: (0, there(j, place))),
+            ]
+            + [pl.BlockSpec(memory_space=pl.ANY)] * len(after),
+            out_specs=[
+                pl.BlockSpec((2, tokens - first, width), lambda j, place: (there(j, place), 0, 0)),
+                near,
+                near,
+            ],
+        ),
+        out_shape=[
+            jax.ShapeDtypeStruct((2 * chips, tokens - first, width), BF16),
+            near_shape,
+            near_shape,
         ],
-        out_specs=pl.BlockSpec((2, tokens, width), lambda j: (j, 0, 0)),
-        out_shape=jax.ShapeDtypeStruct((devices, tokens, width), BF16),
         compiler_params=pltpu.CompilerParams(vmem_limit_bytes=VMEM_BYTES),
         cost_estimate=COST,
-    )(grad, weight)
+    )(place, grad, weight, *after)
 
 
 def lane_pairs(pairs):
@@ -173,6 +199,30 @@
     for term in terms[1:]:
         total = total + term.astype(F32)
     return total
+
+
+class Shares:
+    def __init__(self, own, other, chips):
+        arrived = swap_cores(other, chips)
+        self.shares = [add(own[j], arrived[j]) for j in range(chips)]
+        self.chips, self.step, self.up, self.down = chips, 0, None, None
+
+    def hop(self):
+        self.step += 1
+        s, chips = self.step, self.chips
+        up, down = self.shares[chips - s], self.shares[s]
+        if s > 1:
+            up, down = up + self.up.astype(F32), down + self.down.astype(F32)
+        up, down = up.astype(BF16), down.astype(BF16)
+        self.up = send(up, [(z, z + 1) for z in range(s)])
+        self.down = send(down, [(z, z - 1) for z in range(chips - s, chips)])
+        return [up, down]
+
+    def left(self):
+        return self.chips - 1 - self.step
+
+    def result(self):
+        return add(self.shares[0], self.up, self.down).astype(BF16)
 
 
 class LowSum:
@@ -225,6 +275,7 @@
 ):
     chips = lax.axis_size("col") // 2
     col_index = lax.axis_index("col")
+    place = jnp.stack([lax.div(col_index, 2), lax.rem(col_index, 2)]).astype(jnp.int32)
     tok_rows, width = token_grad.shape
     features, ff = inner_weight.shape
     rank = inner_down.shape[1]
@@ -232,7 +283,8 @@
     scale = 1.0 / math.sqrt(tok_rows * lax.axis_size("row"))
 
     gain_local = lax.dynamic_slice_in_dim(gate_gain, col_index * width, width, 0)
-    sizes = [tok_rows * part // sum(SPLIT) for part in SPLIT]
+    sizes = [tok_rows * part // sum(part for part, _ in SPLIT) for part, _ in SPLIT]
+    firsts = [size * share // 1024 // 16 * 16 for size, (_, share) in zip(sizes, SPLIT)]
     starts = [sum(sizes[:i]) for i in range(len(sizes))]
 
     gathered, gated_parts = [], []
@@ -251,23 +303,41 @@
     down_hi = jnp.pad(outer_down.T, ((LANES - rank, 0), (0, padded - ff)))
     down_lo = jnp.pad(outer_down.T, ((0, LANES - rank), (0, padded - ff)))
 
-    outs, lows, grads = [], [], None
-    for both in gathered:
-        grad_pre, low, grad = hidden_call(both, inner_cat, outer_cat, bias, up_hi, down_lo, down_hi, ff)
-        share = share_call(grad_pre, inner_cat, 2 * chips)
-        outs.append(lax.psum_scatter(share, "col", scatter_dimension=0))
+    near, far, lows, grads = [], [], [], None
+    for index, (both, first) in enumerate(zip(gathered, firsts)):
+        after = []
+        if index:
+            shares = moving
+            while shares.left():
+                after = shares.hop()
+            after = after + lows[-1].spread()
+        grad_pre, low, grad = hidden_call(
+            both, inner_cat, outer_cat, bias, up_hi, down_lo, down_hi, ff, after
+        )
+        after = []
+        if index:
+            near.append(shares.result())
+            lows[-1] = lows[-1].result()
+            after = [near[-1], lows[-1]]
+        share, own, other = share_call(place, grad_pre, inner_cat, chips, first, after)
+        far.append(lax.psum_scatter(share, "col", scatter_dimension=0))
+        moving = Shares(own, other, chips)
         lows.append(LowSum(low, chips))
-        lows[-1].spread()
         grads = grad if grads is None else grads + grad
-    tokens_grad = jnp.concatenate(outs, axis=0)
+    while moving.left():
+        moving.hop()
+    near.append(moving.result())
+    lows[-1].spread()
+    lows[-1] = lows[-1].result()
+    tokens_grad = jnp.concatenate([part for pair in zip(near, far) for part in pair], axis=0)
 
     hidden_sums = sum_rows((grads[:, :ff] * scale).astype(BF16))
     inner_up_grad = hidden_sums[:rank]
     outer_down_grad = hidden_sums[rank:].T
 
     feature_part = 0.0
-    for start, size, gated, piece in zip(starts, sizes, gated_parts, lows):
-        low, tokens = piece.result(), tokens_in[start : start + size]
+    for start, size, gated, low in zip(starts, sizes, gated_parts, lows):
+        tokens = tokens_in[start : start + size]
         feature_part = feature_part + jnp.concatenate(
             [dot_tn(low[:, :rank], gated), dot_tn(low[:, rank:], tokens)], axis=0
         )

time: 362 us -> 364 us (level)
  starting transfers between devices: 24 us -> 70.3 us
  waiting for transfers between devices: 186 us -> 142 us
  Pallas kernels: 88.5 us -> 92.2 us
    all_gather x2, waiting for transfers between devices: 122 us -> 70.5 us  [local(): gathered.append(lax.all_gather(both, 'col', axis=0))]
    ppermute x6 -> x18, waiting for transfers between devices: 16.6 us -> 64.7 us  [send(): return lax.ppermute(value, 'col', lane_pairs(pairs))]
    ppermute x6 -> x18, starting transfers between devices: 13.4 us -> 61.4 us  [send(): return lax.ppermute(value, 'col', lane_pairs(pairs))]
    reduce_scatter x2, waiting for transfers between devices: 39.9 us -> 0.04 us  [local(): far.append(lax.psum_scatter(share, 'col', scatter_dimension=0))]
  transfers between devices with their start and end apart: 19 -> 33, of which waited for: 12 -> 13; matrix products, arithmetic and copies ran while one was open for 9% -> 10% of each run, Pallas kernels for 25% -> 25%
where the time goes in v1:
time: 364 us; the launch traced here: 362 us
  waiting for transfers between devices  142 us (39%)
  Pallas kernels  92.2 us (25%)
  starting transfers between devices  70.3 us (19%)
  other arithmetic  36.1 us (10%)
  between operations  14.1 us (4%)
  local copies, waits for them, and re-layouts  5.72 us (2%)
    all_gather x2, waiting for transfers between devices, local(): gathered.append(lax.all_gather(both, 'col', axis=0))  70.5 us
    ppermute x18, waiting for transfers between devices, send(): return lax.ppermute(value, 'col', lane_pairs(pairs))  64.7 us
    pallas_call x2, Pallas kernels, hidden_call(): pl.pallas_call(functools.partial(hidden_kernel, ff), grid=(steps,), in_sp...  62.1 us
    ppermute x18, starting transfers between devices, send(): return lax.ppermute(value, 'col', lane_pairs(pairs))  61.4 us
    pallas_call x2, Pallas kernels, share_call(): pl.pallas_call(share_kernel, grid_spec=pltpu.PrefetchScalarGridSpec(num_s...  30 us
    concatenate x1, other arithmetic, local(): inner_cat = jnp.concatenate([inner_weight.T, blank, inner_down.T], axis=0)  25.9 us
  transfers between devices with their start and end apart: 33, of which 13 were waited for; matrix products, arithmetic and copies ran while one was open for 10% of the time, Pallas kernels for 25%

profile of v1, /device:TPU:8, one launch (start us, length us, event | category | flops | bytes accessed | tf_op | source)
XLA Modules:
  0.0 362.4 jit_solution(1197500084522895251)
XLA Ops:
  7.2 1.5 slice_bitcast_fusion.1
  8.7 0.8 dynamic_slice.3
  9.8 1.2 pad_maximum_fusion.2
  11.1 1.2 pad_maximum_fusion.3
  13.8 25.9 %pad_maximum_fusion = (bf16[1792,5120]{1,0:T(8,128)(2,1)}, bf16[1792,5120]{1,0:T(8,128)(2,1)}) fusion(bf16[64,5120]{1,0:T(8,128)(2,1)S(1)} %bitcast.70, bf16[1728,5120]{1,0:T(8,128)(2,1)} %bitcast.68, bf16[64,5120]{1,0:T(8,128)(2,1)S(1)} %copy-done.8, bf16[1728,5120]{1,0:T(8,128)(2,1)} %bitcast.69), kind=kLoop, calls=%fused_computation | loop fusion | flops 73400320 | bytes 73400320 | tf_op jit(solution)/shard_map/concatenate | solution.py:299
  39.7 69.2 %all-gather.5.cloned.1.call-done = bf16[16,512,640]{2,1,0:T(8,128)(2,1)} async-done(((bf16[2,512,640]{2,1,0:T(8,128)(2,1)}), bf16[16,512,640]{2,1,0:T(8,128)(2,1)}) %all-gather.5.cloned.1.call-update) | async-done | bytes 10485776 | tf_op jit(solution)/shard_map/all_gather | solution.py:294
  108.9 30.9 %shard_map.137 = (bf16[512,1792]{1,0:T(8,128)(2,1)}, bf16[512,128]{1,0:T(8,128)(2,1)S(1)}, f32[128,1792]{1,0:T(8,128)}) custom-call(bf16[8,2,512,640]{3,2,1,0:T(8,128)(2,1)} %bitcast.75, bf16[1792,5120]{1,0:T(8,128)(2,1)} %get-tuple-element.49.inner_ref.weight_ref, bf16[1792,5120]{1,0:T(8,128)(2,1)} %get-tuple-element.50.outer_ref, ...), custom_call_target="tpu_custom_call" | custom-call | flops 20000000000 | bytes 36000000 | tf_op jit(solution)/shard_map/pallas_call | solution.py:97
  139.8 15.0 %shard_map.138 = (bf16[8,320,640]{2,1,0:T(8,128)(2,1)}, bf16[4,192,640]{2,1,0:T(8,128)(2,1)S(1)}, bf16[4,192,640]{2,1,0:T(8,128)(2,1)}) custom-call(s32[2]{0:T(128)S(1)} %pad_add_fusion.place_ref, bf16[512,1792]{1,0:T(8,128)(2,1)} %get-tuple-element.17.grad_ref, bf16[1792,5120]{1,0:T(8,128)(2,1)} %get-tuple-element.49.inner_ref.weight_ref), custom_call_target="tpu_custom_call" | custom-call | flops 20000000000 | bytes 36000000 | tf_op jit(solution)/shard_map/pallas_call | solution.py:159
  155.2 2.4 collective-permute-done
  158.8 1.3 collective-permute-start.1
  160.2 1.3 collective-permute-start.5
  161.5 2.1 collective-permute-start.10
  163.6 14.5 %collective-permute-start.8 = (bf16[512,128]{1,0:T(8,128)(2,1)S(1)}, bf16[512,128]{1,0:T(8,128)(2,1)S(1)}, u32[]{:S(2)}, u32[]{:S(2)}) collective-permute-start(bf16[512,128]{1,0:T(8,128)(2,1)S(1)} %add_convert_fusion.5.refs_2_), channel_id=1, source_target_pairs={{0,2},{1,3},{2,4},{3,5},{4,6},{5,7},{6,0},{7,1},{8,10},{9,11},{10,... | collective-permute-start | bytes 393224 | tf_op jit(solution)/shard_map/ppermute | solution.py:190
  178.2 5.2 %collective-permute-start.9 = (bf16[512,128]{1,0:T(8,128)(2,1)S(1)}, bf16[512,128]{1,0:T(8,128)(2,1)S(1)}, u32[]{:S(2)}, u32[]{:S(2)}) collective-permute-start(bf16[512,128]{1,0:T(8,128)(2,1)S(1)} %add_convert_fusion.5.refs_2_), channel_id=1, source_target_pairs={{0,4},{1,5},{2,6},{3,7},{4,0},{5,1},{6,2},{7,3},{8,12},{9,13},{10,... | collective-permute-start | bytes 393224 | tf_op jit(solution)/shard_map/ppermute | solution.py:190
  183.4 10.5 %collective-permute-done.5 = bf16[192,640]{1,0:T(8,128)(2,1)S(1)} collective-permute-done((bf16[192,640]{1,0:T(8,128)(2,1)S(1)}, bf16[192,640]{1,0:T(8,128)(2,1)S(1)}, u32[]{:S(2)}, u32[]{:S(2)}) %collective-permute-start.5) | collective-permute-done | bytes 245792 | tf_op jit(solution)/shard_map/ppermute | solution.py:190
  194.1 1.9 collective-permute-start.2
  196.0 15.5 %collective-permute-done.10 = bf16[512,128]{1,0:T(8,128)(2,1)S(1)} collective-permute-done((bf16[512,128]{1,0:T(8,128)(2,1)S(1)}, bf16[512,128]{1,0:T(8,128)(2,1)S(1)}, u32[]{:S(2)}, u32[]{:S(2)}) %collective-permute-start.10) | collective-permute-done | bytes 131104 | tf_op jit(solution)/shard_map/ppermute | solution.py:190
  211.6 12.1 %collective-permute-start.6 = (bf16[192,640]{1,0:T(8,128)(2,1)S(1)}, bf16[192,640]{1,0:T(8,128)(2,1)S(1)}, u32[]{:S(2)}, u32[]{:S(2)}) collective-permute-start(bf16[192,640]{1,0:T(8,128)(2,1)S(1)} %get-tuple-element.29.refs_1_), channel_id=1, source_target_pairs={{2,0},{3,1},{4,2},{5,3},{6,4},{7,5},{10,8},{11,9},{12,10},{13,11},... | collective-permute-start | bytes 737288 | tf_op jit(solution)/shard_map/ppermute | solution.py:190
  223.8 1.0 fusion.13.refs_0_
  224.8 1.9 collective-permute-start.3
  226.8 1.3 all-gather.7.cloned.1.call-done
  228.1 31.3 %shard_map.139 = (bf16[512,1792]{1,0:T(8,128)(2,1)}, bf16[512,128]{1,0:T(8,128)(2,1)S(1)}, f32[128,1792]{1,0:T(8,128)}) custom-call(bf16[8,2,512,640]{3,2,1,0:T(8,128)(2,1)} %bitcast.74, bf16[1792,5120]{1,0:T(8,128)(2,1)} %get-tuple-element.49.inner_ref.weight_ref, bf16[1792,5120]{1,0:T(8,128)(2,1)} %get-tuple-element.50.outer_ref, ...), custom_call_target="tpu_custom_call" | custom-call | flops 20000000000 | bytes 36000000 | tf_op jit(solution)/shard_map/pallas_call | solution.py:97
  259.3 1.1 fusion.15.refs_0_
  260.4 15.0 %shard_map.140 = (bf16[8,368,640]{2,1,0:T(8,128)(2,1)}, bf16[4,144,640]{2,1,0:T(8,128)(2,1)S(1)}, bf16[4,144,640]{2,1,0:T(8,128)(2,1)S(1)}) custom-call(s32[2]{0:T(128)S(1)} %pad_add_fusion.place_ref, bf16[512,1792]{1,0:T(8,128)(2,1)} %get-tuple-element.22.grad_ref, bf16[1792,5120]{1,0:T(8,128)(2,1)} %get-tuple-element.49.inner_ref.weight_ref, ...), custom_call_target="tpu_custom_call" | custom-call | flops 20000000000 | bytes 36000000 | tf_op jit(solution)/shard_map/pallas_call | solution.py:159
  275.4 1.3 copy-done.1
  277.0 1.5 fusion.6
  279.0 1.5 collective-permute-start.25
  280.6 1.5 collective-permute-start.27
  282.1 7.1 %collective-permute-start.19 = (bf16[512,128]{1,0:T(8,128)(2,1)S(1)}, bf16[512,128]{1,0:T(8,128)(2,1)S(1)}, u32[]{:S(2)}, u32[]{:S(2)}) collective-permute-start(bf16[512,128]{1,0:T(8,128)(2,1)S(1)} %add_convert_fusion.3), channel_id=1, source_target_pairs={{0,2},{1,3},{2,4},{3,5},{4,6},{5,7},{6,0},{7,1},{8,10},{9,11},{10,... | collective-permute-start | bytes 393224 | tf_op jit(solution)/shard_map/ppermute | solution.py:190
  289.2 1.5 collective-permute-start.21
  292.1 12.0 %collective-permute-done.19 = bf16[512,128]{1,0:T(8,128)(2,1)S(1)} collective-permute-done((bf16[512,128]{1,0:T(8,128)(2,1)S(1)}, bf16[512,128]{1,0:T(8,128)(2,1)S(1)}, u32[]{:S(2)}, u32[]{:S(2)}) %collective-permute-start.19) | collective-permute-done | bytes 131104 | tf_op jit(solution)/shard_map/ppermute | solution.py:190
  304.1 6.3 %collective-permute-done.20 = bf16[512,128]{1,0:T(8,128)(2,1)S(1)} collective-permute-done((bf16[512,128]{1,0:T(8,128)(2,1)S(1)}, bf16[512,128]{1,0:T(8,128)(2,1)S(1)}, u32[]{:S(2)}, u32[]{:S(2)}) %collective-permute-start.20) | collective-permute-done | bytes 131104 | tf_op jit(solution)/shard_map/ppermute | solution.py:190
  311.2 0.8 collective-permute-start.22
  312.6 2.1 collective-permute-start.24
  314.8 3.0 collective-permute-done.22
  317.8 1.3 collective-permute-start.12
  319.1 0.8 collective-permute-done.23
  320.7 9.1 %collective-permute-done.12 = bf16[144,640]{1,0:T(8,128)(2,1)S(1)} collective-permute-done((bf16[144,640]{1,0:T(8,128)(2,1)S(1)}, bf16[144,640]{1,0:T(8,128)(2,1)S(1)}, u32[]{:S(2)}, u32[]{:S(2)}) %collective-permute-start.12) | collective-permute-done | bytes 184352 | tf_op jit(solution)/shard_map/ppermute | solution.py:190
  329.9 1.9 collective-permute-start.13
  332.6 5.7 %collective-permute-done.13 = bf16[144,640]{1,0:T(8,128)(2,1)S(1)} collective-permute-done((bf16[144,640]{1,0:T(8,128)(2,1)S(1)}, bf16[144,640]{1,0:T(8,128)(2,1)S(1)}, u32[]{:S(2)}, u32[]{:S(2)}) %collective-permute-start.13) | collective-permute-done | bytes 184352 | tf_op jit(solution)/shard_map/ppermute | solution.py:190
  338.4 1.3 collective-permute-start.16
  339.7 0.8 add_bitcast_fusion
  340.5 4.5 %collective-permute-start.14 = (bf16[144,640]{1,0:T(8,128)(2,1)S(1)}, bf16[144,640]{1,0:T(8,128)(2,1)S(1)}, u32[]{:S(2)}, u32[]{:S(2)}) collective-permute-start(bf16[144,640]{1,0:T(8,128)(2,1)S(1)} %get-tuple-element.33), channel_id=1, source_target_pairs={{0,2},{1,3},{2,4},{3,5},{4,6},{5,7},{8,10},{9,11},{10,12},{11,13},... | collective-permute-start | bytes 552968 | tf_op jit(solution)/shard_map/ppermute | solution.py:190
  345.1 0.8 collective-permute-done.16
  345.9 1.9 collective-permute-start.17
  347.9 0.8 convert_add_fusion.3
  348.7 4.7 %collective-permute-done.17 = bf16[144,640]{1,0:T(8,128)(2,1)S(1)} collective-permute-done((bf16[144,640]{1,0:T(8,128)(2,1)S(1)}, bf16[144,640]{1,0:T(8,128)(2,1)S(1)}, u32[]{:S(2)}, u32[]{:S(2)}) %collective-permute-start.17) | collective-permute-done | bytes 184352 | tf_op jit(solution)/shard_map/ppermute | solution.py:190
  353.5 2.3 pad_maximum_fusion.4
  (88 shorter events, 9.3 us)
Async XLA Ops:
  7.2 101.7 %all-gather.5.cloned.1.call-start = ((), (), s32[]{:S(2)}) async-start(), calls=%async_computation.4 | async-start | bytes 11796480 | tf_op jit(solution)/shard_map/all_gather | solution.py:294
  7.2 2.3 copy-start.3
  11.0 217.1 %all-gather.7.cloned.1.call-start = ((), (), s32[]{:S(2)}) async-start(), calls=%async_computation.5 | async-start | bytes 11796480 | tf_op jit(solution)/shard_map/all_gather | solution.py:294
  12.3 0.7 copy-start.11
  12.3 1.0 copy-start.9
  12.3 1.1 copy-start.10
  12.3 1.3 copy-start.7
  12.3 1.5 copy-start.8
  12.3 341.2 %reduce-scatter.3.cloned.1.call-start = ((), (), s32[]{:S(2)}) async-start(), calls=%async_computation.2 | async-start | bytes 3686400 | tf_op jit(solution)/shard_map/reduce_scatter | solution.py:323
  13.4 95.5 %copy-start = (bf16[128,1792]{1,0:T(8,128)(2,1)}, bf16[128,1792]{1,0:T(8,128)(2,1)S(1)}, u32[]{:S(2)}) copy-start(bf16[128,1792]{1,0:T(8,128)(2,1)S(1)} %get-tuple-element.47.down_hi_ref) | copy-start | bytes 1376260
  154.8 2.8 collective-permute-start
  155.1 198.4 %reduce-scatter.5.cloned.1.call-start = ((), (), s32[]{:S(2)}) async-start(), calls=%async_computation.3 | async-start | bytes 4239360 | tf_op jit(solution)/shard_map/reduce_scatter | solution.py:323
  157.6 36.3 %copy-start.2 = (bf16[4,192,640]{2,1,0:T(8,128)(2,1)}, bf16[4,192,640]{2,1,0:T(8,128)(2,1)S(1)}, u32[]{:S(2)}) copy-start(bf16[4,192,640]{2,1,0:T(8,128)(2,1)S(1)} %collective-permute-done) | copy-start | bytes 2949124
  157.7 2.3 collective-permute-start.4
  158.4 3.1 collective-permute-start.7
  158.8 24.6 %collective-permute-start.1 = (bf16[192,640]{1,0:T(8,128)(2,1)S(1)}, bf16[192,640]{1,0:T(8,128)(2,1)S(1)}, u32[]{:S(2)}, u32[]{:S(2)}) collective-permute-start(bf16[192,640]{1,0:T(8,128)(2,1)S(1)} %get-tuple-element.32), channel_id=1, source_target_pairs={{0,2},{1,3},{8,10},{9,11},{16,18},{17,19},{24,26},{25,27}} | collective-permute-start | bytes 737288 | tf_op jit(solution)/shard_map/ppermute | solution.py:190
  160.2 33.7 %collective-permute-start.5 = (bf16[192,640]{1,0:T(8,128)(2,1)S(1)}, bf16[192,640]{1,0:T(8,128)(2,1)S(1)}, u32[]{:S(2)}, u32[]{:S(2)}) collective-permute-start(bf16[192,640]{1,0:T(8,128)(2,1)S(1)} %fusion.12), channel_id=1, source_target_pairs={{4,2},{5,3},{6,4},{7,5},{12,10},{13,11},{14,12},{15,13},{20,18},{2... | collective-permute-start | bytes 737288 | tf_op jit(solution)/shard_map/ppermute | solution.py:190
  161.5 50.0 %collective-permute-start.10 = (bf16[512,128]{1,0:T(8,128)(2,1)S(1)}, bf16[512,128]{1,0:T(8,128)(2,1)S(1)}, u32[]{:S(2)}, u32[]{:S(2)}) collective-permute-start(bf16[512,128]{1,0:T(8,128)(2,1)S(1)} %add_convert_fusion.5.refs_2_), channel_id=1, source_target_pairs={{0,6},{1,7},{2,0},{3,1},{4,2},{5,3},{6,4},{7,5},{8,14},{9,15},{10,... | collective-permute-start | bytes 393224 | tf_op jit(solution)/shard_map/ppermute | solution.py:190
  163.6 47.9 %collective-permute-start.8 = (bf16[512,128]{1,0:T(8,128)(2,1)S(1)}, bf16[512,128]{1,0:T(8,128)(2,1)S(1)}, u32[]{:S(2)}, u32[]{:S(2)}) collective-permute-start(bf16[512,128]{1,0:T(8,128)(2,1)S(1)} %add_convert_fusion.5.refs_2_), channel_id=1, source_target_pairs={{0,2},{1,3},{2,4},{3,5},{4,6},{5,7},{6,0},{7,1},{8,10},{9,11},{10,... | collective-permute-start | bytes 393224 | tf_op jit(solution)/shard_map/ppermute | solution.py:190
  178.2 33.4 %collective-permute-start.9 = (bf16[512,128]{1,0:T(8,128)(2,1)S(1)}, bf16[512,128]{1,0:T(8,128)(2,1)S(1)}, u32[]{:S(2)}, u32[]{:S(2)}) collective-permute-start(bf16[512,128]{1,0:T(8,128)(2,1)S(1)} %add_convert_fusion.5.refs_2_), channel_id=1, source_target_pairs={{0,4},{1,5},{2,6},{3,7},{4,0},{5,1},{6,2},{7,3},{8,12},{9,13},{10,... | collective-permute-start | bytes 393224 | tf_op jit(solution)/shard_map/ppermute | solution.py:190
  194.1 29.7 %collective-permute-start.2 = (bf16[192,640]{1,0:T(8,128)(2,1)S(1)}, bf16[192,640]{1,0:T(8,128)(2,1)S(1)}, u32[]{:S(2)}, u32[]{:S(2)}) collective-permute-start(bf16[192,640]{1,0:T(8,128)(2,1)S(1)} %get-tuple-element.30), channel_id=1, source_target_pairs={{0,2},{1,3},{2,4},{3,5},{8,10},{9,11},{10,12},{11,13},{16,18},{17,... | collective-permute-start | bytes 737288 | tf_op jit(solution)/shard_map/ppermute | solution.py:190
  211.6 47.7 %collective-permute-start.6 = (bf16[192,640]{1,0:T(8,128)(2,1)S(1)}, bf16[192,640]{1,0:T(8,128)(2,1)S(1)}, u32[]{:S(2)}, u32[]{:S(2)}) collective-permute-start(bf16[192,640]{1,0:T(8,128)(2,1)S(1)} %get-tuple-element.29.refs_1_), channel_id=1, source_target_pairs={{2,0},{3,1},{4,2},{5,3},{6,4},{7,5},{10,8},{11,9},{12,10},{13,11},... | collective-permute-start | bytes 737288 | tf_op jit(solution)/shard_map/ppermute | solution.py:190
  224.8 34.5 %collective-permute-start.3 = (bf16[192,640]{1,0:T(8,128)(2,1)S(1)}, bf16[192,640]{1,0:T(8,128)(2,1)S(1)}, u32[]{:S(2)}, u32[]{:S(2)}) collective-permute-start(bf16[192,640]{1,0:T(8,128)(2,1)S(1)} %fusion.13.refs_0_), channel_id=1, source_target_pairs={{0,2},{1,3},{2,4},{3,5},{4,6},{5,7},{8,10},{9,11},{10,12},{11,13},... | collective-permute-start | bytes 737288 | tf_op jit(solution)/shard_map/ppermute | solution.py:190
  275.4 1.3 copy-start.1
  276.7 2.2 copy-start.5
  276.7 2.2 copy-start.6
  278.6 3.5 collective-permute-start.18
  279.0 11.8 %collective-permute-start.25 = (bf16[64,1728]{1,0:T(8,128)(2,1)S(1)}, bf16[64,1728]{1,0:T(8,128)(2,1)S(1)}, u32[]{:S(2)}, u32[]{:S(2)}) collective-permute-start(bf16[64,1728]{1,0:T(8,128)(2,1)S(1)} %get-tuple-element.44), channel_id=1, source_target_pairs={{0,8},{8,0},{16,24},{24,16},{1,9},{9,1},{17,25},{25,17},{2,10},{10... | collective-permute-start | bytes 663560 | tf_op jit(solution)/shard_map/ppermute | solution.py:253
  280.6 10.2 %collective-permute-start.27 = (bf16[64,1728]{1,0:T(8,128)(2,1)S(1)}, bf16[64,1728]{1,0:T(8,128)(2,1)S(1)}, u32[]{:S(2)}, u32[]{:S(2)}) collective-permute-start(bf16[64,1728]{1,0:T(8,128)(2,1)S(1)} %get-tuple-element.43), channel_id=1, source_target_pairs={{0,16},{8,24},{16,0},{24,8},{1,17},{9,25},{17,1},{25,9},{2,18},{10... | collective-permute-start | bytes 663560 | tf_op jit(solution)/shard_map/ppermute | solution.py:253
  282.1 28.8 %copy-start.4 = (bf16[1024,640]{1,0:T(8,128)(2,1)S(1)}, bf16[1024,640]{1,0:T(8,128)(2,1)}, u32[]{:S(2)}) copy-start(bf16[1024,640]{1,0:T(8,128)(2,1)} %param.11) | copy-start | bytes 3932164
  282.1 22.0 %collective-permute-start.19 = (bf16[512,128]{1,0:T(8,128)(2,1)S(1)}, bf16[512,128]{1,0:T(8,128)(2,1)S(1)}, u32[]{:S(2)}, u32[]{:S(2)}) collective-permute-start(bf16[512,128]{1,0:T(8,128)(2,1)S(1)} %add_convert_fusion.3), channel_id=1, source_target_pairs={{0,2},{1,3},{2,4},{3,5},{4,6},{5,7},{6,0},{7,1},{8,10},{9,11},{10,... | collective-permute-start | bytes 393224 | tf_op jit(solution)/shard_map/ppermute | solution.py:190
  289.2 21.2 %collective-permute-start.20 = (bf16[512,128]{1,0:T(8,128)(2,1)S(1)}, bf16[512,128]{1,0:T(8,128)(2,1)S(1)}, u32[]{:S(2)}, u32[]{:S(2)}) collective-permute-start(bf16[512,128]{1,0:T(8,128)(2,1)S(1)} %add_convert_fusion.3), channel_id=1, source_target_pairs={{0,4},{1,5},{2,6},{3,7},{4,0},{5,1},{6,2},{7,3},{8,12},{9,13},{10,... | collective-permute-start | bytes 393224 | tf_op jit(solution)/shard_map/ppermute | solution.py:190
  289.2 21.2 %collective-permute-start.21 = (bf16[512,128]{1,0:T(8,128)(2,1)S(1)}, bf16[512,128]{1,0:T(8,128)(2,1)S(1)}, u32[]{:S(2)}, u32[]{:S(2)}) collective-permute-start(bf16[512,128]{1,0:T(8,128)(2,1)S(1)} %add_convert_fusion.3), channel_id=1, source_target_pairs={{0,6},{1,7},{2,0},{3,1},{4,2},{5,3},{6,4},{7,5},{8,14},{9,15},{10,... | collective-permute-start | bytes 393224 | tf_op jit(solution)/shard_map/ppermute | solution.py:190
  290.9 48.8 %collective-permute-start.28 = (bf16[64,1728]{1,0:T(8,128)(2,1)S(1)}, bf16[64,1728]{1,0:T(8,128)(2,1)S(1)}, u32[]{:S(2)}, u32[]{:S(2)}) collective-permute-start(bf16[64,1728]{1,0:T(8,128)(2,1)S(1)} %get-tuple-element.41), channel_id=1, source_target_pairs={{0,8},{8,0},{16,24},{24,16},{1,9},{9,1},{17,25},{25,17},{2,10},{10... | collective-permute-start | bytes 663560 | tf_op jit(solution)/shard_map/ppermute | solution.py:253
  291.5 56.3 %collective-permute-start.26 = (bf16[64,1728]{1,0:T(8,128)(2,1)S(1)}, bf16[64,1728]{1,0:T(8,128)(2,1)S(1)}, u32[]{:S(2)}, u32[]{:S(2)}) collective-permute-start(bf16[64,1728]{1,0:T(8,128)(2,1)S(1)} %get-tuple-element.42), channel_id=1, source_target_pairs={{0,16},{8,24},{16,0},{24,8},{1,17},{9,25},{17,1},{25,9},{2,18},{10... | collective-permute-start | bytes 663560 | tf_op jit(solution)/shard_map/ppermute | solution.py:253
  304.1 8.5 %collective-permute-start.11 = (bf16[4,144,640]{2,1,0:T(8,128)(2,1)S(1)}, bf16[4,144,640]{2,1,0:T(8,128)(2,1)S(1)}, u32[]{:S(2)}, u32[]{:S(2)}) collective-permute-start(bf16[4,144,640]{2,1,0:T(8,128)(2,1)S(1)} %get-tuple-element.24), channel_id=1, source_target_pairs={{0,1},{1,0},{2,3},{3,2},{4,5},{5,4},{6,7},{7,6},{8,9},{9,8},{10,11... | collective-permute-start | bytes 2211848 | tf_op jit(solution)/shard_map/ppermute | solution.py:194
  311.2 6.6 %collective-permute-start.22 = (bf16[128,640]{1,0:T(8,128)(2,1)S(1)}, bf16[128,640]{1,0:T(8,128)(2,1)S(1)}, u32[]{:S(2)}, u32[]{:S(2)}) collective-permute-start(bf16[128,640]{1,0:T(8,128)(2,1)S(1)} %fusion.23), channel_id=1, source_target_pairs={{0,8},{8,0},{16,24},{24,16},{1,9},{9,1},{17,25},{25,17},{2,10},{10... | collective-permute-start | bytes 491528 | tf_op jit(solution)/shard_map/ppermute | solution.py:264
  311.9 8.0 %collective-permute-start.23 = (bf16[128,640]{1,0:T(8,128)(2,1)S(1)}, bf16[128,640]{1,0:T(8,128)(2,1)S(1)}, u32[]{:S(2)}, u32[]{:S(2)}) collective-permute-start(bf16[128,640]{1,0:T(8,128)(2,1)S(1)} %fusion.23), channel_id=1, source_target_pairs={{0,16},{8,24},{16,0},{24,8},{1,17},{9,25},{17,1},{25,9},{2,18},{10... | collective-permute-start | bytes 491528 | tf_op jit(solution)/shard_map/ppermute | solution.py:264
  312.6 7.3 %collective-permute-start.24 = (bf16[128,640]{1,0:T(8,128)(2,1)S(1)}, bf16[128,640]{1,0:T(8,128)(2,1)S(1)}, u32[]{:S(2)}, u32[]{:S(2)}) collective-permute-start(bf16[128,640]{1,0:T(8,128)(2,1)S(1)} %fusion.23), channel_id=1, source_target_pairs={{0,24},{8,16},{16,8},{24,0},{1,25},{9,17},{17,9},{25,1},{2,26},{10... | collective-permute-start | bytes 491528 | tf_op jit(solution)/shard_map/ppermute | solution.py:264
  317.8 12.0 %collective-permute-start.12 = (bf16[144,640]{1,0:T(8,128)(2,1)S(1)}, bf16[144,640]{1,0:T(8,128)(2,1)S(1)}, u32[]{:S(2)}, u32[]{:S(2)}) collective-permute-start(bf16[144,640]{1,0:T(8,128)(2,1)S(1)} %get-tuple-element.35), channel_id=1, source_target_pairs={{0,2},{1,3},{8,10},{9,11},{16,18},{17,19},{24,26},{25,27}} | collective-permute-start | bytes 552968 | tf_op jit(solution)/shard_map/ppermute | solution.py:190
  320.0 12.6 %collective-permute-start.15 = (bf16[144,640]{1,0:T(8,128)(2,1)S(1)}, bf16[144,640]{1,0:T(8,128)(2,1)S(1)}, u32[]{:S(2)}, u32[]{:S(2)}) collective-permute-start(bf16[144,640]{1,0:T(8,128)(2,1)S(1)} %get-tuple-element.36), channel_id=1, source_target_pairs={{6,4},{7,5},{14,12},{15,13},{22,20},{23,21},{30,28},{31,29}} | collective-permute-start | bytes 552968 | tf_op jit(solution)/shard_map/ppermute | solution.py:190
  329.9 8.3 %collective-permute-start.13 = (bf16[144,640]{1,0:T(8,128)(2,1)S(1)}, bf16[144,640]{1,0:T(8,128)(2,1)S(1)}, u32[]{:S(2)}, u32[]{:S(2)}) collective-permute-start(bf16[144,640]{1,0:T(8,128)(2,1)S(1)} %fusion.17), channel_id=1, source_target_pairs={{0,2},{1,3},{2,4},{3,5},{8,10},{9,11},{10,12},{11,13},{16,18},{17,... | collective-permute-start | bytes 552968 | tf_op jit(solution)/shard_map/ppermute | solution.py:190
  338.4 7.4 %collective-permute-start.16 = (bf16[144,640]{1,0:T(8,128)(2,1)S(1)}, bf16[144,640]{1,0:T(8,128)(2,1)S(1)}, u32[]{:S(2)}, u32[]{:S(2)}) collective-permute-start(bf16[144,640]{1,0:T(8,128)(2,1)S(1)} %get-tuple-element.34), channel_id=1, source_target_pairs={{4,2},{5,3},{6,4},{7,5},{12,10},{13,11},{14,12},{15,13},{20,18},{2... | collective-permute-start | bytes 552968 | tf_op jit(solution)/shard_map/ppermute | solution.py:190
  340.5 8.1 %collective-permute-start.14 = (bf16[144,640]{1,0:T(8,128)(2,1)S(1)}, bf16[144,640]{1,0:T(8,128)(2,1)S(1)}, u32[]{:S(2)}, u32[]{:S(2)}) collective-permute-start(bf16[144,640]{1,0:T(8,128)(2,1)S(1)} %get-tuple-element.33), channel_id=1, source_target_pairs={{0,2},{1,3},{2,4},{3,5},{4,6},{5,7},{8,10},{9,11},{10,12},{11,13},... | collective-permute-start | bytes 552968 | tf_op jit(solution)/shard_map/ppermute | solution.py:190
  345.9 7.4 %collective-permute-start.17 = (bf16[144,640]{1,0:T(8,128)(2,1)S(1)}, bf16[144,640]{1,0:T(8,128)(2,1)S(1)}, u32[]{:S(2)}, u32[]{:S(2)}) collective-permute-start(bf16[144,640]{1,0:T(8,128)(2,1)S(1)} %fusion.16), channel_id=1, source_target_pairs={{2,0},{3,1},{4,2},{5,3},{6,4},{7,5},{10,8},{11,9},{12,10},{13,11},... | collective-permute-start | bytes 552968 | tf_op jit(solution)/shard_map/ppermute | solution.py:190
Sparse Core Ops, SparseCore 0:
  11.1 97.7 all-gather.4
  111.1 116.9 all-gather.6
  230.4 42.6 reduce-scatter.2
  275.5 62.4 reduce-scatter.4

commit v2 on v1

--- a/solution.py
+++ b/solution.py
@@ -182,6 +182,17 @@
     )(place, grad, weight, *after)
 
 
+def gate(value, after):
+    anywhere = pl.BlockSpec(memory_space=pl.ANY)
+    return pl.pallas_call(
+        lambda *refs: None,
+        in_specs=[anywhere] * (1 + len(after)),
+        out_specs=anywhere,
+        out_shape=jax.ShapeDtypeStruct(value.shape, value.dtype),
+        input_output_aliases={0: 0},
+    )(value, *after)
+
+
 def lane_pairs(pairs):
     return [(2 * a + core, 2 * b + core) for a, b in pairs for core in (0, 1)]
 
@@ -226,18 +237,29 @@
 
 
 class LowSum:
-    def __init__(self, low, chips):
-        self.chips, self.low = chips, low
-        self.other = swap_cores(low, chips)
-
-    def spread(self):
-        self.mine = add(self.low, self.other).astype(BF16)
-        chips = self.chips
-        self.got = [send(self.mine, [(z, (z + d) % chips) for z in range(chips)]) for d in range(1, chips)]
-        return [self.mine]
+    def __init__(self, low, core, chips):
+        self.core, self.chips, self.step = core, chips, 0
+        half = low.shape[0] // 2
+        first, second = low[:half], low[half:]
+        got = swap_cores(jnp.where(core == 0, second, first), chips)
+        self.mine = add(jnp.where(core == 0, first, second), got)
+        self.up = self.down = jnp.zeros(self.mine.shape, F32)
+
+    def hop(self, after):
+        s, chips = self.step, self.chips
+        self.step += 1
+        to_up = gate((self.mine + self.up).astype(BF16), after)
+        to_down = (self.mine + self.down).astype(BF16)
+        self.up = self.up + send(to_up, [(s, s + 1)]).astype(F32)
+        self.down = self.down + send(to_down, [(chips - 1 - s, chips - 2 - s)]).astype(F32)
+        return [to_up, to_down]
 
     def result(self):
-        return add(self.mine, *self.got).astype(BF16)
+        total = (self.mine + self.up + self.down).astype(BF16)
+        other = swap_cores(total, self.chips)
+        return jnp.concatenate(
+            [jnp.where(self.core == 0, total, other), jnp.where(self.core == 0, other, total)], axis=0
+        )
 
 
 def sum_rows(value):
@@ -275,7 +297,8 @@
 ):
     chips = lax.axis_size("col") // 2
     col_index = lax.axis_index("col")
-    place = jnp.stack([lax.div(col_index, 2), lax.rem(col_index, 2)]).astype(jnp.int32)
+    core = lax.rem(col_index, 2)
+    place = jnp.stack([lax.div(col_index, 2), core]).astype(jnp.int32)
     tok_rows, width = token_grad.shape
     features, ff = inner_weight.shape
     rank = inner_down.shape[1]
@@ -307,31 +330,33 @@
     for index, (both, first) in enumerate(zip(gathered, firsts)):
         after = []
         if index:
-            shares = moving
-            while shares.left():
-                after = shares.hop()
-            after = after + lows[-1].spread()
+            while moving.left():
+                sent = moving.hop()
+                after = sent + summing.hop(sent)
         grad_pre, low, grad = hidden_call(
             both, inner_cat, outer_cat, bias, up_hi, down_lo, down_hi, ff, after
         )
         after = []
         if index:
-            near.append(shares.result())
-            lows[-1] = lows[-1].result()
+            near.append(moving.result())
+            lows.append(summing.result())
             after = [near[-1], lows[-1]]
         share, own, other = share_call(place, grad_pre, inner_cat, chips, first, after)
         far.append(lax.psum_scatter(share, "col", scatter_dimension=0))
         moving = Shares(own, other, chips)
-        lows.append(LowSum(low, chips))
+        summing = LowSum(low, core, chips)
         grads = grad if grads is None else grads + grad
+    hidden_part = (grads[:, :ff] * scale).astype(BF16)
     while moving.left():
-        moving.hop()
+        sent = moving.hop()
+        summing.hop(sent)
+        if moving.step == 1:
+            hidden_part = gate(hidden_part, sent)
     near.append(moving.result())
-    lows[-1].spread()
-    lows[-1] = lows[-1].result()
+    lows.append(summing.result())
     tokens_grad = jnp.concatenate([part for pair in zip(near, far) for part in pair], axis=0)
 
-    hidden_sums = sum_rows((grads[:, :ff] * scale).astype(BF16))
+    hidden_sums = sum_rows(hidden_part)
     inner_up_grad = hidden_sums[:rank]
     outer_down_grad = hidden_sums[rank:].T
 

time: 364 us -> 368 us (1.011)
  other arithmetic: 36.1 us -> 57.9 us
  starting transfers between devices: 70.3 us -> 53.6 us
  waiting for transfers between devices: 142 us -> 134 us
  local copies, waits for them, and re-layouts: 5.72 us -> 10.4 us
    ppermute x18 -> x24, starting transfers between devices: 61.4 us -> 42.1 us  [send(): return lax.ppermute(value, 'col', lane_pairs(pairs))]
    convert_element_type x8, other arithmetic: 1.85 us -> 11.1 us  [hop(): up, down = (up.astype(BF16), down.astype(BF16))]
    convert_element_type x5 -> x11, other arithmetic: 0.31 us -> 9.01 us  [the longest x5 4.47 us: hop(): to_up = gate((self.mine + self.up).astype(BF16), after)]
    ppermute x18 -> x24, waiting for transfers between devices: 64.7 us -> 59.5 us  [send(): return lax.ppermute(value, 'col', lane_pairs(pairs))]
    unnamed x24 -> x80, local copies, waits for them, and re-layouts: 2.56 us -> 7.29 us
  transfers between devices with their start and end apart: 33 -> 41, of which waited for: 13 -> 12; matrix products, arithmetic and copies ran while one was open for 10% -> 16% of each run, Pallas kernels for 25% -> 25%
where the time goes in v2:
time: 368 us; the launch traced here: 366 us
  waiting for transfers between devices  134 us (36%)
  Pallas kernels  92.3 us (25%)
  other arithmetic  57.9 us (16%)
  starting transfers between devices  53.6 us (15%)
  between operations  14.5 us (4%)
  local copies, waits for them, and re-layouts  10.4 us (3%)
    all_gather x2, waiting for transfers between devices, local(): gathered.append(lax.all_gather(both, 'col', axis=0))  69.3 us
    pallas_call x2, Pallas kernels, hidden_call(): pl.pallas_call(functools.partial(hidden_kernel, ff), grid=(steps,), in_sp...  62.3 us
    ppermute x24, waiting for transfers between devices, send(): return lax.ppermute(value, 'col', lane_pairs(pairs))  59.5 us
    ppermute x24, starting transfers between devices, send(): return lax.ppermute(value, 'col', lane_pairs(pairs))  42.1 us
    pallas_call x2, Pallas kernels, share_call(): pl.pallas_call(share_kernel, grid_spec=pltpu.PrefetchScalarGridSpec(num_s...  30 us
    concatenate x1, other arithmetic, local(): inner_cat = jnp.concatenate([inner_weight.T, blank, inner_down.T], axis=0)  25.9 us
    convert_element_type x8, other arithmetic, hop(): up, down = (up.astype(BF16), down.astype(BF16))  11.1 us
  transfers between devices with their start and end apart: 41, of which 12 were waited for; matrix products, arithmetic and copies ran while one was open for 16% of the time, Pallas kernels for 25%

profile of v2, /device:TPU:8, one launch (start us, length us, event | category | flops | bytes accessed | tf_op | source)
XLA Modules:
  0.0 366.2 jit_solution(251925835798048117)
XLA Ops:
  7.2 1.5 slice_bitcast_fusion.1
  14.1 25.9 %pad_maximum_fusion = (bf16[1792,5120]{1,0:T(8,128)(2,1)}, bf16[1792,5120]{1,0:T(8,128)(2,1)}) fusion(bf16[64,5120]{1,0:T(8,128)(2,1)S(1)} %bitcast.70, bf16[1728,5120]{1,0:T(8,128)(2,1)} %bitcast.68, bf16[64,5120]{1,0:T(8,128)(2,1)S(1)} %copy-done.20, bf16[1728,5120]{1,0:T(8,128)(2,1)} %bitcast.69), kind=kLoop, calls=%fused_computation | loop fusion | flops 73400320 | bytes 73400320 | tf_op jit(solution)/shard_map/concatenate | solution.py:322
  40.0 69.2 %all-gather.5.cloned.1.call-done = bf16[16,512,640]{2,1,0:T(8,128)(2,1)} async-done(((bf16[2,512,640]{2,1,0:T(8,128)(2,1)}), bf16[16,512,640]{2,1,0:T(8,128)(2,1)}) %all-gather.5.cloned.1.call-update) | async-done | bytes 10485776 | tf_op jit(solution)/shard_map/all_gather | solution.py:317
  109.2 30.9 %shard_map.137 = (bf16[512,1792]{1,0:T(8,128)(2,1)}, bf16[512,128]{1,0:T(8,128)(2,1)S(1)}, f32[128,1792]{1,0:T(8,128)}) custom-call(bf16[8,2,512,640]{3,2,1,0:T(8,128)(2,1)} %bitcast.75, bf16[1792,5120]{1,0:T(8,128)(2,1)} %get-tuple-element.61.inner_ref.weight_ref, bf16[1792,5120]{1,0:T(8,128)(2,1)} %get-tuple-element.62.outer_ref, ...), custom_call_target="tpu_custom_call" | custom-call | flops 20000000000 | bytes 36000000 | tf_op jit(solution)/shard_map/pallas_call | solution.py:97
  140.1 14.8 %shard_map.138 = (bf16[8,320,640]{2,1,0:T(8,128)(2,1)}, bf16[4,192,640]{2,1,0:T(8,128)(2,1)S(1)}, bf16[4,192,640]{2,1,0:T(8,128)(2,1)S(1)}) custom-call(s32[2]{0:T(128)S(1)} %pad_add_fusion.place_ref, bf16[512,1792]{1,0:T(8,128)(2,1)} %get-tuple-element.17.grad_ref, bf16[1792,5120]{1,0:T(8,128)(2,1)} %get-tuple-element.61.inner_ref.weight_ref), custom_call_target="tpu_custom_call" | custom-call | flops 20000000000 | bytes 36000000 | tf_op jit(solution)/shard_map/pallas_call | solution.py:159
  155.6 2.0 collective-permute-done.7
  158.3 1.9 bitcast_convert_fusion.1
  161.0 1.3 collective-permute-start.11
  162.3 1.3 collective-permute-start.1
  163.6 1.3 collective-permute-start.8
  167.3 8.9 %collective-permute-done.11 = bf16[256,128]{1,0:T(8,128)(2,1)S(1)} collective-permute-done((bf16[256,128]{1,0:T(8,128)(2,1)S(1)}, bf16[256,128]{1,0:T(8,128)(2,1)S(1)}, u32[]{:S(2)}, u32[]{:S(2)}) %collective-permute-start.11) | collective-permute-done | bytes 65568 | tf_op jit(solution)/shard_map/ppermute | solution.py:201
  176.2 4.9 %collective-permute-done.8 = bf16[256,128]{1,0:T(8,128)(2,1)S(1)} collective-permute-done((bf16[256,128]{1,0:T(8,128)(2,1)}, bf16[256,128]{1,0:T(8,128)(2,1)S(1)}, u32[]{:S(2)}, u32[]{:S(2)}) %collective-permute-start.8) | collective-permute-done | bytes 65568 | tf_op jit(solution)/shard_map/ppermute | solution.py:201
  181.7 16.9 %collective-permute-done.5 = bf16[192,640]{1,0:T(8,128)(2,1)S(1)} collective-permute-done((bf16[192,640]{1,0:T(8,128)(2,1)S(1)}, bf16[192,640]{1,0:T(8,128)(2,1)S(1)}, u32[]{:S(2)}, u32[]{:S(2)}) %collective-permute-start.5) | collective-permute-done | bytes 245792 | tf_op jit(solution)/shard_map/ppermute | solution.py:201
  198.6 2.0 fusion.10
  200.6 1.6 collective-permute-start.9
  202.2 1.9 collective-permute-start.2
  204.1 3.9 %collective-permute-start.13 = (bf16[256,128]{1,0:T(8,128)(2,1)S(1)}, bf16[256,128]{1,0:T(8,128)(2,1)S(1)}, u32[]{:S(2)}, u32[]{:S(2)}) collective-permute-start(bf16[256,128]{1,0:T(8,128)(2,1)S(1)} %get-tuple-element.59.refs_3_), channel_id=1, source_target_pairs={{2,0},{3,1},{10,8},{11,9},{18,16},{19,17},{26,24},{27,25}} | collective-permute-start | bytes 196616 | tf_op jit(solution)/shard_map/ppermute | solution.py:201
  208.8 9.3 %collective-permute-done.2 = bf16[192,640]{1,0:T(8,128)(2,1)S(1)} collective-permute-done((bf16[192,640]{1,0:T(8,128)(2,1)}, bf16[192,640]{1,0:T(8,128)(2,1)S(1)}, u32[]{:S(2)}, u32[]{:S(2)}) %collective-permute-start.2) | collective-permute-done | bytes 245792 | tf_op jit(solution)/shard_map/ppermute | solution.py:201
  218.1 1.7 fusion.13.refs_1_.refs_0_
  220.5 1.9 collective-permute-start.6
  222.4 3.9 %collective-permute-start.3 = (bf16[192,640]{1,0:T(8,128)(2,1)}, bf16[192,640]{1,0:T(8,128)(2,1)S(1)}, u32[]{:S(2)}, u32[]{:S(2)}) collective-permute-start(bf16[192,640]{1,0:T(8,128)(2,1)} %fusion.13.refs_1_.refs_0_), channel_id=1, source_target_pairs={{0,2},{1,3},{2,4},{3,5},{4,6},{5,7},{8,10},{9,11},{10,12},{11,13},... | collective-permute-start | bytes 737288 | tf_op jit(solution)/shard_map/ppermute | solution.py:201
  228.3 31.4 %shard_map.142 = (bf16[512,1792]{1,0:T(8,128)(2,1)}, bf16[512,128]{1,0:T(8,128)(2,1)S(1)}, f32[128,1792]{1,0:T(8,128)}) custom-call(bf16[8,2,512,640]{3,2,1,0:T(8,128)(2,1)} %bitcast.74, bf16[1792,5120]{1,0:T(8,128)(2,1)} %get-tuple-element.61.inner_ref.weight_ref, bf16[1792,5120]{1,0:T(8,128)(2,1)} %get-tuple-element.62.outer_ref, ...), custom_call_target="tpu_custom_call" | custom-call | flops 20000000000 | bytes 36000000 | tf_op jit(solution)/shard_map/pallas_call | solution.py:97
  260.9 15.1 %shard_map.143 = (bf16[8,368,640]{2,1,0:T(8,128)(2,1)}, bf16[4,144,640]{2,1,0:T(8,128)(2,1)S(1)}, bf16[4,144,640]{2,1,0:T(8,128)(2,1)S(1)}) custom-call(s32[2]{0:T(128)S(1)} %pad_add_fusion.place_ref, bf16[512,1792]{1,0:T(8,128)(2,1)} %get-tuple-element.22.grad_ref, bf16[1792,5120]{1,0:T(8,128)(2,1)} %get-tuple-element.61.inner_ref.weight_ref, ...), custom_call_target="tpu_custom_call" | custom-call | flops 20000000000 | bytes 36000000 | tf_op jit(solution)/shard_map/pallas_call | solution.py:159
  277.2 2.1 fusion.1.refs_0_
  283.4 1.4 collective-permute-start.16
  284.8 1.9 fusion.4
  286.7 1.3 collective-permute-start.19
  288.6 1.4 collective-permute-start.23
  290.0 7.0 %collective-permute-done.16 = bf16[144,640]{1,0:T(8,128)(2,1)} collective-permute-done((bf16[144,640]{1,0:T(8,128)(2,1)}, bf16[144,640]{1,0:T(8,128)(2,1)}, u32[]{:S(2)}, u32[]{:S(2)}) %collective-permute-start.16) | collective-permute-done | bytes 184352 | tf_op jit(solution)/shard_map/ppermute | solution.py:201
  298.7 1.9 collective-permute-start.17
  301.2 1.5 fusion.26.refs_0_
  302.7 9.0 %collective-permute-done.17 = bf16[144,640]{1,0:T(8,128)(2,1)S(1)} collective-permute-done((bf16[144,640]{1,0:T(8,128)(2,1)S(1)}, bf16[144,640]{1,0:T(8,128)(2,1)S(1)}, u32[]{:S(2)}, u32[]{:S(2)}) %collective-permute-start.17) | collective-permute-done | bytes 184352 | tf_op jit(solution)/shard_map/ppermute | solution.py:201
  311.7 1.8 fusion.19
  313.5 1.7 collective-permute-start.24
  315.3 2.0 collective-permute-start.33
  317.3 1.5 collective-permute-start.35
  320.1 1.6 add_convert_fusion.4
  324.4 1.5 collective-permute-start.36
  325.9 1.5 collective-permute-start.34
  328.7 5.4 %collective-permute-start.18 = (bf16[144,640]{1,0:T(8,128)(2,1)}, bf16[144,640]{1,0:T(8,128)(2,1)}, u32[]{:S(2)}, u32[]{:S(2)}) collective-permute-start(bf16[144,640]{1,0:T(8,128)(2,1)} %get-tuple-element.37.refs_1_), channel_id=1, source_target_pairs={{0,2},{1,3},{2,4},{3,5},{4,6},{5,7},{8,10},{9,11},{10,12},{11,13},... | collective-permute-start | bytes 552968 | tf_op jit(solution)/shard_map/ppermute | solution.py:201
  334.8 1.9 collective-permute-start.28
  338.3 1.9 add_bitcast_fusion
  341.2 1.9 convert_add_fusion.3
  343.1 2.5 collective-permute-start.21
  347.3 2.6 collective-permute-start.32
  349.9 2.8 collective-permute-done.21
  353.8 2.7 collective-permute-done.31
  357.3 2.3 pad_maximum_fusion.4
  (178 shorter events, 35.0 us)
Async XLA Ops:
  7.2 102.1 %all-gather.5.cloned.1.call-start = ((), (), s32[]{:S(2)}) async-start(), calls=%async_computation.4 | async-start | bytes 11796480 | tf_op jit(solution)/shard_map/all_gather | solution.py:317
  11.3 215.2 %all-gather.7.cloned.1.call-start = ((), (), s32[]{:S(2)}) async-start(), calls=%async_computation.5 | async-start | bytes 11796480 | tf_op jit(solution)/shard_map/all_gather | solution.py:317
  12.6 344.7 %reduce-scatter.3.cloned.1.call-start = ((), (), s32[]{:S(2)}) async-start(), calls=%async_computation.2 | async-start | bytes 3686400 | tf_op jit(solution)/shard_map/reduce_scatter | solution.py:345
  13.7 95.5 %copy-start.2 = (bf16[128,1792]{1,0:T(8,128)(2,1)}, bf16[128,1792]{1,0:T(8,128)(2,1)S(1)}, u32[]{:S(2)}) copy-start(bf16[128,1792]{1,0:T(8,128)(2,1)S(1)} %get-tuple-element.51.down_hi_ref) | copy-start | bytes 1376260
  154.9 3.4 collective-permute-start
  155.3 2.4 collective-permute-start.7
  155.6 201.8 %reduce-scatter.5.cloned.1.call-start = ((), (), s32[]{:S(2)}) async-start(), calls=%async_computation.3 | async-start | bytes 4239360 | tf_op jit(solution)/shard_map/reduce_scatter | solution.py:345
  157.7 3.3 collective-permute-start.10
  160.2 4.7 %collective-permute-start.4 = (bf16[192,640]{1,0:T(8,128)(2,1)S(1)}, bf16[192,640]{1,0:T(8,128)(2,1)S(1)}, u32[]{:S(2)}, u32[]{:S(2)}) collective-permute-start(bf16[192,640]{1,0:T(8,128)(2,1)S(1)} %get-tuple-element.35.refs_2_), channel_id=1, source_target_pairs={{6,4},{7,5},{14,12},{15,13},{22,20},{23,21},{30,28},{31,29}} | collective-permute-start | bytes 737288 | tf_op jit(solution)/shard_map/ppermute | solution.py:201
  161.0 15.2 %collective-permute-start.11 = (bf16[256,128]{1,0:T(8,128)(2,1)S(1)}, bf16[256,128]{1,0:T(8,128)(2,1)S(1)}, u32[]{:S(2)}, u32[]{:S(2)}) collective-permute-start(bf16[256,128]{1,0:T(8,128)(2,1)S(1)} %fusion.25), channel_id=1, source_target_pairs={{4,2},{5,3},{12,10},{13,11},{20,18},{21,19},{28,26},{29,27}} | collective-permute-start | bytes 196616 | tf_op jit(solution)/shard_map/ppermute | solution.py:201
  162.3 19.4 %collective-permute-start.1 = (bf16[192,640]{1,0:T(8,128)(2,1)}, bf16[192,640]{1,0:T(8,128)(2,1)S(1)}, u32[]{:S(2)}, u32[]{:S(2)}) collective-permute-start(bf16[192,640]{1,0:T(8,128)(2,1)} %get-tuple-element.36.refs_1_), channel_id=1, source_target_pairs={{0,2},{1,3},{8,10},{9,11},{16,18},{17,19},{24,26},{25,27}} | collective-permute-start | bytes 737288 | tf_op jit(solution)/shard_map/ppermute | solution.py:201
  163.6 17.4 %collective-permute-start.8 = (bf16[256,128]{1,0:T(8,128)(2,1)}, bf16[256,128]{1,0:T(8,128)(2,1)S(1)}, u32[]{:S(2)}, u32[]{:S(2)}) collective-permute-start(bf16[256,128]{1,0:T(8,128)(2,1)} %shard_map.139), channel_id=1, source_target_pairs={{0,2},{1,3},{8,10},{9,11},{16,18},{17,19},{24,26},{25,27}} | collective-permute-start | bytes 196616 | tf_op jit(solution)/shard_map/ppermute | solution.py:201
  166.0 34.7 %copy-start.14 = (bf16[192,640]{1,0:T(8,128)(2,1)}, bf16[192,640]{1,0:T(8,128)(2,1)S(1)}, u32[]{:S(2)}) copy-start(bf16[192,640]{1,0:T(8,128)(2,1)S(1)} %fusion.12.refs_2_) | copy-start | bytes 737284
  166.0 32.6 %collective-permute-start.5 = (bf16[192,640]{1,0:T(8,128)(2,1)S(1)}, bf16[192,640]{1,0:T(8,128)(2,1)S(1)}, u32[]{:S(2)}, u32[]{:S(2)}) collective-permute-start(bf16[192,640]{1,0:T(8,128)(2,1)S(1)} %fusion.12.refs_2_), channel_id=1, source_target_pairs={{4,2},{5,3},{6,4},{7,5},{12,10},{13,11},{14,12},{15,13},{20,18},{2... | collective-permute-start | bytes 737288 | tf_op jit(solution)/shard_map/ppermute | solution.py:201
  200.6 7.4 %collective-permute-start.9 = (bf16[256,128]{1,0:T(8,128)(2,1)}, bf16[256,128]{1,0:T(8,128)(2,1)S(1)}, u32[]{:S(2)}, u32[]{:S(2)}) collective-permute-start(bf16[256,128]{1,0:T(8,128)(2,1)} %shard_map.140), channel_id=1, source_target_pairs={{2,4},{3,5},{10,12},{11,13},{18,20},{19,21},{26,28},{27,29}} | collective-permute-start | bytes 196616 | tf_op jit(solution)/shard_map/ppermute | solution.py:201
  202.2 15.9 %collective-permute-start.2 = (bf16[192,640]{1,0:T(8,128)(2,1)}, bf16[192,640]{1,0:T(8,128)(2,1)S(1)}, u32[]{:S(2)}, u32[]{:S(2)}) collective-permute-start(bf16[192,640]{1,0:T(8,128)(2,1)} %get-tuple-element.34.refs_1_), channel_id=1, source_target_pairs={{0,2},{1,3},{2,4},{3,5},{8,10},{9,11},{10,12},{11,13},{16,18},{17,... | collective-permute-start | bytes 737288 | tf_op jit(solution)/shard_map/ppermute | solution.py:201
  204.1 22.2 %collective-permute-start.13 = (bf16[256,128]{1,0:T(8,128)(2,1)S(1)}, bf16[256,128]{1,0:T(8,128)(2,1)S(1)}, u32[]{:S(2)}, u32[]{:S(2)}) collective-permute-start(bf16[256,128]{1,0:T(8,128)(2,1)S(1)} %get-tuple-element.59.refs_3_), channel_id=1, source_target_pairs={{2,0},{3,1},{10,8},{11,9},{18,16},{19,17},{26,24},{27,25}} | collective-permute-start | bytes 196616 | tf_op jit(solution)/shard_map/ppermute | solution.py:201
  219.8 6.5 %collective-permute-start.12 = (bf16[256,128]{1,0:T(8,128)(2,1)}, bf16[256,128]{1,0:T(8,128)(2,1)S(1)}, u32[]{:S(2)}, u32[]{:S(2)}) collective-permute-start(bf16[256,128]{1,0:T(8,128)(2,1)} %shard_map.141.refs_2_), channel_id=1, source_target_pairs={{4,6},{5,7},{12,14},{13,15},{20,22},{21,23},{28,30},{29,31}} | collective-permute-start | bytes 196616 | tf_op jit(solution)/shard_map/ppermute | solution.py:201
  220.5 39.4 %collective-permute-start.6 = (bf16[192,640]{1,0:T(8,128)(2,1)S(1)}, bf16[192,640]{1,0:T(8,128)(2,1)S(1)}, u32[]{:S(2)}, u32[]{:S(2)}) collective-permute-start(bf16[192,640]{1,0:T(8,128)(2,1)S(1)} %copy-done), channel_id=1, source_target_pairs={{2,0},{3,1},{4,2},{5,3},{6,4},{7,5},{10,8},{11,9},{12,10},{13,11},... | collective-permute-start | bytes 737288 | tf_op jit(solution)/shard_map/ppermute | solution.py:201
  222.4 37.4 %collective-permute-start.3 = (bf16[192,640]{1,0:T(8,128)(2,1)}, bf16[192,640]{1,0:T(8,128)(2,1)S(1)}, u32[]{:S(2)}, u32[]{:S(2)}) collective-permute-start(bf16[192,640]{1,0:T(8,128)(2,1)} %fusion.13.refs_1_.refs_0_), channel_id=1, source_target_pairs={{0,2},{1,3},{2,4},{3,5},{4,6},{5,7},{8,10},{9,11},{10,12},{11,13},... | collective-permute-start | bytes 737288 | tf_op jit(solution)/shard_map/ppermute | solution.py:201
  226.4 33.3 %collective-permute-start.14 = (bf16[256,128]{1,0:T(8,128)(2,1)S(1)}, bf16[256,128]{1,0:T(8,128)(2,1)S(1)}, u32[]{:S(2)}, u32[]{:S(2)}) collective-permute-start(bf16[256,128]{1,0:T(8,128)(2,1)S(1)} %add_convert_fusion.5), channel_id=1, source_target_pairs={{0,1},{1,0},{2,3},{3,2},{4,5},{5,4},{6,7},{7,6},{8,9},{9,8},{10,11... | collective-permute-start | bytes 196616 | tf_op jit(solution)/shard_map/ppermute | solution.py:205
  259.8 20.9 %copy-start.30 = (bf16[256,128]{1,0:T(8,128)(2,1)}, bf16[256,128]{1,0:T(8,128)(2,1)S(1)}, u32[]{:S(2)}) copy-start(bf16[256,128]{1,0:T(8,128)(2,1)S(1)} %get-tuple-element.57) | copy-start | bytes 196612
  259.8 20.9 %copy-start.31 = (bf16[256,128]{1,0:T(8,128)(2,1)}, bf16[256,128]{1,0:T(8,128)(2,1)S(1)}, u32[]{:S(2)}) copy-start(bf16[256,128]{1,0:T(8,128)(2,1)S(1)} %get-tuple-element.58) | copy-start | bytes 196612
  276.1 3.3 collective-permute-start.22
  276.7 5.0 %collective-permute-start.15 = (bf16[4,144,640]{2,1,0:T(8,128)(2,1)S(1)}, bf16[4,144,640]{2,1,0:T(8,128)(2,1)S(1)}, u32[]{:S(2)}, u32[]{:S(2)}) collective-permute-start(bf16[4,144,640]{2,1,0:T(8,128)(2,1)S(1)} %get-tuple-element.24), channel_id=1, source_target_pairs={{0,1},{1,0},{2,3},{3,2},{4,5},{5,4},{6,7},{7,6},{8,9},{9,8},{10,11... | collective-permute-start | bytes 2211848 | tf_op jit(solution)/shard_map/ppermute | solution.py:205
  280.1 7.9 %collective-permute-start.26 = (bf16[256,128]{1,0:T(8,128)(2,1)}, bf16[256,128]{1,0:T(8,128)(2,1)S(1)}, u32[]{:S(2)}, u32[]{:S(2)}) collective-permute-start(bf16[256,128]{1,0:T(8,128)(2,1)} %get-tuple-element.29.refs_0_), channel_id=1, source_target_pairs={{6,4},{7,5},{14,12},{15,13},{22,20},{23,21},{30,28},{31,29}} | collective-permute-start | bytes 196616 | tf_op jit(solution)/shard_map/ppermute | solution.py:201
  283.4 13.6 %collective-permute-start.16 = (bf16[144,640]{1,0:T(8,128)(2,1)}, bf16[144,640]{1,0:T(8,128)(2,1)}, u32[]{:S(2)}, u32[]{:S(2)}) collective-permute-start(bf16[144,640]{1,0:T(8,128)(2,1)} %get-tuple-element.39.refs_1_), channel_id=1, source_target_pairs={{0,2},{1,3},{8,10},{9,11},{16,18},{17,19},{24,26},{25,27}} | collective-permute-start | bytes 552968 | tf_op jit(solution)/shard_map/ppermute | solution.py:201
  286.7 16.1 %collective-permute-start.19 = (bf16[144,640]{1,0:T(8,128)(2,1)}, bf16[144,640]{1,0:T(8,128)(2,1)}, u32[]{:S(2)}, u32[]{:S(2)}) collective-permute-start(bf16[144,640]{1,0:T(8,128)(2,1)} %get-tuple-element.40.refs_2_), channel_id=1, source_target_pairs={{6,4},{7,5},{14,12},{15,13},{22,20},{23,21},{30,28},{31,29}} | collective-permute-start | bytes 552968 | tf_op jit(solution)/shard_map/ppermute | solution.py:201
  288.6 26.6 %copy-start.4 = (bf16[128,1728]{1,0:T(8,128)(2,1)S(1)}, bf16[128,1728]{1,0:T(8,128)(2,1)}, u32[]{:S(2)}) copy-start(bf16[128,1728]{1,0:T(8,128)(2,1)} %shard_map.147) | copy-start | bytes 1327108
  288.6 12.0 %collective-permute-start.23 = (bf16[256,128]{1,0:T(8,128)(2,1)}, bf16[256,128]{1,0:T(8,128)(2,1)S(1)}, u32[]{:S(2)}, u32[]{:S(2)}) collective-permute-start(bf16[256,128]{1,0:T(8,128)(2,1)} %shard_map.144), channel_id=1, source_target_pairs={{0,2},{1,3},{8,10},{9,11},{16,18},{17,19},{24,26},{25,27}} | collective-permute-start | bytes 196616 | tf_op jit(solution)/shard_map/ppermute | solution.py:201
  298.7 13.0 %collective-permute-start.17 = (bf16[144,640]{1,0:T(8,128)(2,1)S(1)}, bf16[144,640]{1,0:T(8,128)(2,1)S(1)}, u32[]{:S(2)}, u32[]{:S(2)}) collective-permute-start(bf16[144,640]{1,0:T(8,128)(2,1)S(1)} %fusion.17.refs_1_), channel_id=1, source_target_pairs={{0,2},{1,3},{2,4},{3,5},{8,10},{9,11},{10,12},{11,13},{16,18},{17,... | collective-permute-start | bytes 552968 | tf_op jit(solution)/shard_map/ppermute | solution.py:201
  313.5 20.6 %copy-start.8 = (bf16[256,128]{1,0:T(8,128)(2,1)S(1)}, bf16[256,128]{1,0:T(8,128)(2,1)}, u32[]{:S(2)}) copy-start(bf16[256,128]{1,0:T(8,128)(2,1)} %get-tuple-element.30) | copy-start | bytes 196612
  313.5 20.6 %copy-start.22 = (bf16[256,128]{1,0:T(8,128)(2,1)S(1)}, bf16[256,128]{1,0:T(8,128)(2,1)}, u32[]{:S(2)}) copy-start(bf16[256,128]{1,0:T(8,128)(2,1)} %copy-done.21) | copy-start | bytes 196612
  313.5 6.0 %collective-permute-start.24 = (bf16[256,128]{1,0:T(8,128)(2,1)}, bf16[256,128]{1,0:T(8,128)(2,1)S(1)}, u32[]{:S(2)}, u32[]{:S(2)}) collective-permute-start(bf16[256,128]{1,0:T(8,128)(2,1)} %shard_map.145), channel_id=1, source_target_pairs={{2,4},{3,5},{10,12},{11,13},{18,20},{19,21},{26,28},{27,29}} | collective-permute-start | bytes 196616 | tf_op jit(solution)/shard_map/ppermute | solution.py:201
  315.3 7.7 %collective-permute-start.33 = (bf16[64,1728]{1,0:T(8,128)(2,1)S(1)}, bf16[64,1728]{1,0:T(8,128)(2,1)S(1)}, u32[]{:S(2)}, u32[]{:S(2)}) collective-permute-start(bf16[64,1728]{1,0:T(8,128)(2,1)S(1)} %get-tuple-element.48), channel_id=1, source_target_pairs={{0,8},{8,0},{16,24},{24,16},{1,9},{9,1},{17,25},{25,17},{2,10},{10... | collective-permute-start | bytes 663560 | tf_op jit(solution)/shard_map/ppermute | solution.py:275
  317.3 6.2 %collective-permute-start.35 = (bf16[64,1728]{1,0:T(8,128)(2,1)S(1)}, bf16[64,1728]{1,0:T(8,128)(2,1)S(1)}, u32[]{:S(2)}, u32[]{:S(2)}) collective-permute-start(bf16[64,1728]{1,0:T(8,128)(2,1)S(1)} %get-tuple-element.47), channel_id=1, source_target_pairs={{0,16},{8,24},{16,0},{24,8},{1,17},{9,25},{17,1},{25,9},{2,18},{10... | collective-permute-start | bytes 663560 | tf_op jit(solution)/shard_map/ppermute | solution.py:275
  321.7 12.4 %collective-permute-start.27 = (bf16[256,128]{1,0:T(8,128)(2,1)S(1)}, bf16[256,128]{1,0:T(8,128)(2,1)S(1)}, u32[]{:S(2)}, u32[]{:S(2)}) collective-permute-start(bf16[256,128]{1,0:T(8,128)(2,1)S(1)} %get-tuple-element.56), channel_id=1, source_target_pairs={{4,2},{5,3},{12,10},{13,11},{20,18},{21,19},{28,26},{29,27}} | collective-permute-start | bytes 196616 | tf_op jit(solution)/shard_map/ppermute | solution.py:201
  324.4 13.9 %collective-permute-start.36 = (bf16[64,1728]{1,0:T(8,128)(2,1)}, bf16[64,1728]{1,0:T(8,128)(2,1)}, u32[]{:S(2)}, u32[]{:S(2)}) collective-permute-start(bf16[64,1728]{1,0:T(8,128)(2,1)} %get-tuple-element.45), channel_id=1, source_target_pairs={{0,8},{8,0},{16,24},{24,16},{1,9},{9,1},{17,25},{25,17},{2,10},{10... | collective-permute-start | bytes 663560 | tf_op jit(solution)/shard_map/ppermute | solution.py:275
  325.9 15.3 %collective-permute-start.34 = (bf16[64,1728]{1,0:T(8,128)(2,1)}, bf16[64,1728]{1,0:T(8,128)(2,1)}, u32[]{:S(2)}, u32[]{:S(2)}) collective-permute-start(bf16[64,1728]{1,0:T(8,128)(2,1)} %get-tuple-element.46), channel_id=1, source_target_pairs={{0,16},{8,24},{16,0},{24,8},{1,17},{9,25},{17,1},{25,9},{2,18},{10... | collective-permute-start | bytes 663560 | tf_op jit(solution)/shard_map/ppermute | solution.py:275
  327.4 9.3 %collective-permute-start.20 = (bf16[144,640]{1,0:T(8,128)(2,1)S(1)}, bf16[144,640]{1,0:T(8,128)(2,1)S(1)}, u32[]{:S(2)}, u32[]{:S(2)}) collective-permute-start(bf16[144,640]{1,0:T(8,128)(2,1)S(1)} %copy-done.17), channel_id=1, source_target_pairs={{4,2},{5,3},{6,4},{7,5},{12,10},{13,11},{14,12},{15,13},{20,18},{2... | collective-permute-start | bytes 552968 | tf_op jit(solution)/shard_map/ppermute | solution.py:201
  328.7 21.2 %collective-permute-start.18 = (bf16[144,640]{1,0:T(8,128)(2,1)}, bf16[144,640]{1,0:T(8,128)(2,1)}, u32[]{:S(2)}, u32[]{:S(2)}) collective-permute-start(bf16[144,640]{1,0:T(8,128)(2,1)} %get-tuple-element.37.refs_1_), channel_id=1, source_target_pairs={{0,2},{1,3},{2,4},{3,5},{4,6},{5,7},{8,10},{9,11},{10,12},{11,13},... | collective-permute-start | bytes 552968 | tf_op jit(solution)/shard_map/ppermute | solution.py:201
  334.8 5.3 %collective-permute-start.28 = (bf16[256,128]{1,0:T(8,128)(2,1)}, bf16[256,128]{1,0:T(8,128)(2,1)}, u32[]{:S(2)}, u32[]{:S(2)}) collective-permute-start(bf16[256,128]{1,0:T(8,128)(2,1)} %add_convert_fusion.3), channel_id=1, source_target_pairs={{2,0},{3,1},{10,8},{11,9},{18,16},{19,17},{26,24},{27,25}} | collective-permute-start | bytes 196616 | tf_op jit(solution)/shard_map/ppermute | solution.py:201
  337.5 2.7 collective-permute-start.25
  341.1 4.5 %collective-permute-start.29 = (bf16[256,128]{1,0:T(8,128)(2,1)S(1)}, bf16[256,128]{1,0:T(8,128)(2,1)S(1)}, u32[]{:S(2)}, u32[]{:S(2)}) collective-permute-start(bf16[256,128]{1,0:T(8,128)(2,1)S(1)} %add_convert_fusion.2), channel_id=1, source_target_pairs={{0,1},{1,0},{2,3},{3,2},{4,5},{5,4},{6,7},{7,6},{8,9},{9,8},{10,11... | collective-permute-start | bytes 196616 | tf_op jit(solution)/shard_map/ppermute | solution.py:205
  343.1 9.6 %collective-permute-start.21 = (bf16[144,640]{1,0:T(8,128)(2,1)S(1)}, bf16[144,640]{1,0:T(8,128)(2,1)S(1)}, u32[]{:S(2)}, u32[]{:S(2)}) collective-permute-start(bf16[144,640]{1,0:T(8,128)(2,1)S(1)} %copy-done.16), channel_id=1, source_target_pairs={{2,0},{3,1},{4,2},{5,3},{6,4},{7,5},{10,8},{11,9},{12,10},{13,11},... | collective-permute-start | bytes 552968 | tf_op jit(solution)/shard_map/ppermute | solution.py:201
  346.4 7.4 %collective-permute-start.30 = (bf16[128,640]{1,0:T(8,128)(2,1)S(1)}, bf16[128,640]{1,0:T(8,128)(2,1)S(1)}, u32[]{:S(2)}, u32[]{:S(2)}) collective-permute-start(bf16[128,640]{1,0:T(8,128)(2,1)S(1)} %fusion.23), channel_id=1, source_target_pairs={{0,8},{8,0},{16,24},{24,16},{1,9},{9,1},{17,25},{25,17},{2,10},{10... | collective-permute-start | bytes 491528 | tf_op jit(solution)/shard_map/ppermute | solution.py:286
  347.0 9.5 %collective-permute-start.31 = (bf16[128,640]{1,0:T(8,128)(2,1)S(1)}, bf16[128,640]{1,0:T(8,128)(2,1)S(1)}, u32[]{:S(2)}, u32[]{:S(2)}) collective-permute-start(bf16[128,640]{1,0:T(8,128)(2,1)S(1)} %fusion.23), channel_id=1, source_target_pairs={{0,16},{8,24},{16,0},{24,8},{1,17},{9,25},{17,1},{25,9},{2,18},{10... | collective-permute-start | bytes 491528 | tf_op jit(solution)/shard_map/ppermute | solution.py:286
  347.3 9.2 %collective-permute-start.32 = (bf16[128,640]{1,0:T(8,128)(2,1)S(1)}, bf16[128,640]{1,0:T(8,128)(2,1)S(1)}, u32[]{:S(2)}, u32[]{:S(2)}) collective-permute-start(bf16[128,640]{1,0:T(8,128)(2,1)S(1)} %fusion.23), channel_id=1, source_target_pairs={{0,24},{8,16},{16,8},{24,0},{1,25},{9,17},{17,9},{25,1},{2,26},{10... | collective-permute-start | bytes 491528 | tf_op jit(solution)/shard_map/ppermute | solution.py:286
  (33 other events, 175.6 us)
Sparse Core Ops, SparseCore 0:
  11.5 97.7 all-gather.4
  111.4 109.6 all-gather.6
  223.5 38.4 reduce-scatter.2
  276.2 50.1 reduce-scatter.4

commit v3 on v2

--- a/solution.py
+++ b/solution.py
@@ -16,7 +16,7 @@
 COLS = 256
 VMEM_BYTES = 52 * 1024 * 1024
 COST = pl.CostEstimate(flops=20_000_000_000, bytes_accessed=36_000_000, transcendentals=0)
-SPLIT = ((512, 384), (512, 288))
+SPLIT = ((512, 256), (512, 0))
 
 
 def dot_nn(left, right):
@@ -127,9 +127,9 @@
     )(both, inner_cat, outer_cat, bias, up, down_lo, down_hi, *after)
 
 
-def share_kernel(place_ref, grad_ref, weight_ref, *refs):
-    share_ref, own_ref, other_ref = refs[-3:]
-    first, width = own_ref.shape[1:]
+def share_kernel(first, place_ref, grad_ref, weight_ref, *refs):
+    share_ref, near_refs = (refs[-3], refs[-2:]) if first else (refs[-1], ())
+    width = share_ref.shape[2]
     if width % LANES == 0:
         share = dot_nn(grad_ref[...], weight_ref[...]).astype(BF16)
         shares = [share[:, :width], share[:, width:]]
@@ -140,24 +140,28 @@
         ]
     for part in (0, 1):
         share_ref[part] = shares[part][first:]
-
-    @pl.when(place_ref[1] == 0)
-    def _():
-        own_ref[0], other_ref[0] = shares[0][:first], shares[1][:first]
-
-    @pl.when(place_ref[1] != 0)
-    def _():
-        own_ref[0], other_ref[0] = shares[1][:first], shares[0][:first]
+    for turn, near_ref in enumerate(near_refs):
+
+        @pl.when(place_ref[1] == 0)
+        def _():
+            near_ref[0] = shares[turn][:first]
+
+        @pl.when(place_ref[1] != 0)
+        def _():
+            near_ref[0] = shares[1 - turn][:first]
 
 
 def share_call(place, grad, weight, chips, first, after=()):
     tokens, padded = grad.shape
     width = weight.shape[1] // (2 * chips)
     there = lambda j, place: lax.rem(place[0] + j, chips)
-    near = pl.BlockSpec((1, first, width), lambda j, place: (j, 0, 0))
-    near_shape = jax.ShapeDtypeStruct((chips, first, width), BF16)
+    out_specs = [pl.BlockSpec((2, tokens - first, width), lambda j, place: (there(j, place), 0, 0))]
+    out_shape = [jax.ShapeDtypeStruct((2 * chips, tokens - first, width), BF16)]
+    if first:
+        out_specs += [pl.BlockSpec((1, first, width), lambda j, place: (j, 0, 0))] * 2
+        out_shape += [jax.ShapeDtypeStruct((chips, first, width), BF16)] * 2
     return pl.pallas_call(
-        share_kernel,
+        functools.partial(share_kernel, first),
         grid_spec=pltpu.PrefetchScalarGridSpec(
             num_scalar_prefetch=1,
             grid=(chips,),
@@ -166,17 +170,9 @@
                 pl.BlockSpec((padded, 2 * width), lambda j, place: (0, there(j, place))),
             ]
             + [pl.BlockSpec(memory_space=pl.ANY)] * len(after),
-            out_specs=[
-                pl.BlockSpec((2, tokens - first, width), lambda j, place: (there(j, place), 0, 0)),
-                near,
-                near,
-            ],
+            out_specs=out_specs,
         ),
-        out_shape=[
-            jax.ShapeDtypeStruct((2 * chips, tokens - first, width), BF16),
-            near_shape,
-            near_shape,
-        ],
+        out_shape=out_shape,
         compiler_params=pltpu.CompilerParams(vmem_limit_bytes=VMEM_BYTES),
         cost_estimate=COST,
     )(place, grad, weight, *after)
@@ -248,11 +244,15 @@
     def hop(self, after):
         s, chips = self.step, self.chips
         self.step += 1
-        to_up = gate((self.mine + self.up).astype(BF16), after)
+        to_up = (self.mine + self.up).astype(BF16)
+        to_up = gate(to_up, after) if after else to_up
         to_down = (self.mine + self.down).astype(BF16)
         self.up = self.up + send(to_up, [(s, s + 1)]).astype(F32)
         self.down = self.down + send(to_down, [(chips - 1 - s, chips - 2 - s)]).astype(F32)
         return [to_up, to_down]
+
+    def left(self):
+        return self.chips - 1 - self.step
 
     def result(self):
         total = (self.mine + self.up + self.down).astype(BF16)
@@ -326,35 +326,32 @@
     down_hi = jnp.pad(outer_down.T, ((LANES - rank, 0), (0, padded - ff)))
     down_lo = jnp.pad(outer_down.T, ((0, LANES - rank), (0, padded - ff)))
 
-    near, far, lows, grads = [], [], [], None
+    far, moving, lows, grads = [], [], [], None
     for index, (both, first) in enumerate(zip(gathered, firsts)):
-        after = []
-        if index:
-            while moving.left():
-                sent = moving.hop()
-                after = sent + summing.hop(sent)
+        def advance(left):
+            sent = []
+            while index and lows[-1].left() > left:
+                ready = moving[-1].hop() if moving[-1] else []
+                sent = ready + lows[-1].hop(ready)
+            return sent
+
         grad_pre, low, grad = hidden_call(
-            both, inner_cat, outer_cat, bias, up_hi, down_lo, down_hi, ff, after
+            both, inner_cat, outer_cat, bias, up_hi, down_lo, down_hi, ff, advance(0)
         )
-        after = []
-        if index:
-            near.append(moving.result())
-            lows.append(summing.result())
-            after = [near[-1], lows[-1]]
-        share, own, other = share_call(place, grad_pre, inner_cat, chips, first, after)
+        share, *shares = share_call(place, grad_pre, inner_cat, chips, first)
         far.append(lax.psum_scatter(share, "col", scatter_dimension=0))
-        moving = Shares(own, other, chips)
-        summing = LowSum(low, core, chips)
+        moving.append(Shares(*shares, chips) if first else None)
+        lows.append(LowSum(low, core, chips))
         grads = grad if grads is None else grads + grad
     hidden_part = (grads[:, :ff] * scale).astype(BF16)
-    while moving.left():
-        sent = moving.hop()
-        summing.hop(sent)
-        if moving.step == 1:
-            hidden_part = gate(hidden_part, sent)
-    near.append(moving.result())
-    lows.append(summing.result())
-    tokens_grad = jnp.concatenate([part for pair in zip(near, far) for part in pair], axis=0)
+    while lows[-1].left():
+        ready = moving[-1].hop() if moving[-1] else []
+        lows[-1].hop(ready)
+    lows = [summing.result() for summing in lows]
+    outs = []
+    for shares, rest in zip(moving, far):
+        outs += [shares.result(), rest] if shares else [rest]
+    tokens_grad = jnp.concatenate(outs, axis=0)
 
     hidden_sums = sum_rows(hidden_part)
     inner_up_grad = hidden_sums[:rank]

time: 368 us -> 343 us (0.932)
  other arithmetic: 57.9 us -> 40.4 us
  starting transfers between devices: 53.6 us -> 38 us
  waiting for transfers between devices: 134 us -> 146 us
    ppermute x24 -> x18, starting transfers between devices: 42.1 us -> 29 us  [send(): return lax.ppermute(value, 'col', lane_pairs(pairs))]
    all_gather x2, waiting for transfers between devices: 69.3 us -> 78.8 us  [local(): gathered.append(lax.all_gather(both, 'col', axis=0))]
    convert_element_type x8 -> x4, other arithmetic: 11.1 us -> 3.32 us  [hop(): up, down = (up.astype(BF16), down.astype(BF16))]
    ppermute x24 -> x18, waiting for transfers between devices: 59.5 us -> 56.3 us  [send(): return lax.ppermute(value, 'col', lane_pairs(pairs))]
  transfers between devices with their start and end apart: 41 -> 34, of which waited for: 12 -> 16; matrix products, arithmetic and copies ran while one was open for 16% -> 11% of each run, Pallas kernels for 25% -> 27%
where the time goes in v3:
time: 343 us; the launch traced here: 338 us
  waiting for transfers between devices  146 us (43%)
  Pallas kernels  90.1 us (26%)
  other arithmetic  40.4 us (12%)
  starting transfers between devices  38 us (11%)
  between operations  14.3 us (4%)
  local copies, waits for them, and re-layouts  7.74 us (2%)
    all_gather x2, waiting for transfers between devices, local(): gathered.append(lax.all_gather(both, 'col', axis=0))  78.8 us
    pallas_call x2, Pallas kernels, hidden_call(): pl.pallas_call(functools.partial(hidden_kernel, ff), grid=(steps,), in_sp...  60.6 us
    ppermute x18, waiting for transfers between devices, send(): return lax.ppermute(value, 'col', lane_pairs(pairs))  56.3 us
    pallas_call x2, Pallas kernels, share_call(): pl.pallas_call(functools.partial(share_kernel, first), grid_spec=pltpu.Pr...  29.5 us
    ppermute x18, starting transfers between devices, send(): return lax.ppermute(value, 'col', lane_pairs(pairs))  29 us
    concatenate x1, other arithmetic, local(): inner_cat = jnp.concatenate([inner_weight.T, blank, inner_down.T], axis=0)  25.9 us
  transfers between devices with their start and end apart: 34, of which 16 were waited for; matrix products, arithmetic and copies ran while one was open for 11% of the time, Pallas kernels for 27%

profile of v3, /device:TPU:8, one launch (start us, length us, event | category | flops | bytes accessed | tf_op | source)
XLA Modules:
  0.0 338.1 jit_solution(4828807354966166018)
XLA Ops:
  7.2 1.5 slice_bitcast_fusion.1
  9.8 1.2 pad_maximum_fusion.2
  11.0 1.2 pad_maximum_fusion.3
  13.8 25.9 %pad_maximum_fusion = (bf16[1792,5120]{1,0:T(8,128)(2,1)}, bf16[1792,5120]{1,0:T(8,128)(2,1)}) fusion(bf16[64,5120]{1,0:T(8,128)(2,1)S(1)} %bitcast.47, bf16[1728,5120]{1,0:T(8,128)(2,1)} %bitcast.45, bf16[64,5120]{1,0:T(8,128)(2,1)S(1)} %copy-done.12, bf16[1728,5120]{1,0:T(8,128)(2,1)} %bitcast.46), kind=kLoop, calls=%fused_computation | loop fusion | flops 73400320 | bytes 73400320 | tf_op jit(solution)/shard_map/concatenate | solution.py:322
  39.7 69.2 %all-gather.5.cloned.1.call-done = bf16[16,512,640]{2,1,0:T(8,128)(2,1)} async-done(((bf16[2,512,640]{2,1,0:T(8,128)(2,1)}), bf16[16,512,640]{2,1,0:T(8,128)(2,1)}) %all-gather.5.cloned.1.call-update) | async-done | bytes 10485776 | tf_op jit(solution)/shard_map/all_gather | solution.py:317
  108.9 30.9 %shard_map.137 = (bf16[512,1792]{1,0:T(8,128)(2,1)}, bf16[512,128]{1,0:T(8,128)(2,1)S(1)}, f32[128,1792]{1,0:T(8,128)}) custom-call(bf16[8,2,512,640]{3,2,1,0:T(8,128)(2,1)} %bitcast.52, bf16[1792,5120]{1,0:T(8,128)(2,1)} %get-tuple-element.51.inner_ref.weight_ref, bf16[1792,5120]{1,0:T(8,128)(2,1)} %get-tuple-element.52.outer_ref, ...), custom_call_target="tpu_custom_call" | custom-call | flops 20000000000 | bytes 36000000 | tf_op jit(solution)/shard_map/pallas_call | solution.py:97
  139.7 15.0 %shard_map.138 = (bf16[8,384,640]{2,1,0:T(8,128)(2,1)}, bf16[4,128,640]{2,1,0:T(8,128)(2,1)S(1)}, bf16[4,128,640]{2,1,0:T(8,128)(2,1)S(1)}) custom-call(s32[2]{0:T(128)S(1)} %pad_add_fusion.place_ref, bf16[512,1792]{1,0:T(8,128)(2,1)} %get-tuple-element.14.grad_ref, bf16[1792,5120]{1,0:T(8,128)(2,1)} %get-tuple-element.51.inner_ref.weight_ref), custom_call_target="tpu_custom_call" | custom-call | flops 20000000000 | bytes 36000000 | tf_op jit(solution)/shard_map/pallas_call | solution.py:163
  155.4 1.6 collective-permute-done.7
  158.5 1.3 collective-permute-start.4
  159.9 1.3 collective-permute-start.11
  161.2 1.4 collective-permute-start.1
  162.7 1.3 collective-permute-start.8
  164.0 1.0 fusion.14.refs_2_
  165.0 1.3 collective-permute-start.5
  166.3 10.0 %collective-permute-done.11 = bf16[256,128]{1,0:T(8,128)(2,1)S(1)} collective-permute-done((bf16[256,128]{1,0:T(8,128)(2,1)S(1)}, bf16[256,128]{1,0:T(8,128)(2,1)S(1)}, u32[]{:S(2)}, u32[]{:S(2)}) %collective-permute-start.11) | collective-permute-done | bytes 65568 | tf_op jit(solution)/shard_map/ppermute | solution.py:197
  176.6 1.5 add_convert_fusion.6
  178.1 10.9 %collective-permute-done.5 = bf16[128,640]{1,0:T(8,128)(2,1)S(1)} collective-permute-done((bf16[128,640]{1,0:T(8,128)(2,1)S(1)}, bf16[128,640]{1,0:T(8,128)(2,1)S(1)}, u32[]{:S(2)}, u32[]{:S(2)}) %collective-permute-start.5) | collective-permute-done | bytes 163872 | tf_op jit(solution)/shard_map/ppermute | solution.py:197
  189.9 1.6 collective-permute-start.9
  191.5 2.1 collective-permute-start.2
  193.7 2.7 collective-permute-done.9
  197.1 9.9 %collective-permute-done.2 = bf16[128,640]{1,0:T(8,128)(2,1)S(1)} collective-permute-done((bf16[128,640]{1,0:T(8,128)(2,1)}, bf16[128,640]{1,0:T(8,128)(2,1)S(1)}, u32[]{:S(2)}, u32[]{:S(2)}) %collective-permute-start.2) | collective-permute-done | bytes 163872 | tf_op jit(solution)/shard_map/ppermute | solution.py:197
  207.7 9.6 %all-gather.7.cloned.1.call-done = bf16[16,512,640]{2,1,0:T(8,128)(2,1)} async-done(((bf16[2,512,640]{2,1,0:T(8,128)(2,1)}), bf16[16,512,640]{2,1,0:T(8,128)(2,1)}) %all-gather.7.cloned.1.call-update) | async-done | bytes 10485776 | tf_op jit(solution)/shard_map/all_gather | solution.py:317
  217.3 0.9 copy-done.1
  219.0 29.8 %shard_map.142 = (bf16[512,1792]{1,0:T(8,128)(2,1)}, bf16[512,128]{1,0:T(8,128)(2,1)S(1)}, f32[128,1792]{1,0:T(8,128)}) custom-call(bf16[8,2,512,640]{3,2,1,0:T(8,128)(2,1)} %bitcast.51, bf16[1792,5120]{1,0:T(8,128)(2,1)} %get-tuple-element.51.inner_ref.weight_ref, bf16[1792,5120]{1,0:T(8,128)(2,1)} %get-tuple-element.52.outer_ref, ...), custom_call_target="tpu_custom_call" | custom-call | flops 20000000000 | bytes 36000000 | tf_op jit(solution)/shard_map/pallas_call | solution.py:97
  248.8 1.5 copy-done.5
  250.3 14.5 %shard_map.143 = bf16[8,512,640]{2,1,0:T(8,128)(2,1)} custom-call(s32[2]{0:T(128)S(1)} %pad_add_fusion.place_ref, bf16[512,1792]{1,0:T(8,128)(2,1)S(1)} %copy-done.5, bf16[1792,5120]{1,0:T(8,128)(2,1)} %get-tuple-element.51.inner_ref.weight_ref), custom_call_target="tpu_custom_call" | custom-call | flops 20000000000 | bytes 36000000 | tf_op jit(solution)/shard_map/pallas_call | solution.py:163
  264.8 1.7 collective-permute-start.13
  266.5 1.9 collective-permute-start.6
  269.1 7.1 %collective-permute-start.3 = (bf16[128,640]{1,0:T(8,128)(2,1)S(1)}, bf16[128,640]{1,0:T(8,128)(2,1)S(1)}, u32[]{:S(2)}, u32[]{:S(2)}) collective-permute-start(bf16[128,640]{1,0:T(8,128)(2,1)S(1)} %copy-done.2), channel_id=1, source_target_pairs={{0,2},{1,3},{2,4},{3,5},{4,6},{5,7},{8,10},{9,11},{10,12},{11,13},... | collective-permute-start | bytes 491528 | tf_op jit(solution)/shard_map/ppermute | solution.py:197
  276.4 1.5 fusion.1
  278.0 1.5 collective-permute-start.26
  279.6 1.4 collective-permute-start.16
  281.8 6.0 %collective-permute-done.16 = bf16[256,128]{1,0:T(8,128)(2,1)S(1)} collective-permute-done((bf16[256,128]{1,0:T(8,128)(2,1)S(1)}, bf16[256,128]{1,0:T(8,128)(2,1)S(1)}, u32[]{:S(2)}, u32[]{:S(2)}) %collective-permute-start.16) | collective-permute-done | bytes 65568 | tf_op jit(solution)/shard_map/ppermute | solution.py:197
  287.8 1.2 collective-permute-done.14
  289.0 1.3 collective-permute-start.17
  290.6 1.5 collective-permute-start.28
  292.1 3.2 collective-permute-done.17
  295.3 1.3 collective-permute-start.20
  297.0 7.5 %collective-permute-done.20 = bf16[256,128]{1,0:T(8,128)(2,1)S(1)} collective-permute-done((bf16[256,128]{1,0:T(8,128)(2,1)S(1)}, bf16[256,128]{1,0:T(8,128)(2,1)S(1)}, u32[]{:S(2)}, u32[]{:S(2)}) %collective-permute-start.20) | collective-permute-done | bytes 65568 | tf_op jit(solution)/shard_map/ppermute | solution.py:197
  305.2 1.3 collective-permute-start.21
  306.6 5.7 %collective-permute-done.21 = bf16[256,128]{1,0:T(8,128)(2,1)S(1)} collective-permute-done((bf16[256,128]{1,0:T(8,128)(2,1)S(1)}, bf16[256,128]{1,0:T(8,128)(2,1)S(1)}, u32[]{:S(2)}, u32[]{:S(2)}) %collective-permute-start.21) | collective-permute-done | bytes 65568 | tf_op jit(solution)/shard_map/ppermute | solution.py:197
  312.7 1.4 collective-permute-start.27
  314.7 1.8 collective-permute-start.23
  316.6 0.9 collective-permute-start.24
  318.3 2.8 collective-permute-done.29
  322.7 1.9 collective-permute-done.23
  324.6 3.7 %collective-permute-done.25 = bf16[128,640]{1,0:T(8,128)(2,1)S(1)} collective-permute-done((bf16[128,640]{1,0:T(8,128)(2,1)S(1)}, bf16[128,640]{1,0:T(8,128)(2,1)S(1)}, u32[]{:S(2)}, u32[]{:S(2)}) %collective-permute-start.25) | collective-permute-done | bytes 163872 | tf_op jit(solution)/shard_map/ppermute | solution.py:286
  329.1 2.4 pad_maximum_fusion.4
  (112 shorter events, 15.7 us)
Async XLA Ops:
  7.2 101.7 %all-gather.5.cloned.1.call-start = ((), (), s32[]{:S(2)}) async-start(), calls=%async_computation.4 | async-start | bytes 11796480 | tf_op jit(solution)/shard_map/all_gather | solution.py:317
  7.2 2.3 copy-start.9
  11.0 206.3 %all-gather.7.cloned.1.call-start = ((), (), s32[]{:S(2)}) async-start(), calls=%async_computation.5 | async-start | bytes 11796480 | tf_op jit(solution)/shard_map/all_gather | solution.py:317
  12.2 1.3 copy-start.11
  12.3 1.5 copy-start.12
  12.3 316.8 %reduce-scatter.3.cloned.1.call-start = ((), (), s32[]{:S(2)}) async-start(), calls=%async_computation.2 | async-start | bytes 4423680 | tf_op jit(solution)/shard_map/reduce_scatter | solution.py:342
  154.7 174.4 %reduce-scatter.5.cloned.1.call-start = ((), (), s32[]{:S(2)}) async-start(), calls=%async_computation.3 | async-start | bytes 5898240 | tf_op jit(solution)/shard_map/reduce_scatter | solution.py:342
  154.8 3.0 collective-permute-start
  155.2 1.9 collective-permute-start.7
  157.1 2.8 copy-start.7
  157.1 2.8 copy-start.15
  157.1 2.8 collective-permute-start.10
  158.5 2.7 copy-start.14
  158.5 5.4 %collective-permute-start.4 = (bf16[128,640]{1,0:T(8,128)(2,1)S(1)}, bf16[128,640]{1,0:T(8,128)(2,1)}, u32[]{:S(2)}, u32[]{:S(2)}) collective-permute-start(bf16[128,640]{1,0:T(8,128)(2,1)S(1)} %get-tuple-element.31.refs_2_), channel_id=1, source_target_pairs={{6,4},{7,5},{14,12},{15,13},{22,20},{23,21},{30,28},{31,29}} | collective-permute-start | bytes 491528 | tf_op jit(solution)/shard_map/ppermute | solution.py:197
  159.9 16.3 %collective-permute-start.11 = (bf16[256,128]{1,0:T(8,128)(2,1)S(1)}, bf16[256,128]{1,0:T(8,128)(2,1)S(1)}, u32[]{:S(2)}, u32[]{:S(2)}) collective-permute-start(bf16[256,128]{1,0:T(8,128)(2,1)S(1)} %fusion.19), channel_id=1, source_target_pairs={{4,2},{5,3},{12,10},{13,11},{20,18},{21,19},{28,26},{29,27}} | collective-permute-start | bytes 196616 | tf_op jit(solution)/shard_map/ppermute | solution.py:197
  161.2 35.2 %copy-start.8 = (bf16[256,128]{1,0:T(8,128)(2,1)S(1)}, bf16[256,128]{1,0:T(8,128)(2,1)}, u32[]{:S(2)}) copy-start(bf16[256,128]{1,0:T(8,128)(2,1)} %copy-done.7) | copy-start | bytes 196612
  161.2 16.9 %collective-permute-start.1 = (bf16[128,640]{1,0:T(8,128)(2,1)}, bf16[128,640]{1,0:T(8,128)(2,1)S(1)}, u32[]{:S(2)}, u32[]{:S(2)}) collective-permute-start(bf16[128,640]{1,0:T(8,128)(2,1)} %get-tuple-element.32.refs_1_), channel_id=1, source_target_pairs={{0,2},{1,3},{8,10},{9,11},{16,18},{17,19},{24,26},{25,27}} | collective-permute-start | bytes 491528 | tf_op jit(solution)/shard_map/ppermute | solution.py:197
  162.7 13.9 %collective-permute-start.8 = (bf16[256,128]{1,0:T(8,128)(2,1)}, bf16[256,128]{1,0:T(8,128)(2,1)S(1)}, u32[]{:S(2)}, u32[]{:S(2)}) collective-permute-start(bf16[256,128]{1,0:T(8,128)(2,1)} %shard_map.139), channel_id=1, source_target_pairs={{0,2},{1,3},{8,10},{9,11},{16,18},{17,19},{24,26},{25,27}} | collective-permute-start | bytes 196616 | tf_op jit(solution)/shard_map/ppermute | solution.py:197
  165.0 25.0 %copy-start.13 = (bf16[128,640]{1,0:T(8,128)(2,1)}, bf16[128,640]{1,0:T(8,128)(2,1)S(1)}, u32[]{:S(2)}) copy-start(bf16[128,640]{1,0:T(8,128)(2,1)S(1)} %fusion.14.refs_2_) | copy-start | bytes 491524
  165.0 24.1 %collective-permute-start.5 = (bf16[128,640]{1,0:T(8,128)(2,1)S(1)}, bf16[128,640]{1,0:T(8,128)(2,1)S(1)}, u32[]{:S(2)}, u32[]{:S(2)}) collective-permute-start(bf16[128,640]{1,0:T(8,128)(2,1)S(1)} %fusion.14.refs_2_), channel_id=1, source_target_pairs={{4,2},{5,3},{6,4},{7,5},{12,10},{13,11},{14,12},{15,13},{20,18},{2... | collective-permute-start | bytes 491528 | tf_op jit(solution)/shard_map/ppermute | solution.py:197
  189.9 27.4 %copy-start = (bf16[128,640]{1,0:T(8,128)(2,1)S(1)}, bf16[128,640]{1,0:T(8,128)(2,1)}, u32[]{:S(2)}) copy-start(bf16[128,640]{1,0:T(8,128)(2,1)} %get-tuple-element.29.refs_2_.refs_1_) | copy-start | bytes 491524
  189.9 6.5 %collective-permute-start.9 = (bf16[256,128]{1,0:T(8,128)(2,1)}, bf16[256,128]{1,0:T(8,128)(2,1)S(1)}, u32[]{:S(2)}, u32[]{:S(2)}) collective-permute-start(bf16[256,128]{1,0:T(8,128)(2,1)} %shard_map.140), channel_id=1, source_target_pairs={{2,4},{3,5},{10,12},{11,13},{18,20},{19,21},{26,28},{27,29}} | collective-permute-start | bytes 196616 | tf_op jit(solution)/shard_map/ppermute | solution.py:197
  191.5 15.4 %collective-permute-start.2 = (bf16[128,640]{1,0:T(8,128)(2,1)}, bf16[128,640]{1,0:T(8,128)(2,1)S(1)}, u32[]{:S(2)}, u32[]{:S(2)}) collective-permute-start(bf16[128,640]{1,0:T(8,128)(2,1)} %get-tuple-element.30.refs_1_), channel_id=1, source_target_pairs={{0,2},{1,3},{2,4},{3,5},{8,10},{9,11},{10,12},{11,13},{16,18},{17,... | collective-permute-start | bytes 491528 | tf_op jit(solution)/shard_map/ppermute | solution.py:197
  248.8 1.5 copy-start.5
  264.8 3.7 %copy-start.4 = (bf16[256,128]{1,0:T(8,128)(2,1)S(1)}, bf16[256,128]{1,0:T(8,128)(2,1)}, u32[]{:S(2)}) copy-start(bf16[256,128]{1,0:T(8,128)(2,1)} %shard_map.141.refs_2_) | copy-start | bytes 196612
  264.8 4.3 %copy-start.2 = (bf16[128,640]{1,0:T(8,128)(2,1)S(1)}, bf16[128,640]{1,0:T(8,128)(2,1)}, u32[]{:S(2)}) copy-start(bf16[128,640]{1,0:T(8,128)(2,1)} %fusion.15.refs_1_.refs_0_) | copy-start | bytes 491524
  264.8 14.7 %collective-permute-start.13 = (bf16[256,128]{1,0:T(8,128)(2,1)S(1)}, bf16[256,128]{1,0:T(8,128)(2,1)S(1)}, u32[]{:S(2)}, u32[]{:S(2)}) collective-permute-start(bf16[256,128]{1,0:T(8,128)(2,1)S(1)} %get-tuple-element.49.refs_3_), channel_id=1, source_target_pairs={{2,0},{3,1},{10,8},{11,9},{18,16},{19,17},{26,24},{27,25}} | collective-permute-start | bytes 196616 | tf_op jit(solution)/shard_map/ppermute | solution.py:197
  266.5 38.7 %collective-permute-start.6 = (bf16[128,640]{1,0:T(8,128)(2,1)S(1)}, bf16[128,640]{1,0:T(8,128)(2,1)S(1)}, u32[]{:S(2)}, u32[]{:S(2)}) collective-permute-start(bf16[128,640]{1,0:T(8,128)(2,1)S(1)} %copy-done), channel_id=1, source_target_pairs={{2,0},{3,1},{4,2},{5,3},{6,4},{7,5},{10,8},{11,9},{12,10},{13,11},... | collective-permute-start | bytes 491528 | tf_op jit(solution)/shard_map/ppermute | solution.py:197
  268.5 12.6 %collective-permute-start.12 = (bf16[256,128]{1,0:T(8,128)(2,1)S(1)}, bf16[256,128]{1,0:T(8,128)(2,1)S(1)}, u32[]{:S(2)}, u32[]{:S(2)}) collective-permute-start(bf16[256,128]{1,0:T(8,128)(2,1)S(1)} %copy-done.4), channel_id=1, source_target_pairs={{4,6},{5,7},{12,14},{13,15},{20,22},{21,23},{28,30},{29,31}} | collective-permute-start | bytes 196616 | tf_op jit(solution)/shard_map/ppermute | solution.py:197
  269.1 37.3 %collective-permute-start.3 = (bf16[128,640]{1,0:T(8,128)(2,1)S(1)}, bf16[128,640]{1,0:T(8,128)(2,1)S(1)}, u32[]{:S(2)}, u32[]{:S(2)}) collective-permute-start(bf16[128,640]{1,0:T(8,128)(2,1)S(1)} %copy-done.2), channel_id=1, source_target_pairs={{0,2},{1,3},{2,4},{3,5},{4,6},{5,7},{8,10},{9,11},{10,12},{11,13},... | collective-permute-start | bytes 491528 | tf_op jit(solution)/shard_map/ppermute | solution.py:197
  276.3 1.7 collective-permute-start.15
  277.9 12.4 %copy-start.10 = (bf16[1024,640]{1,0:T(8,128)(2,1)S(1)}, bf16[1024,640]{1,0:T(8,128)(2,1)}, u32[]{:S(2)}) copy-start(bf16[1024,640]{1,0:T(8,128)(2,1)} %param.11) | copy-start | bytes 3932164
  278.0 34.5 %collective-permute-start.26 = (bf16[64,1728]{1,0:T(8,128)(2,1)S(1)}, bf16[64,1728]{1,0:T(8,128)(2,1)S(1)}, u32[]{:S(2)}, u32[]{:S(2)}) collective-permute-start(bf16[64,1728]{1,0:T(8,128)(2,1)S(1)} %get-tuple-element.38), channel_id=1, source_target_pairs={{0,8},{8,0},{16,24},{24,16},{1,9},{9,1},{17,25},{25,17},{2,10},{10... | collective-permute-start | bytes 663560 | tf_op jit(solution)/shard_map/ppermute | solution.py:275
  279.6 17.1 %copy-start.6 = (bf16[1024,640]{1,0:T(8,128)(2,1)S(1)}, bf16[1024,640]{1,0:T(8,128)(2,1)}, u32[]{:S(2)}) copy-start(bf16[1024,640]{1,0:T(8,128)(2,1)} %param.10) | copy-start | bytes 3932164
  279.6 8.2 %collective-permute-start.16 = (bf16[256,128]{1,0:T(8,128)(2,1)S(1)}, bf16[256,128]{1,0:T(8,128)(2,1)S(1)}, u32[]{:S(2)}, u32[]{:S(2)}) collective-permute-start(bf16[256,128]{1,0:T(8,128)(2,1)S(1)} %get-tuple-element.23), channel_id=1, source_target_pairs={{0,2},{1,3},{8,10},{9,11},{16,18},{17,19},{24,26},{25,27}} | collective-permute-start | bytes 196616 | tf_op jit(solution)/shard_map/ppermute | solution.py:197
  281.0 9.6 %collective-permute-start.19 = (bf16[256,128]{1,0:T(8,128)(2,1)S(1)}, bf16[256,128]{1,0:T(8,128)(2,1)S(1)}, u32[]{:S(2)}, u32[]{:S(2)}) collective-permute-start(bf16[256,128]{1,0:T(8,128)(2,1)S(1)} %get-tuple-element.23), channel_id=1, source_target_pairs={{6,4},{7,5},{14,12},{15,13},{22,20},{23,21},{30,28},{31,29}} | collective-permute-start | bytes 196616 | tf_op jit(solution)/shard_map/ppermute | solution.py:197
  287.8 1.3 collective-permute-start.14
  289.0 6.2 %collective-permute-start.17 = (bf16[256,128]{1,0:T(8,128)(2,1)S(1)}, bf16[256,128]{1,0:T(8,128)(2,1)S(1)}, u32[]{:S(2)}, u32[]{:S(2)}) collective-permute-start(bf16[256,128]{1,0:T(8,128)(2,1)S(1)} %fusion.20), channel_id=1, source_target_pairs={{2,4},{3,5},{10,12},{11,13},{18,20},{19,21},{26,28},{27,29}} | collective-permute-start | bytes 196616 | tf_op jit(solution)/shard_map/ppermute | solution.py:197
  290.6 21.9 %collective-permute-start.28 = (bf16[64,1728]{1,0:T(8,128)(2,1)S(1)}, bf16[64,1728]{1,0:T(8,128)(2,1)S(1)}, u32[]{:S(2)}, u32[]{:S(2)}) collective-permute-start(bf16[64,1728]{1,0:T(8,128)(2,1)S(1)} %get-tuple-element.37), channel_id=1, source_target_pairs={{0,16},{8,24},{16,0},{24,8},{1,17},{9,25},{17,1},{25,9},{2,18},{10... | collective-permute-start | bytes 663560 | tf_op jit(solution)/shard_map/ppermute | solution.py:275
  295.3 9.1 %collective-permute-start.20 = (bf16[256,128]{1,0:T(8,128)(2,1)S(1)}, bf16[256,128]{1,0:T(8,128)(2,1)S(1)}, u32[]{:S(2)}, u32[]{:S(2)}) collective-permute-start(bf16[256,128]{1,0:T(8,128)(2,1)S(1)} %get-tuple-element.46), channel_id=1, source_target_pairs={{4,2},{5,3},{12,10},{13,11},{20,18},{21,19},{28,26},{29,27}} | collective-permute-start | bytes 196616 | tf_op jit(solution)/shard_map/ppermute | solution.py:197
  304.5 2.1 collective-permute-start.18
  305.2 7.1 %collective-permute-start.21 = (bf16[256,128]{1,0:T(8,128)(2,1)S(1)}, bf16[256,128]{1,0:T(8,128)(2,1)S(1)}, u32[]{:S(2)}, u32[]{:S(2)}) collective-permute-start(bf16[256,128]{1,0:T(8,128)(2,1)S(1)} %add_convert_fusion.3), channel_id=1, source_target_pairs={{2,0},{3,1},{10,8},{11,9},{18,16},{19,17},{26,24},{27,25}} | collective-permute-start | bytes 196616 | tf_op jit(solution)/shard_map/ppermute | solution.py:197
  312.4 1.7 collective-permute-start.22
  312.6 8.5 %collective-permute-start.29 = (bf16[64,1728]{1,0:T(8,128)(2,1)S(1)}, bf16[64,1728]{1,0:T(8,128)(2,1)S(1)}, u32[]{:S(2)}, u32[]{:S(2)}) collective-permute-start(bf16[64,1728]{1,0:T(8,128)(2,1)S(1)} %get-tuple-element.35), channel_id=1, source_target_pairs={{0,8},{8,0},{16,24},{24,16},{1,9},{9,1},{17,25},{25,17},{2,10},{10... | collective-permute-start | bytes 663560 | tf_op jit(solution)/shard_map/ppermute | solution.py:275
  312.7 9.2 %collective-permute-start.27 = (bf16[64,1728]{1,0:T(8,128)(2,1)S(1)}, bf16[64,1728]{1,0:T(8,128)(2,1)S(1)}, u32[]{:S(2)}, u32[]{:S(2)}) collective-permute-start(bf16[64,1728]{1,0:T(8,128)(2,1)S(1)} %get-tuple-element.36), channel_id=1, source_target_pairs={{0,16},{8,24},{16,0},{24,8},{1,17},{9,25},{17,1},{25,9},{2,18},{10... | collective-permute-start | bytes 663560 | tf_op jit(solution)/shard_map/ppermute | solution.py:275
  314.7 9.9 %collective-permute-start.23 = (bf16[128,640]{1,0:T(8,128)(2,1)S(1)}, bf16[128,640]{1,0:T(8,128)(2,1)S(1)}, u32[]{:S(2)}, u32[]{:S(2)}) collective-permute-start(bf16[128,640]{1,0:T(8,128)(2,1)S(1)} %fusion.11), channel_id=1, source_target_pairs={{0,8},{8,0},{16,24},{24,16},{1,9},{9,1},{17,25},{25,17},{2,10},{10... | collective-permute-start | bytes 491528 | tf_op jit(solution)/shard_map/ppermute | solution.py:286
  316.6 8.0 %collective-permute-start.24 = (bf16[128,640]{1,0:T(8,128)(2,1)S(1)}, bf16[128,640]{1,0:T(8,128)(2,1)S(1)}, u32[]{:S(2)}, u32[]{:S(2)}) collective-permute-start(bf16[128,640]{1,0:T(8,128)(2,1)S(1)} %fusion.11), channel_id=1, source_target_pairs={{0,16},{8,24},{16,0},{24,8},{1,17},{9,25},{17,1},{25,9},{2,18},{10... | collective-permute-start | bytes 491528 | tf_op jit(solution)/shard_map/ppermute | solution.py:286
  317.5 10.8 %collective-permute-start.25 = (bf16[128,640]{1,0:T(8,128)(2,1)S(1)}, bf16[128,640]{1,0:T(8,128)(2,1)S(1)}, u32[]{:S(2)}, u32[]{:S(2)}) collective-permute-start(bf16[128,640]{1,0:T(8,128)(2,1)S(1)} %fusion.11), channel_id=1, source_target_pairs={{0,24},{8,16},{16,8},{24,0},{1,25},{9,17},{17,9},{25,1},{2,26},{10... | collective-permute-start | bytes 491528 | tf_op jit(solution)/shard_map/ppermute | solution.py:286
  (5 other events, 4.5 us)
Sparse Core Ops, SparseCore 0:
  11.1 97.7 all-gather.4
  111.1 106.1 all-gather.6
  219.6 44.4 reduce-scatter.2
  266.3 62.7 reduce-scatter.4

commit v4 on v0

--- a/solution.py
+++ b/solution.py
@@ -16,7 +16,7 @@
 COLS = 256
 VMEM_BYTES = 52 * 1024 * 1024
 COST = pl.CostEstimate(flops=20_000_000_000, bytes_accessed=36_000_000, transcendentals=0)
-SPLIT = (512, 512)
+SPLIT = (304, 304, 416)
 
 
 def dot_nn(left, right):
@@ -31,10 +31,8 @@
     return lax.dot_general(left, right, (((0,), (0,)), ((), ())), preferred_element_type=F32)
 
 
-def hidden_kernel(
-    ff, both_ref, inner_ref, outer_ref, bias_ref, up_ref, down_lo_ref, down_hi_ref,
-    grad_ref, low_ref, grads_ref, pre_acc, hid_acc, hidden_ref,
-):
+def hidden_kernel(ff, place_ref, both_ref, inner_ref, outer_ref, bias_ref, up_ref, down_lo_ref, down_hi_ref, *refs):
+    grad_ref, low_ref, grads_ref, pre_acc, hid_acc, hidden_ref = refs[-6:]
     step = pl.program_id(0)
     _, _, tokens, width = both_ref.shape
     padded = pre_acc.shape[1]
@@ -91,44 +89,50 @@
                 grad_ref[:, here] = jnp.where(lane + start < ff, grad_ref[:, here], jnp.zeros_like(low))
 
 
-def hidden_call(both, inner_cat, outer_cat, bias, up, down_lo, down_hi, ff):
+def hidden_call(place, both, inner_cat, outer_cat, bias, up, down_lo, down_hi, ff, after=()):
     devices, _, tokens, width = both.shape
     padded = inner_cat.shape[0]
     steps = devices // 2
-    whole = lambda k: (0, 0)
+    whole = lambda k, place: (0, 0)
+    there = lambda k, place: (0, lax.rem(place[0] + k, steps))
     return pl.pallas_call(
         functools.partial(hidden_kernel, ff),
+        grid_spec=pltpu.PrefetchScalarGridSpec(
+        num_scalar_prefetch=1,
         grid=(steps,),
         in_specs=[
-            pl.BlockSpec((2, 2, tokens, width), lambda k: (k, 0, 0, 0)),
-            pl.BlockSpec((padded, 2 * width), lambda k: (0, k)),
-            pl.BlockSpec((padded, 2 * width), lambda k: (0, k)),
+            pl.BlockSpec((2, 2, tokens, width), lambda k, place: (k, 0, 0, 0)),
+            pl.BlockSpec((padded, 2 * width), there),
+            pl.BlockSpec((padded, 2 * width), there),
             pl.BlockSpec((1, padded), whole),
             pl.BlockSpec((LANES, padded), whole),
             pl.BlockSpec((LANES, padded), whole),
             pl.BlockSpec((LANES, padded), whole),
-        ],
+        ]
+        + [pl.BlockSpec(memory_space=pl.ANY)] * len(after),
         out_specs=[
             pl.BlockSpec((tokens, padded), whole),
             pl.BlockSpec((tokens, LANES), whole),
             pl.BlockSpec((LANES, padded), whole),
-        ],
-        out_shape=[
-            jax.ShapeDtypeStruct((tokens, padded), BF16),
-            jax.ShapeDtypeStruct((tokens, LANES), BF16),
-            jax.ShapeDtypeStruct((LANES, padded), F32),
         ],
         scratch_shapes=[
             pltpu.VMEM((tokens, padded), F32),
             pltpu.VMEM((tokens, padded), F32),
             pltpu.VMEM((tokens, padded), BF16),
         ],
+        ),
+        out_shape=[
+            jax.ShapeDtypeStruct((tokens, padded), BF16),
+            jax.ShapeDtypeStruct((tokens, LANES), BF16),
+            jax.ShapeDtypeStruct((LANES, padded), F32),
+        ],
         compiler_params=pltpu.CompilerParams(vmem_limit_bytes=VMEM_BYTES),
         cost_estimate=COST,
-    )(both, inner_cat, outer_cat, bias, up, down_lo, down_hi)
-
-
-def share_kernel(grad_ref, weight_ref, share_ref):
+    )(place, both, inner_cat, outer_cat, bias, up, down_lo, down_hi, *after)
+
+
+def share_kernel(grad_ref, weight_ref, *refs):
+    share_ref = refs[-1]
     width = share_ref.shape[2]
     if width % LANES == 0:
         share = dot_nn(grad_ref[...], weight_ref[...]).astype(BF16)
@@ -139,7 +143,7 @@
             share_ref[part] = dot_nn(grad_ref[...], weight_ref[:, here]).astype(BF16)
 
 
-def share_call(grad, weight, devices):
+def share_call(grad, weight, devices, after=()):
     tokens, padded = grad.shape
     width = weight.shape[1] // devices
     return pl.pallas_call(
@@ -148,12 +152,24 @@
         in_specs=[
             pl.BlockSpec((tokens, padded), lambda j: (0, 0)),
             pl.BlockSpec((padded, 2 * width), lambda j: (0, j)),
-        ],
+        ]
+        + [pl.BlockSpec(memory_space=pl.ANY)] * len(after),
         out_specs=pl.BlockSpec((2, tokens, width), lambda j: (j, 0, 0)),
         out_shape=jax.ShapeDtypeStruct((devices, tokens, width), BF16),
         compiler_params=pltpu.CompilerParams(vmem_limit_bytes=VMEM_BYTES),
         cost_estimate=COST,
-    )(grad, weight)
+    )(grad, weight, *after)
+
+
+def gate(value, after):
+    anywhere = pl.BlockSpec(memory_space=pl.ANY)
+    return pl.pallas_call(
+        lambda *refs: None,
+        in_specs=[anywhere] * (1 + len(after)),
+        out_specs=anywhere,
+        out_shape=jax.ShapeDtypeStruct(value.shape, value.dtype),
+        input_output_aliases={0: 0},
+    )(value, *after)
 
 
 def lane_pairs(pairs):
@@ -175,19 +191,63 @@
     return total
 
 
+class Gather:
+    def __init__(self, block, chips):
+        self.own, self.chips = block, chips
+        self.up, self.down = [block], [block]
+
+    def hop(self, after=()):
+        s, chips = len(self.up), self.chips
+        if s == chips:
+            return []
+        up, down = (gate(value, after) if after else value for value in (self.up[-1], self.down[-1]))
+        self.up.append(send(up, [(z, z + 1) for z in range(s - 1, chips - 1)]))
+        self.down.append(send(down, [(z, z - 1) for z in range(1, chips - s + 1)]))
+        return [up, down]
+
+    def result(self, core):
+        chips = self.chips
+        while len(self.up) < chips:
+            self.hop()
+        mine = [self.own] + [self.down[j] + self.up[chips - j] for j in range(1, chips)]
+        ends = sorted({1, chips - 1})
+        rest = [j for j in range(chips) if j not in ends]
+        other = [None] * chips
+        for group in (rest, ends):
+            got = swap_cores(jnp.stack([mine[j] for j in group]), chips)
+            for place, j in enumerate(group):
+                other[j] = got[place]
+        pairs = [(jnp.where(core == 0, a, b), jnp.where(core == 0, b, a)) for a, b in zip(mine, other)]
+        return jnp.stack([block for pair in pairs for block in pair])
+
+
 class LowSum:
-    def __init__(self, low, chips):
-        self.chips, self.low = chips, low
-        self.other = swap_cores(low, chips)
-
-    def spread(self):
-        self.mine = add(self.low, self.other).astype(BF16)
-        chips = self.chips
-        self.got = [send(self.mine, [(z, (z + d) % chips) for z in range(chips)]) for d in range(1, chips)]
-        return [self.mine]
+    def __init__(self, low, core, chips):
+        self.core, self.chips, self.step = core, chips, 0
+        half = low.shape[0] // 2
+        first, second = low[:half], low[half:]
+        got = swap_cores(jnp.where(core == 0, second, first), chips)
+        self.mine = add(jnp.where(core == 0, first, second), got)
+        self.up = self.down = jnp.zeros(self.mine.shape, F32)
+
+    def hop(self):
+        s, chips = self.step, self.chips
+        self.step += 1
+        to_up = (self.mine + self.up).astype(BF16)
+        to_down = (self.mine + self.down).astype(BF16)
+        self.up = self.up + send(to_up, [(s, s + 1)]).astype(F32)
+        self.down = self.down + send(to_down, [(chips - 1 - s, chips - 2 - s)]).astype(F32)
+        return [to_up, to_down]
+
+    def left(self):
+        return self.chips - 1 - self.step
 
     def result(self):
-        return add(self.mine, *self.got).astype(BF16)
+        total = (self.mine + self.up + self.down).astype(BF16)
+        other = swap_cores(total, self.chips)
+        return jnp.concatenate(
+            [jnp.where(self.core == 0, total, other), jnp.where(self.core == 0, other, total)], axis=0
+        )
 
 
 def sum_rows(value):
@@ -225,6 +285,7 @@
 ):
     chips = lax.axis_size("col") // 2
     col_index = lax.axis_index("col")
+    core = lax.rem(col_index, 2)
     tok_rows, width = token_grad.shape
     features, ff = inner_weight.shape
     rank = inner_down.shape[1]
@@ -239,7 +300,8 @@
     for start, size in zip(starts, sizes):
         gated = (gain_local[None, :] * token_grad[start : start + size].astype(F32)).astype(BF16)
         both = jnp.stack([tokens_in[start : start + size], gated])
-        gathered.append(lax.all_gather(both, "col", axis=0))
+        late = start + size == tok_rows
+        gathered.append(Gather(both, chips) if late else lax.all_gather(both, "col", axis=0))
         gated_parts.append(gated)
 
     gap = padded - ff - rank
@@ -251,26 +313,47 @@
     down_hi = jnp.pad(outer_down.T, ((LANES - rank, 0), (0, padded - ff)))
     down_lo = jnp.pad(outer_down.T, ((0, LANES - rank), (0, padded - ff)))
 
-    outs, lows, grads = [], [], None
-    for both in gathered:
-        grad_pre, low, grad = hidden_call(both, inner_cat, outer_cat, bias, up_hi, down_lo, down_hi, ff)
-        share = share_call(grad_pre, inner_cat, 2 * chips)
+    outs, lows, sums, grads = [], [], [], None
+    here = jnp.stack([lax.div(col_index, 2)]).astype(jnp.int32)
+    start_block = jnp.zeros_like(here)
+    coming = gathered[-1]
+    for index, both in enumerate(gathered):
+        late = both is coming
+        after, between = [], []
+        if late:
+            both = both.result(core)
+        elif index:
+            after = coming.up[1:] + coming.down[1:]
+            if len(sums) == 1:
+                sums.append(sums[0].result())
+                after = after + sums[1:]
+            coming.hop()
+        grad_pre, low, grad = hidden_call(
+            here if late else start_block, both, inner_cat, outer_cat, bias, up_hi, down_lo, down_hi, ff, after
+        )
+        if not late:
+            between = coming.hop([low])
+        share = share_call(grad_pre, inner_cat, 2 * chips, between)
         outs.append(lax.psum_scatter(share, "col", scatter_dimension=0))
-        lows.append(LowSum(low, chips))
-        lows[-1].spread()
+        lows.append(low)
+        if not index:
+            sums.append(LowSum(gate(low, [share]), core, chips))
+            while sums[0].left():
+                sums[0].hop()
         grads = grad if grads is None else grads + grad
+    hidden_part = (grads[:, :ff] * scale).astype(BF16)
+    sums.append(LowSum(jnp.concatenate(lows[1:], axis=0), core, chips))
+    while sums[-1].left():
+        sums[-1].hop()
+    low = jnp.concatenate([sums[1], sums[-1].result()], axis=0)
     tokens_grad = jnp.concatenate(outs, axis=0)
 
-    hidden_sums = sum_rows((grads[:, :ff] * scale).astype(BF16))
+    hidden_sums = sum_rows(hidden_part)
     inner_up_grad = hidden_sums[:rank]
     outer_down_grad = hidden_sums[rank:].T
 
-    feature_part = 0.0
-    for start, size, gated, piece in zip(starts, sizes, gated_parts, lows):
-        low, tokens = piece.result(), tokens_in[start : start + size]
-        feature_part = feature_part + jnp.concatenate(
-            [dot_tn(low[:, :rank], gated), dot_tn(low[:, rank:], tokens)], axis=0
-        )
+    gated = jnp.concatenate(gated_parts, axis=0)
+    feature_part = jnp.concatenate([dot_tn(low[:, :rank], gated), dot_tn(low[:, rank:], tokens_in)], axis=0)
     feature_sums = sum_rows_at_once((feature_part * scale).astype(BF16))
     outer_up_grad = feature_sums[:rank]
     inner_down_grad = feature_sums[rank:].T

time: 362 us -> 401 us (1.11)
  waiting for transfers between devices: 186 us -> 146 us
  other arithmetic: 34.6 us -> 60.6 us
  Pallas kernels: 88.5 us -> 114 us
  starting transfers between devices: 24 us -> 42.7 us
  local copies, waits for them, and re-layouts: 8.69 us -> 14.1 us
    all_gather x2, waiting for transfers between devices: 122 us -> 32.2 us  [local(): lax.all_gather(both, 'col', axis=0)]
    ppermute x6 -> x18, waiting for transfers between devices: 16.6 us -> 99.1 us  [send(): return lax.ppermute(value, 'col', lane_pairs(pairs))]
    reduce_scatter x2 -> x3, waiting for transfers between devices: 39.9 us -> 4.33 us  [local(): outs.append(lax.psum_scatter(share, 'col', scatter_dimension=0))]
    pallas_call x2 -> x7, Pallas kernels: 60.6 us -> 79.4 us  [the longest x3 79.4 us: hidden_call(): pl.pallas_call(functools.partial(hidden_kernel, ff), grid_spec=pltpu.Pref...]
    ppermute x6 -> x18, starting transfers between devices: 13.4 us -> 31.6 us  [send(): return lax.ppermute(value, 'col', lane_pairs(pairs))]
    unnamed x0 -> x7, other arithmetic: none -> 11.4 us
    pallas_call x2 -> x3, Pallas kernels: 27.9 us -> 35.1 us  [share_call(): pl.pallas_call(share_kernel, grid=(devices // 2,), in_specs=[pl.BlockSpec...]
    another operation x0 -> x4, other arithmetic: none -> 6.2 us  [the longest x3 4.64 us: result(): got = swap_cores(jnp.stack([mine[j] for j in group]), chips)]
  transfers between devices with their start and end apart: 19 -> 36, of which waited for: 12 -> 19; matrix products, arithmetic and copies ran while one was open for 9% -> 15% of each run, Pallas kernels for 25% -> 29%
where the time goes in v4:
time: 401 us; the launch traced here: 393 us
  waiting for transfers between devices  146 us (36%)
  Pallas kernels  114 us (28%)
  other arithmetic  60.6 us (15%)
  starting transfers between devices  42.7 us (11%)
  between operations  14.7 us (4%)
  local copies, waits for them, and re-layouts  14.1 us (4%)
    ppermute x18, waiting for transfers between devices, send(): return lax.ppermute(value, 'col', lane_pairs(pairs))  99.1 us
    pallas_call x3, Pallas kernels, hidden_call(): pl.pallas_call(functools.partial(hidden_kernel, ff), grid_spec=pltpu.Pref...  79.4 us
    pallas_call x3, Pallas kernels, share_call(): pl.pallas_call(share_kernel, grid=(devices // 2,), in_specs=[pl.BlockSpec...  35.1 us
    all_gather x2, waiting for transfers between devices, local(): lax.all_gather(both, 'col', axis=0)  32.2 us
    ppermute x18, starting transfers between devices, send(): return lax.ppermute(value, 'col', lane_pairs(pairs))  31.6 us
    concatenate x1, other arithmetic, local(): inner_cat = jnp.concatenate([inner_weight.T, blank, inner_down.T], axis=0)  25.8 us
    unnamed x7, other arithmetic  11.4 us
    unnamed x64, local copies, waits for them, and re-layouts  9.13 us
  transfers between devices with their start and end apart: 36, of which 19 were waited for; matrix products, arithmetic and copies ran while one was open for 15% of the time, Pallas kernels for 29%

profile of v4, /device:TPU:8, one launch (start us, length us, event | category | flops | bytes accessed | tf_op | source)
XLA Modules:
  0.0 393.3 jit_solution(4050877680010947597)
XLA Ops:
  12.4 2.0 slice_bitcast_fusion.3
  16.6 25.8 %pad_maximum_fusion = (bf16[1792,5120]{1,0:T(8,128)(2,1)}, bf16[1792,5120]{1,0:T(8,128)(2,1)}) fusion(bf16[64,5120]{1,0:T(8,128)(2,1)S(1)} %bitcast.71, bf16[1728,5120]{1,0:T(8,128)(2,1)} %bitcast.64, bf16[64,5120]{1,0:T(8,128)(2,1)S(1)} %copy-done.23, bf16[1728,5120]{1,0:T(8,128)(2,1)} %bitcast.65), kind=kLoop, calls=%fused_computation | loop fusion | flops 73400320 | bytes 73400320 | tf_op jit(solution)/shard_map/concatenate | solution.py:309
  42.4 32.1 %all-gather.5.cloned.1.call-done = bf16[16,304,640]{2,1,0:T(8,128)(2,1)} async-done(((bf16[2,304,640]{2,1,0:T(8,128)(2,1)}), bf16[16,304,640]{2,1,0:T(8,128)(2,1)}) %all-gather.5.cloned.1.call-update) | async-done | bytes 6225936 | tf_op jit(solution)/shard_map/all_gather | solution.py:304
  74.5 22.7 %shard_map.137 = (bf16[304,1792]{1,0:T(8,128)(2,1)}, bf16[304,128]{1,0:T(8,128)(2,1)S(1)}, f32[128,1792]{1,0:T(8,128)}) custom-call(s32[1]{0:T(128)} %constant.7.clone.1.place_ref, bf16[8,2,304,640]{3,2,1,0:T(8,128)(2,1)} %bitcast.77, bf16[1792,5120]{1,0:T(8,128)(2,1)} %get-tuple-element.51.inner_ref.weight_ref, ...), custom_call_target="tpu_custom_call" | custom-call | flops 20000000000 | bytes 36000000 | tf_op jit(solution)/shard_map/pallas_call | solution.py:98
  99.0 11.5 %shard_map.139.refs_1_ = bf16[8,304,640]{2,1,0:T(8,128)(2,1)} custom-call(bf16[304,1792]{1,0:T(8,128)(2,1)} %get-tuple-element.14.grad_ref, bf16[1792,5120]{1,0:T(8,128)(2,1)} %get-tuple-element.51.inner_ref.weight_ref, bf16[2,416,640]{2,1,0:T(8,128)(2,1)S(1)} %copy-done, bf16[2,416,640]{2,1,0:T(8,128)(2,1)S(1)} %copy-done), custom_call_target="tpu_custom_call" | custom-call | flops 20000000000 | bytes 36000000 | tf_op jit(solution)/shard_map/pallas_call | solution.py:149
  115.6 4.8 %collective-permute-done.3 = bf16[152,128]{1,0:T(8,128)(2,1)S(1)} collective-permute-done((bf16[152,128]{1,0:T(8,128)(2,1)S(1)}, bf16[152,128]{1,0:T(8,128)(2,1)S(1)}, u32[]{:S(2)}, u32[]{:S(2)}) %collective-permute-start.3) | collective-permute-done | bytes 38944 | tf_op jit(solution)/shard_map/ppermute | solution.py:180
  121.8 1.9 collective-permute-start.1
  123.7 4.2 %collective-permute-start = (bf16[2,416,640]{2,1,0:T(8,128)(2,1)S(1)}, bf16[2,416,640]{2,1,0:T(8,128)(2,1)}, u32[]{:S(2)}, u32[]{:S(2)}) collective-permute-start(bf16[2,416,640]{2,1,0:T(8,128)(2,1)S(1)} %copy-done.1), channel_id=1, source_target_pairs={{0,2},{1,3},{2,4},{3,5},{4,6},{5,7},{8,10},{9,11},{10,12},{11,13},... | collective-permute-start | bytes 3194888 | tf_op jit(solution)/shard_map/ppermute | solution.py:180
  129.9 32.3 %collective-permute-done.7 = bf16[152,128]{1,0:T(8,128)(2,1)S(1)} collective-permute-done((bf16[152,128]{1,0:T(8,128)(2,1)S(1)}, bf16[152,128]{1,0:T(8,128)(2,1)S(1)}, u32[]{:S(2)}, u32[]{:S(2)}) %collective-permute-start.7) | collective-permute-done | bytes 38944 | tf_op jit(solution)/shard_map/ppermute | solution.py:180
  163.6 1.6 collective-permute-done.8
  166.6 4.2 %collective-permute-start.11 = (bf16[2,416,640]{2,1,0:T(8,128)(2,1)}, bf16[2,416,640]{2,1,0:T(8,128)(2,1)}, u32[]{:S(2)}, u32[]{:S(2)}) collective-permute-start(bf16[2,416,640]{2,1,0:T(8,128)(2,1)} %collective-permute-done.1.refs_1_), channel_id=1, source_target_pairs={{2,0},{3,1},{4,2},{5,3},{10,8},{11,9},{12,10},{13,11},{18,16},{19,... | collective-permute-start | bytes 3194888 | tf_op jit(solution)/shard_map/ppermute | solution.py:180
  170.8 2.7 collective-permute-start.10
  173.5 21.7 %shard_map.141 = (bf16[304,1792]{1,0:T(8,128)(2,1)}, bf16[304,128]{1,0:T(8,128)(2,1)S(1)}, f32[128,1792]{1,0:T(8,128)}) custom-call(s32[1]{0:T(128)} %constant.7.clone.1.place_ref, bf16[8,2,304,640]{3,2,1,0:T(8,128)(2,1)} %bitcast.76, bf16[1792,5120]{1,0:T(8,128)(2,1)} %get-tuple-element.51.inner_ref.weight_ref, ...), custom_call_target="tpu_custom_call" | custom-call | flops 20000000000 | bytes 36000000 | tf_op jit(solution)/shard_map/pallas_call | solution.py:98
  195.3 23.7 %collective-permute-done.11.refs_0_ = bf16[2,416,640]{2,1,0:T(8,128)(2,1)} collective-permute-done((bf16[2,416,640]{2,1,0:T(8,128)(2,1)}, bf16[2,416,640]{2,1,0:T(8,128)(2,1)}, u32[]{:S(2)}, u32[]{:S(2)}) %collective-permute-start.11) | collective-permute-done | bytes 1064992 | tf_op jit(solution)/shard_map/ppermute | solution.py:180
  219.0 1.9 add.131
  221.0 1.8 collective-permute-start.13
  222.8 3.7 collective-permute-start.14
  226.4 1.6 pad_maximum_fusion.2
  228.1 1.8 add.132
  229.9 19.7 %collective-permute-done.14 = bf16[2,416,640]{2,1,0:T(8,128)(2,1)S(1)} collective-permute-done((bf16[2,416,640]{2,1,0:T(8,128)(2,1)}, bf16[2,416,640]{2,1,0:T(8,128)(2,1)S(1)}, u32[]{:S(2)}, u32[]{:S(2)}) %collective-permute-start.14) | collective-permute-done | bytes 1064992 | tf_op jit(solution)/shard_map/ppermute | solution.py:180
  249.6 1.5 add.133
  251.1 1.6 pad_maximum_fusion.3
  252.6 11.2 %shard_map.144 = bf16[8,304,640]{2,1,0:T(8,128)(2,1)} custom-call(bf16[304,1792]{1,0:T(8,128)(2,1)} %get-tuple-element.16.grad_ref, bf16[1792,5120]{1,0:T(8,128)(2,1)} %get-tuple-element.51.inner_ref.weight_ref, bf16[2,416,640]{2,1,0:T(8,128)(2,1)S(1)} %copy-done.3, bf16[2,416,640]{2,1,0:T(8,128)(2,1)} %shard_map.143.refs_1_), custom_call_target="tpu_custom_call" | custom-call | flops 20000000000 | bytes 36000000 | tf_op jit(solution)/shard_map/pallas_call | solution.py:149
  263.9 1.9 fusion.24
  265.9 1.9 select_dynamic-update-slice_fusion.1
  267.8 1.7 select_dynamic-update-slice_fusion
  269.5 1.6 bitcast_dynamic-update-slice_fusion.5
  271.1 1.6 bitcast_dynamic-update-slice_fusion.4
  272.7 1.6 bitcast_dynamic-update-slice_fusion.3
  274.3 1.6 bitcast_dynamic-update-slice_fusion.2
  275.8 1.6 bitcast_dynamic-update-slice_fusion.1
  277.4 1.6 bitcast_dynamic-update-slice_fusion.both_ref
  279.0 3.2 copy-done.28
  282.2 35.0 %shard_map.145 = (bf16[416,1792]{1,0:T(8,128)(2,1)}, bf16[416,128]{1,0:T(8,128)(2,1)S(1)}, f32[128,1792]{1,0:T(8,128)}) custom-call(s32[1]{0:T(128)} %bitcast.14.place_ref, bf16[8,2,416,640]{3,2,1,0:T(8,128)(2,1)} %copy-done.28, bf16[1792,5120]{1,0:T(8,128)(2,1)} %get-tuple-element.51.inner_ref.weight_ref, bf16[1792,5120]{1,0:T(8,128)(2,1)} %get-tuple-element.52.outer_ref, ...), custom_call_target="tpu_custom_call" | custom-call | flops 20000000000 | bytes 36000000 | tf_op jit(solution)/shard_map/pallas_call | solution.py:98
  318.6 12.4 %shard_map.146 = bf16[8,416,640]{2,1,0:T(8,128)(2,1)} custom-call(bf16[416,1792]{1,0:T(8,128)(2,1)S(1)} %copy-done.7, bf16[1792,5120]{1,0:T(8,128)(2,1)} %get-tuple-element.51.inner_ref.weight_ref), custom_call_target="tpu_custom_call" | custom-call | flops 20000000000 | bytes 36000000 | tf_op jit(solution)/shard_map/pallas_call | solution.py:149
  336.6 3.7 collective-permute-done.17
  341.9 4.9 %collective-permute-done.18 = bf16[360,128]{1,0:T(8,128)(2,1)S(1)} collective-permute-done((bf16[360,128]{1,0:T(8,128)(2,1)S(1)}, bf16[360,128]{1,0:T(8,128)(2,1)S(1)}, u32[]{:S(2)}, u32[]{:S(2)}) %collective-permute-start.18) | collective-permute-done | bytes 92192 | tf_op jit(solution)/shard_map/ppermute | solution.py:180
  348.1 1.7 collective-permute-start.29
  352.0 5.5 %collective-permute-done.21 = bf16[360,128]{1,0:T(8,128)(2,1)S(1)} collective-permute-done((bf16[360,128]{1,0:T(8,128)(2,1)S(1)}, bf16[360,128]{1,0:T(8,128)(2,1)S(1)}, u32[]{:S(2)}, u32[]{:S(2)}) %collective-permute-start.21) | collective-permute-done | bytes 92192 | tf_op jit(solution)/shard_map/ppermute | solution.py:180
  359.1 1.7 collective-permute-start.30
  362.3 2.8 collective-permute-done.22
  367.9 1.7 collective-permute-start.25
  369.6 1.5 collective-permute-start.24
  372.3 2.0 collective-permute-done.25
  374.3 2.5 collective-permute-done.24
  376.7 2.2 collective-permute-done.26
  379.8 4.3 %reduce-scatter.8.cloned.1.call-done = bf16[1,416,640]{2,1,0:T(8,128)(2,1)} async-done(((bf16[8,416,640]{2,1,0:T(8,128)(2,1)}), bf16[1,416,640]{2,1,0:T(8,128)(2,1)}) %reduce-scatter.8.cloned.1.call-update) | async-done | bytes 532496 | tf_op jit(solution)/shard_map/reduce_scatter | solution.py:337
  384.1 2.4 pad_maximum_fusion.4
  (158 shorter events, 40.1 us)
Async XLA Ops:
  7.2 67.3 %all-gather.5.cloned.1.call-start = ((), (), s32[]{:S(2)}) async-start(), calls=%async_computation.6 | async-start | bytes 7004160 | tf_op jit(solution)/shard_map/all_gather | solution.py:304
  9.3 5.1 %copy-start.29 = (f32[640]{0:T(1024)}, f32[640]{0:T(1024)S(1)}, u32[]{:S(2)}) copy-start(f32[640]{0:T(1024)S(1)} %dynamic_slice.3) | copy-start | bytes 7684
  11.2 162.4 %all-gather.7.cloned.1.call-start = ((), (), s32[]{:S(2)}) async-start(), calls=%async_computation.7 | async-start | bytes 7004160 | tf_op jit(solution)/shard_map/all_gather | solution.py:304
  12.2 367.6 %reduce-scatter.4.cloned.1.call-start = ((), (), s32[]{:S(2)}) async-start(), calls=%async_computation.3 | async-start | bytes 3502080 | tf_op jit(solution)/shard_map/reduce_scatter | solution.py:337
  111.3 1.3 collective-permute-start.2
  113.4 8.3 %copy-start.1 = (bf16[2,416,640]{2,1,0:T(8,128)(2,1)S(1)}, bf16[2,416,640]{2,1,0:T(8,128)(2,1)}, u32[]{:S(2)}) copy-start(bf16[2,416,640]{2,1,0:T(8,128)(2,1)} %shard_map.138.refs_0_.refs_1_) | copy-start | bytes 3194884
  113.5 7.0 %collective-permute-start.3 = (bf16[152,128]{1,0:T(8,128)(2,1)S(1)}, bf16[152,128]{1,0:T(8,128)(2,1)S(1)}, u32[]{:S(2)}, u32[]{:S(2)}) collective-permute-start(bf16[152,128]{1,0:T(8,128)(2,1)S(1)} %get-tuple-element.25), channel_id=1, source_target_pairs={{0,2},{1,3},{8,10},{9,11},{16,18},{17,19},{24,26},{25,27}} | collective-permute-start | bytes 116744 | tf_op jit(solution)/shard_map/ppermute | solution.py:180
  114.9 264.9 %reduce-scatter.6.cloned.1.call-start = ((), (), s32[]{:S(2)}) async-start(), calls=%async_computation.4 | async-start | bytes 3502080 | tf_op jit(solution)/shard_map/reduce_scatter | solution.py:337
  115.0 12.9 %collective-permute-start.6 = (bf16[152,128]{1,0:T(8,128)(2,1)S(1)}, bf16[152,128]{1,0:T(8,128)(2,1)S(1)}, u32[]{:S(2)}, u32[]{:S(2)}) collective-permute-start(bf16[152,128]{1,0:T(8,128)(2,1)S(1)} %get-tuple-element.25), channel_id=1, source_target_pairs={{6,4},{7,5},{14,12},{15,13},{22,20},{23,21},{30,28},{31,29}} | collective-permute-start | bytes 116744 | tf_op jit(solution)/shard_map/ppermute | solution.py:180
  120.5 7.4 %collective-permute-start.4 = (bf16[152,128]{1,0:T(8,128)(2,1)S(1)}, bf16[152,128]{1,0:T(8,128)(2,1)S(1)}, u32[]{:S(2)}, u32[]{:S(2)}) collective-permute-start(bf16[152,128]{1,0:T(8,128)(2,1)S(1)} %fusion.15), channel_id=1, source_target_pairs={{2,4},{3,5},{10,12},{11,13},{18,20},{19,21},{26,28},{27,29}} | collective-permute-start | bytes 116744 | tf_op jit(solution)/shard_map/ppermute | solution.py:180
  121.8 44.8 %collective-permute-start.1 = (bf16[2,416,640]{2,1,0:T(8,128)(2,1)S(1)}, bf16[2,416,640]{2,1,0:T(8,128)(2,1)}, u32[]{:S(2)}, u32[]{:S(2)}) collective-permute-start(bf16[2,416,640]{2,1,0:T(8,128)(2,1)S(1)} %copy-done.1), channel_id=1, source_target_pairs={{2,0},{3,1},{4,2},{5,3},{6,4},{7,5},{10,8},{11,9},{12,10},{13,11},... | collective-permute-start | bytes 3194888 | tf_op jit(solution)/shard_map/ppermute | solution.py:180
  123.7 47.1 %collective-permute-start = (bf16[2,416,640]{2,1,0:T(8,128)(2,1)S(1)}, bf16[2,416,640]{2,1,0:T(8,128)(2,1)}, u32[]{:S(2)}, u32[]{:S(2)}) collective-permute-start(bf16[2,416,640]{2,1,0:T(8,128)(2,1)S(1)} %copy-done.1), channel_id=1, source_target_pairs={{0,2},{1,3},{2,4},{3,5},{4,6},{5,7},{8,10},{9,11},{10,12},{11,13},... | collective-permute-start | bytes 3194888 | tf_op jit(solution)/shard_map/ppermute | solution.py:180
  128.0 34.3 %collective-permute-start.7 = (bf16[152,128]{1,0:T(8,128)(2,1)S(1)}, bf16[152,128]{1,0:T(8,128)(2,1)S(1)}, u32[]{:S(2)}, u32[]{:S(2)}) collective-permute-start(bf16[152,128]{1,0:T(8,128)(2,1)S(1)} %get-tuple-element.50), channel_id=1, source_target_pairs={{4,2},{5,3},{12,10},{13,11},{20,18},{21,19},{28,26},{29,27}} | collective-permute-start | bytes 116744 | tf_op jit(solution)/shard_map/ppermute | solution.py:180
  129.3 34.3 %collective-permute-start.5 = (bf16[152,128]{1,0:T(8,128)(2,1)S(1)}, bf16[152,128]{1,0:T(8,128)(2,1)S(1)}, u32[]{:S(2)}, u32[]{:S(2)}) collective-permute-start(bf16[152,128]{1,0:T(8,128)(2,1)S(1)} %get-tuple-element.49), channel_id=1, source_target_pairs={{4,6},{5,7},{12,14},{13,15},{20,22},{21,23},{28,30},{29,31}} | collective-permute-start | bytes 116744 | tf_op jit(solution)/shard_map/ppermute | solution.py:180
  162.3 2.9 collective-permute-start.8
  165.3 1.3 collective-permute-start.9
  166.6 28.7 %copy-start.24 = (bf16[152,128]{1,0:T(8,128)(2,1)}, bf16[152,128]{1,0:T(8,128)(2,1)S(1)}, u32[]{:S(2)}) copy-start(bf16[152,128]{1,0:T(8,128)(2,1)S(1)} %get-tuple-element.48) | copy-start | bytes 116740
  166.6 52.4 %collective-permute-start.11 = (bf16[2,416,640]{2,1,0:T(8,128)(2,1)}, bf16[2,416,640]{2,1,0:T(8,128)(2,1)}, u32[]{:S(2)}, u32[]{:S(2)}) collective-permute-start(bf16[2,416,640]{2,1,0:T(8,128)(2,1)} %collective-permute-done.1.refs_1_), channel_id=1, source_target_pairs={{2,0},{3,1},{4,2},{5,3},{10,8},{11,9},{12,10},{13,11},{18,16},{19,... | collective-permute-start | bytes 3194888 | tf_op jit(solution)/shard_map/ppermute | solution.py:180
  170.8 48.2 %collective-permute-start.10 = (bf16[2,416,640]{2,1,0:T(8,128)(2,1)}, bf16[2,416,640]{2,1,0:T(8,128)(2,1)S(1)}, u32[]{:S(2)}, u32[]{:S(2)}) collective-permute-start(bf16[2,416,640]{2,1,0:T(8,128)(2,1)} %collective-permute-done.refs_0_), channel_id=1, source_target_pairs={{2,4},{3,5},{4,6},{5,7},{10,12},{11,13},{12,14},{13,15},{18,20},{1... | collective-permute-start | bytes 3194888 | tf_op jit(solution)/shard_map/ppermute | solution.py:180
  195.3 25.6 %copy-start.4 = (bf16[304,128]{1,0:T(8,128)(2,1)}, bf16[304,128]{1,0:T(8,128)(2,1)S(1)}, u32[]{:S(2)}) copy-start(bf16[304,128]{1,0:T(8,128)(2,1)S(1)} %get-tuple-element.17.refs_1_) | copy-start | bytes 233476
  221.0 5.5 %copy-start.14 = (bf16[1,2,416,640]{3,2,1,0:T(8,128)(2,1)S(1)}, bf16[1,2,416,640]{3,2,1,0:T(8,128)(2,1)}, u32[]{:S(2)}) copy-start(bf16[1,2,416,640]{3,2,1,0:T(8,128)(2,1)} %get-tuple-element.33) | copy-start | bytes 3194884
  221.0 7.1 %collective-permute-start.13 = (bf16[2,416,640]{2,1,0:T(8,128)(2,1)}, bf16[2,416,640]{2,1,0:T(8,128)(2,1)}, u32[]{:S(2)}, u32[]{:S(2)}) collective-permute-start(bf16[2,416,640]{2,1,0:T(8,128)(2,1)} %shard_map.142.refs_0_), channel_id=1, source_target_pairs={{4,6},{5,7},{12,14},{13,15},{20,22},{21,23},{28,30},{29,31}} | collective-permute-start | bytes 3194888 | tf_op jit(solution)/shard_map/ppermute | solution.py:180
  222.8 26.8 %collective-permute-start.14 = (bf16[2,416,640]{2,1,0:T(8,128)(2,1)}, bf16[2,416,640]{2,1,0:T(8,128)(2,1)S(1)}, u32[]{:S(2)}, u32[]{:S(2)}) collective-permute-start(bf16[2,416,640]{2,1,0:T(8,128)(2,1)} %shard_map.143.refs_1_), channel_id=1, source_target_pairs={{2,0},{3,1},{10,8},{11,9},{18,16},{19,17},{26,24},{27,25}} | collective-permute-start | bytes 3194888 | tf_op jit(solution)/shard_map/ppermute | solution.py:180
  228.0 37.8 %collective-permute-start.12 = (bf16[2,2,416,640]{3,2,1,0:T(8,128)(2,1)}, bf16[2,2,416,640]{3,2,1,0:T(8,128)(2,1)}, u32[]{:S(2)}, u32[]{:S(2)}) collective-permute-start(bf16[2,2,416,640]{3,2,1,0:T(8,128)(2,1)} %pad_maximum_fusion.2), channel_id=1, source_target_pairs={{0,1},{1,0},{2,3},{3,2},{4,5},{5,4},{6,7},{7,6},{8,9},{9,8},{10,11... | collective-permute-start | bytes 6389768 | tf_op jit(solution)/shard_map/ppermute | solution.py:184
  229.9 21.2 %copy-start.8 = (bf16[2,416,640]{2,1,0:T(8,128)(2,1)}, bf16[2,416,640]{2,1,0:T(8,128)(2,1)S(1)}, u32[]{:S(2)}) copy-start(bf16[2,416,640]{2,1,0:T(8,128)(2,1)S(1)} %add.132) | copy-start | bytes 3194884
  252.6 16.8 %collective-permute-start.15 = (bf16[2,2,416,640]{3,2,1,0:T(8,128)(2,1)}, bf16[2,2,416,640]{3,2,1,0:T(8,128)(2,1)}, u32[]{:S(2)}, u32[]{:S(2)}) collective-permute-start(bf16[2,2,416,640]{3,2,1,0:T(8,128)(2,1)} %pad_maximum_fusion.3), channel_id=1, source_target_pairs={{0,1},{1,0},{2,3},{3,2},{4,5},{5,4},{6,7},{7,6},{8,9},{9,8},{10,11... | collective-permute-start | bytes 6389768 | tf_op jit(solution)/shard_map/ppermute | solution.py:184
  263.9 120.2 %reduce-scatter.8.cloned.1.call-start = ((), (), s32[]{:S(2)}) async-start(), calls=%async_computation.5 | async-start | bytes 4792320 | tf_op jit(solution)/shard_map/reduce_scatter | solution.py:337
  331.0 3.8 copy-start.30
  331.0 10.6 %copy-start.21 = (f32[128,1792]{1,0:T(8,128)S(1)}, f32[128,1792]{1,0:T(8,128)}, u32[]{:S(2)}) copy-start(f32[128,1792]{1,0:T(8,128)} %get-tuple-element.22) | copy-start | bytes 2752516
  331.0 10.6 %copy-start.19 = (f32[128,1792]{1,0:T(8,128)S(1)}, f32[128,1792]{1,0:T(8,128)}, u32[]{:S(2)}) copy-start(f32[128,1792]{1,0:T(8,128)} %get-tuple-element.20) | copy-start | bytes 2752516
  331.0 10.6 %copy-start.20 = (f32[128,1792]{1,0:T(8,128)S(1)}, f32[128,1792]{1,0:T(8,128)}, u32[]{:S(2)}) copy-start(f32[128,1792]{1,0:T(8,128)} %get-tuple-element.21) | copy-start | bytes 2752516
  331.9 1.5 collective-permute-start.16
  333.4 6.8 %collective-permute-start.17 = (bf16[360,128]{1,0:T(8,128)(2,1)S(1)}, bf16[360,128]{1,0:T(8,128)(2,1)S(1)}, u32[]{:S(2)}, u32[]{:S(2)}) collective-permute-start(bf16[360,128]{1,0:T(8,128)(2,1)S(1)} %get-tuple-element.23), channel_id=1, source_target_pairs={{0,2},{1,3},{8,10},{9,11},{16,18},{17,19},{24,26},{25,27}} | collective-permute-start | bytes 276488 | tf_op jit(solution)/shard_map/ppermute | solution.py:180
  335.9 5.9 %collective-permute-start.20 = (bf16[360,128]{1,0:T(8,128)(2,1)S(1)}, bf16[360,128]{1,0:T(8,128)(2,1)S(1)}, u32[]{:S(2)}, u32[]{:S(2)}) collective-permute-start(bf16[360,128]{1,0:T(8,128)(2,1)S(1)} %get-tuple-element.23), channel_id=1, source_target_pairs={{6,4},{7,5},{14,12},{15,13},{22,20},{23,21},{30,28},{31,29}} | collective-permute-start | bytes 276488 | tf_op jit(solution)/shard_map/ppermute | solution.py:180
  340.3 6.4 %collective-permute-start.18 = (bf16[360,128]{1,0:T(8,128)(2,1)S(1)}, bf16[360,128]{1,0:T(8,128)(2,1)S(1)}, u32[]{:S(2)}, u32[]{:S(2)}) collective-permute-start(bf16[360,128]{1,0:T(8,128)(2,1)S(1)} %fusion.12), channel_id=1, source_target_pairs={{2,4},{3,5},{10,12},{11,13},{18,20},{19,21},{26,28},{27,29}} | collective-permute-start | bytes 276488 | tf_op jit(solution)/shard_map/ppermute | solution.py:180
  346.8 10.7 %collective-permute-start.21 = (bf16[360,128]{1,0:T(8,128)(2,1)S(1)}, bf16[360,128]{1,0:T(8,128)(2,1)S(1)}, u32[]{:S(2)}, u32[]{:S(2)}) collective-permute-start(bf16[360,128]{1,0:T(8,128)(2,1)S(1)} %get-tuple-element.46), channel_id=1, source_target_pairs={{4,2},{5,3},{12,10},{13,11},{20,18},{21,19},{28,26},{29,27}} | collective-permute-start | bytes 276488 | tf_op jit(solution)/shard_map/ppermute | solution.py:180
  348.1 10.8 %collective-permute-start.29 = (bf16[64,1728]{1,0:T(8,128)(2,1)S(1)}, bf16[64,1728]{1,0:T(8,128)(2,1)S(1)}, u32[]{:S(2)}, u32[]{:S(2)}) collective-permute-start(bf16[64,1728]{1,0:T(8,128)(2,1)S(1)} %get-tuple-element.37), channel_id=1, source_target_pairs={{0,16},{8,24},{16,0},{24,8},{1,17},{9,25},{17,1},{25,9},{2,18},{10... | collective-permute-start | bytes 663560 | tf_op jit(solution)/shard_map/ppermute | solution.py:263
  349.9 9.0 %collective-permute-start.27 = (bf16[64,1728]{1,0:T(8,128)(2,1)S(1)}, bf16[64,1728]{1,0:T(8,128)(2,1)S(1)}, u32[]{:S(2)}, u32[]{:S(2)}) collective-permute-start(bf16[64,1728]{1,0:T(8,128)(2,1)S(1)} %get-tuple-element.38), channel_id=1, source_target_pairs={{0,8},{8,0},{16,24},{24,16},{1,9},{9,1},{17,25},{25,17},{2,10},{10... | collective-permute-start | bytes 663560 | tf_op jit(solution)/shard_map/ppermute | solution.py:263
  351.3 10.9 %collective-permute-start.19 = (bf16[360,128]{1,0:T(8,128)(2,1)S(1)}, bf16[360,128]{1,0:T(8,128)(2,1)S(1)}, u32[]{:S(2)}, u32[]{:S(2)}) collective-permute-start(bf16[360,128]{1,0:T(8,128)(2,1)S(1)} %get-tuple-element.45), channel_id=1, source_target_pairs={{4,6},{5,7},{12,14},{13,15},{20,22},{21,23},{28,30},{29,31}} | collective-permute-start | bytes 276488 | tf_op jit(solution)/shard_map/ppermute | solution.py:180
  357.6 9.0 %copy-start.25 = (bf16[152,128]{1,0:T(8,128)(2,1)S(1)}, bf16[152,128]{1,0:T(8,128)(2,1)}, u32[]{:S(2)}) copy-start(bf16[152,128]{1,0:T(8,128)(2,1)} %copy-done.24) | copy-start | bytes 116740
  357.6 7.5 %collective-permute-start.22 = (bf16[360,128]{1,0:T(8,128)(2,1)S(1)}, bf16[360,128]{1,0:T(8,128)(2,1)S(1)}, u32[]{:S(2)}, u32[]{:S(2)}) collective-permute-start(bf16[360,128]{1,0:T(8,128)(2,1)S(1)} %add_convert_fusion.3), channel_id=1, source_target_pairs={{2,0},{3,1},{10,8},{11,9},{18,16},{19,17},{26,24},{27,25}} | collective-permute-start | bytes 276488 | tf_op jit(solution)/shard_map/ppermute | solution.py:180
  359.0 7.6 %copy-start.10 = (bf16[1024,640]{1,0:T(8,128)(2,1)S(1)}, bf16[1024,640]{1,0:T(8,128)(2,1)}, u32[]{:S(2)}) copy-start(bf16[1024,640]{1,0:T(8,128)(2,1)} %param.10) | copy-start | bytes 3932164
  359.1 6.5 %collective-permute-start.30 = (bf16[64,1728]{1,0:T(8,128)(2,1)S(1)}, bf16[64,1728]{1,0:T(8,128)(2,1)S(1)}, u32[]{:S(2)}, u32[]{:S(2)}) collective-permute-start(bf16[64,1728]{1,0:T(8,128)(2,1)S(1)} %get-tuple-element.35), channel_id=1, source_target_pairs={{0,8},{8,0},{16,24},{24,16},{1,9},{9,1},{17,25},{25,17},{2,10},{10... | collective-permute-start | bytes 663560 | tf_op jit(solution)/shard_map/ppermute | solution.py:263
  360.8 10.7 %collective-permute-start.28 = (bf16[64,1728]{1,0:T(8,128)(2,1)S(1)}, bf16[64,1728]{1,0:T(8,128)(2,1)S(1)}, u32[]{:S(2)}, u32[]{:S(2)}) collective-permute-start(bf16[64,1728]{1,0:T(8,128)(2,1)S(1)} %get-tuple-element.36), channel_id=1, source_target_pairs={{0,16},{8,24},{16,0},{24,8},{1,17},{9,25},{17,1},{25,9},{2,18},{10... | collective-permute-start | bytes 663560 | tf_op jit(solution)/shard_map/ppermute | solution.py:263
  365.2 1.4 collective-permute-start.23
  367.9 6.4 %collective-permute-start.25 = (bf16[128,640]{1,0:T(8,128)(2,1)S(1)}, bf16[128,640]{1,0:T(8,128)(2,1)S(1)}, u32[]{:S(2)}, u32[]{:S(2)}) collective-permute-start(bf16[128,640]{1,0:T(8,128)(2,1)S(1)} %fusion.8), channel_id=1, source_target_pairs={{0,16},{8,24},{16,0},{24,8},{1,17},{9,25},{17,1},{25,9},{2,18},{10... | collective-permute-start | bytes 491528 | tf_op jit(solution)/shard_map/ppermute | solution.py:274
  369.6 7.1 %collective-permute-start.24 = (bf16[128,640]{1,0:T(8,128)(2,1)S(1)}, bf16[128,640]{1,0:T(8,128)(2,1)S(1)}, u32[]{:S(2)}, u32[]{:S(2)}) collective-permute-start(bf16[128,640]{1,0:T(8,128)(2,1)S(1)} %fusion.8), channel_id=1, source_target_pairs={{0,8},{8,0},{16,24},{24,16},{1,9},{9,1},{17,25},{25,17},{2,10},{10... | collective-permute-start | bytes 491528 | tf_op jit(solution)/shard_map/ppermute | solution.py:274
  371.1 7.9 %collective-permute-start.26 = (bf16[128,640]{1,0:T(8,128)(2,1)S(1)}, bf16[128,640]{1,0:T(8,128)(2,1)S(1)}, u32[]{:S(2)}, u32[]{:S(2)}) collective-permute-start(bf16[128,640]{1,0:T(8,128)(2,1)S(1)} %fusion.8), channel_id=1, source_target_pairs={{0,24},{8,16},{16,8},{24,0},{1,25},{9,17},{17,9},{25,1},{2,26},{10... | collective-permute-start | bytes 491528 | tf_op jit(solution)/shard_map/ppermute | solution.py:274
  (20 other events, 31.6 us)
Sparse Core Ops, SparseCore 0:
  11.3 63.1 all-gather.4
  76.2 77.9 all-gather.6
  156.5 62.3 reduce-scatter.3
  264.0 38.5 reduce-scatter.5
  331.1 52.9 reduce-scatter.7

commit v5 on v3

--- a/solution.py
+++ b/solution.py
@@ -16,7 +16,7 @@
 COLS = 256
 VMEM_BYTES = 52 * 1024 * 1024
 COST = pl.CostEstimate(flops=20_000_000_000, bytes_accessed=36_000_000, transcendentals=0)
-SPLIT = ((512, 256), (512, 0))
+SPLIT = ((512, 320), (512, 0))
 
 
 def dot_nn(left, right):
@@ -31,49 +31,55 @@
     return lax.dot_general(left, right, (((0,), (0,)), ((), ())), preferred_element_type=F32)
 
 
-def hidden_kernel(ff, both_ref, inner_ref, outer_ref, bias_ref, up_ref, down_lo_ref, down_hi_ref, *refs):
+def hidden_kernel(ff, both_ref, weight_ref, bias_ref, up_ref, down_lo_ref, down_hi_ref, *refs):
     grad_ref, low_ref, grads_ref, pre_acc, hid_acc, hidden_ref = refs[-6:]
-    step = pl.program_id(0)
+    step, last = pl.program_id(0), pl.num_programs(0) - 1
     _, _, tokens, width = both_ref.shape
     padded = pre_acc.shape[1]
-
-    def product(which, weight_ref):
-        first, second = both_ref[0, which], both_ref[1, which]
+    rank = LANES // 2
+    tail = slice(padded - LANES, padded)
+    tiles = [slice(start, start + COLS) for start in range(0, padded, COLS)]
+
+    def product():
+        first, second = both_ref[0, 0], both_ref[1, 0]
         if width % LANES == 0:
             return dot_nt(jnp.concatenate([first, second], axis=1), weight_ref[...])
         return dot_nt(first, weight_ref[:, :width]) + dot_nt(second, weight_ref[:, width:])
 
     @pl.when(step == 0)
     def _():
-        pre_acc[...] = product(0, inner_ref)
-        hid_acc[...] = product(1, outer_ref)
-
-    @pl.when(step > 0)
+        pre_acc[...] = product()
+
+    @pl.when(step == 1)
     def _():
-        pre_acc[...] += product(0, inner_ref)
-        hid_acc[...] += product(1, outer_ref)
-
-    @pl.when(step == pl.num_programs(0) - 1)
+        hid_acc[...] = product()
+
+    @pl.when(jnp.logical_and(step > 1, lax.rem(step, 2) == 0))
     def _():
-        tail = slice(padded - LANES, padded)
+        pre_acc[...] += product()
+
+    @pl.when(jnp.logical_and(jnp.logical_and(step > 1, lax.rem(step, 2) == 1), step < last))
+    def _():
+        hid_acc[...] += product()
+
+    @pl.when(step == last)
+    def _():
         inner_low = pre_acc[:, tail].astype(BF16)
-        grad_low = hid_acc[:, tail].astype(BF16)
-        rank = LANES // 2
-        low = jnp.zeros((tokens, LANES), F32)
-        for start in range(0, padded, COLS):
-            cols = slice(start, start + COLS)
+        value = product()
+        for cols in tiles:
             pre = pre_acc[:, cols] + dot_nn(inner_low, up_ref[:, cols]) + bias_ref[:, cols]
             square = pre * pre
-            tangent = jnp.tanh(SLOPE_SCALE * pre * (1.0 + CUBIC * square))
+            tangent = jnp.tanh(pre * (SLOPE_SCALE + SLOPE_SCALE * CUBIC * square))
             half = 0.5 + 0.5 * tangent
-            hidden = (pre * half).astype(BF16)
-            slope = half + 0.5 * pre * (1.0 - tangent * tangent) * (
-                SLOPE_SCALE + 3.0 * CUBIC * SLOPE_SCALE * square
+            hidden_ref[:, cols] = (pre * half).astype(BF16)
+            pre_acc[:, cols] = half + pre * (1.0 - tangent * tangent) * (
+                0.5 * SLOPE_SCALE + 1.5 * CUBIC * SLOPE_SCALE * square
             )
+        hid_acc[...] += value
+        grad_low = hid_acc[:, tail].astype(BF16)
+        for cols in tiles:
             grad_hidden = hid_acc[:, cols] + dot_nn(grad_low, down_hi_ref[:, cols])
-            grad_pre = (grad_hidden * slope).astype(BF16)
-            hidden_ref[:, cols] = hidden
-            grad_ref[:, cols] = grad_pre
+            grad_ref[:, cols] = (grad_hidden * pre_acc[:, cols]).astype(BF16)
         low = dot_nt(hidden_ref[...], down_lo_ref[...]) + dot_nt(grad_ref[...], up_ref[...])
         low = low.astype(BF16)
         low_ref[...] = low
@@ -89,18 +95,16 @@
                 grad_ref[:, here] = jnp.where(lane + start < ff, grad_ref[:, here], jnp.zeros_like(low))
 
 
-def hidden_call(both, inner_cat, outer_cat, bias, up, down_lo, down_hi, ff, after=()):
+def hidden_call(both, weights, bias, up, down_lo, down_hi, ff, after=()):
     devices, _, tokens, width = both.shape
-    padded = inner_cat.shape[0]
-    steps = devices // 2
-    whole = lambda k: (0, 0)
+    padded = weights.shape[0] // 2
+    whole = lambda s: (0, 0)
     return pl.pallas_call(
         functools.partial(hidden_kernel, ff),
-        grid=(steps,),
+        grid=(devices,),
         in_specs=[
-            pl.BlockSpec((2, 2, tokens, width), lambda k: (k, 0, 0, 0)),
-            pl.BlockSpec((padded, 2 * width), lambda k: (0, k)),
-            pl.BlockSpec((padded, 2 * width), lambda k: (0, k)),
+            pl.BlockSpec((2, 1, tokens, width), lambda s: (s // 2, s % 2, 0, 0)),
+            pl.BlockSpec((padded, 2 * width), lambda s: (s % 2, s // 2)),
             pl.BlockSpec((1, padded), whole),
             pl.BlockSpec((LANES, padded), whole),
             pl.BlockSpec((LANES, padded), whole),
@@ -124,7 +128,7 @@
         ],
         compiler_params=pltpu.CompilerParams(vmem_limit_bytes=VMEM_BYTES),
         cost_estimate=COST,
-    )(both, inner_cat, outer_cat, bias, up, down_lo, down_hi, *after)
+    )(both, weights, bias, up, down_lo, down_hi, *after)
 
 
 def share_kernel(first, place_ref, grad_ref, weight_ref, *refs):
@@ -319,8 +323,9 @@
 
     gap = padded - ff - rank
     blank = jnp.zeros((gap, features), BF16)
-    inner_cat = jnp.concatenate([inner_weight.T, blank, inner_down.T], axis=0)
-    outer_cat = jnp.concatenate([outer_weight.T, blank, outer_up], axis=0)
+    weights = jnp.concatenate(
+        [inner_weight.T, blank, inner_down.T, outer_weight.T, blank, outer_up], axis=0
+    )
     bias = jnp.pad(inner_bias, (0, padded - ff))[None, :]
     up_hi = jnp.pad(inner_up, ((LANES - rank, 0), (0, padded - ff)))
     down_hi = jnp.pad(outer_down.T, ((LANES - rank, 0), (0, padded - ff)))
@@ -336,9 +341,15 @@
             return sent
 
         grad_pre, low, grad = hidden_call(
-            both, inner_cat, outer_cat, bias, up_hi, down_lo, down_hi, ff, advance(0)
+            both, weights, bias, up_hi, down_lo, down_hi, ff, advance(0)
         )
-        share, *shares = share_call(place, grad_pre, inner_cat, chips, first)
+        if index:
+            lows[-1] = lows[-1].result()
+            after = [lows[-1]]
+            if moving[-1]:
+                moving[-1] = moving[-1].result()
+                after.append(moving[-1])
+        share, *shares = share_call(place, grad_pre, weights, chips, first, after if index else ())
         far.append(lax.psum_scatter(share, "col", scatter_dimension=0))
         moving.append(Shares(*shares, chips) if first else None)
         lows.append(LowSum(low, core, chips))
@@ -347,10 +358,12 @@
     while lows[-1].left():
         ready = moving[-1].hop() if moving[-1] else []
         lows[-1].hop(ready)
-    lows = [summing.result() for summing in lows]
+    lows[-1] = lows[-1].result()
+    if moving[-1]:
+        moving[-1] = moving[-1].result()
     outs = []
-    for shares, rest in zip(moving, far):
-        outs += [shares.result(), rest] if shares else [rest]
+    for near, rest in zip(moving, far):
+        outs += [rest] if near is None else [near, rest]
     tokens_grad = jnp.concatenate(outs, axis=0)
 
     hidden_sums = sum_rows(hidden_part)

time: 343 us -> 341 us (level)
    reduce_scatter x2, waiting for transfers between devices: 0.01 us -> 9.95 us  [local(): far.append(lax.psum_scatter(share, 'col', scatter_dimension=0))]
    all_gather x2, waiting for transfers between devices: 78.8 us -> 69.6 us  [local(): gathered.append(lax.all_gather(both, 'col', axis=0))]
    ppermute x18, starting transfers between devices: 29 us -> 25.2 us  [send(): return lax.ppermute(value, 'col', lane_pairs(pairs))]
    concatenate x1 -> x2, other arithmetic: 25.9 us -> 25.6 us  [the longest x1 25.6 us: local(): jnp.concatenate([inner_weight.T, blank, inner_down.T, outer_weight.T, bla...]
  transfers between devices with their start and end apart: 34 -> 34, of which waited for: 16 -> 17; matrix products, arithmetic and copies ran while one was open for 11% -> 11% of each run, Pallas kernels for 27% -> 27%
where the time goes in v5:
time: 341 us; the launch traced here: 337 us
  waiting for transfers between devices  148 us (43%)
  Pallas kernels  90.4 us (27%)
  other arithmetic  39.8 us (12%)
  starting transfers between devices  36.6 us (11%)
  between operations  14.4 us (4%)
  local copies, waits for them, and re-layouts  6.87 us (2%)
    all_gather x2, waiting for transfers between devices, local(): gathered.append(lax.all_gather(both, 'col', axis=0))  69.6 us
    pallas_call x2, Pallas kernels, hidden_call(): pl.pallas_call(functools.partial(hidden_kernel, ff), grid=(devices,), in_...  60 us
    ppermute x18, waiting for transfers between devices, send(): return lax.ppermute(value, 'col', lane_pairs(pairs))  58.2 us
    pallas_call x2, Pallas kernels, share_call(): pl.pallas_call(functools.partial(share_kernel, first), grid_spec=pltpu.Pr...  30.4 us
    concatenate x1, other arithmetic, local(): jnp.concatenate([inner_weight.T, blank, inner_down.T, outer_weight.T, bla...  25.6 us
    ppermute x18, starting transfers between devices, send(): return lax.ppermute(value, 'col', lane_pairs(pairs))  25.2 us
    reduce_scatter x2, waiting for transfers between devices, local(): far.append(lax.psum_scatter(share, 'col', scatter_dimension=0))  9.95 us
  transfers between devices with their start and end apart: 34, of which 17 were waited for; matrix products, arithmetic and copies ran while one was open for 11% of the time, Pallas kernels for 27%

profile of v5, /device:TPU:8, one launch (start us, length us, event | category | flops | bytes accessed | tf_op | source)
XLA Modules:
  0.0 337.1 jit_solution(10650112421586789438)
XLA Ops:
  7.2 1.5 slice_bitcast_fusion.1
  9.8 1.2 pad_maximum_fusion.1
  11.0 1.2 pad_maximum_fusion.2
  13.8 25.6 %pad_maximum_fusion.weight_ref = bf16[3584,5120]{1,0:T(8,128)(2,1)} fusion(bf16[64,5120]{1,0:T(8,128)(2,1)S(1)} %copy-done.15, bf16[1728,5120]{1,0:T(8,128)(2,1)} %bitcast.45, bf16[64,5120]{1,0:T(8,128)(2,1)S(1)} %bitcast.47, bf16[1728,5120]{1,0:T(8,128)(2,1)} %bitcast.46), kind=kLoop, calls=%fused_computation | loop fusion | flops 146800640 | bytes 73400320 | tf_op jit(solution)/shard_map/concatenate | solution.py:326
  39.3 69.5 %all-gather.5.cloned.1.call-done = bf16[16,512,640]{2,1,0:T(8,128)(2,1)} async-done(((bf16[2,512,640]{2,1,0:T(8,128)(2,1)}), bf16[16,512,640]{2,1,0:T(8,128)(2,1)}) %all-gather.5.cloned.1.call-update) | async-done | bytes 10485776 | tf_op jit(solution)/shard_map/all_gather | solution.py:321
  108.9 30.2 %shard_map.137 = (bf16[512,1792]{1,0:T(8,128)(2,1)}, bf16[512,128]{1,0:T(8,128)(2,1)S(1)}, f32[128,1792]{1,0:T(8,128)}) custom-call(bf16[8,2,512,640]{3,2,1,0:T(8,128)(2,1)} %bitcast.52, bf16[3584,5120]{1,0:T(8,128)(2,1)} %pad_maximum_fusion.weight_ref, f32[1,1792]{1,0:T(1,128)S(1)} %broadcast_in_dim.2.bias_ref, bf16[128,1792]{1,0:T(8,128)(2,1)S(1)} %pad.16.up_ref, ...), custom_call_target="tpu_custom_call" | custom-call | flops 20000000000 | bytes 36000000 | tf_op jit(solution)/shard_map/pallas_call | solution.py:102
  139.1 15.1 %shard_map.138 = (bf16[8,352,640]{2,1,0:T(8,128)(2,1)}, bf16[4,160,640]{2,1,0:T(8,128)(2,1)S(1)}, bf16[4,160,640]{2,1,0:T(8,128)(2,1)S(1)}) custom-call(s32[2]{0:T(128)S(1)} %pad_add_fusion.place_ref, bf16[512,1792]{1,0:T(8,128)(2,1)} %get-tuple-element.14.grad_ref, bf16[3584,5120]{1,0:T(8,128)(2,1)} %pad_maximum_fusion.weight_ref), custom_call_target="tpu_custom_call" | custom-call | flops 20000000000 | bytes 36000000 | tf_op jit(solution)/shard_map/pallas_call | solution.py:167
  154.9 1.8 collective-permute-done.7
  158.2 1.3 collective-permute-start.4
  159.6 1.4 collective-permute-start.11
  161.0 1.3 collective-permute-start.1
  162.3 1.3 collective-permute-start.8
  163.6 1.0 fusion.12.refs_2_
  164.7 1.3 collective-permute-start.5
  166.0 10.3 %collective-permute-done.11 = bf16[256,128]{1,0:T(8,128)(2,1)S(1)} collective-permute-done((bf16[256,128]{1,0:T(8,128)(2,1)S(1)}, bf16[256,128]{1,0:T(8,128)(2,1)S(1)}, u32[]{:S(2)}, u32[]{:S(2)}) %collective-permute-start.11) | collective-permute-done | bytes 65568 | tf_op jit(solution)/shard_map/ppermute | solution.py:201
  176.3 2.1 collective-permute-done.8
  179.1 16.5 %collective-permute-done.5 = bf16[160,640]{1,0:T(8,128)(2,1)S(1)} collective-permute-done((bf16[160,640]{1,0:T(8,128)(2,1)S(1)}, bf16[160,640]{1,0:T(8,128)(2,1)S(1)}, u32[]{:S(2)}, u32[]{:S(2)}) %collective-permute-start.5) | collective-permute-done | bytes 204832 | tf_op jit(solution)/shard_map/ppermute | solution.py:201
  195.6 0.9 fusion.10
  196.5 1.4 collective-permute-start.9
  197.9 1.3 collective-permute-start.13
  199.2 1.9 collective-permute-start.2
  201.1 2.9 collective-permute-done.9
  204.7 8.6 %collective-permute-done.2 = bf16[160,640]{1,0:T(8,128)(2,1)S(1)} collective-permute-done((bf16[160,640]{1,0:T(8,128)(2,1)}, bf16[160,640]{1,0:T(8,128)(2,1)S(1)}, u32[]{:S(2)}, u32[]{:S(2)}) %collective-permute-start.2) | collective-permute-done | bytes 204832 | tf_op jit(solution)/shard_map/ppermute | solution.py:201
  214.8 1.9 collective-permute-start.6
  216.7 3.9 %collective-permute-start.3 = (bf16[160,640]{1,0:T(8,128)(2,1)}, bf16[160,640]{1,0:T(8,128)(2,1)}, u32[]{:S(2)}, u32[]{:S(2)}) collective-permute-start(bf16[160,640]{1,0:T(8,128)(2,1)} %fusion.13.refs_1_.refs_0_), channel_id=1, source_target_pairs={{0,2},{1,3},{2,4},{3,5},{4,6},{5,7},{8,10},{9,11},{10,12},{11,13},... | collective-permute-start | bytes 614408 | tf_op jit(solution)/shard_map/ppermute | solution.py:201
  221.3 0.9 add_convert_fusion.5
  222.3 0.9 copy-done.1
  224.1 29.7 %shard_map.142 = (bf16[512,1792]{1,0:T(8,128)(2,1)}, bf16[512,128]{1,0:T(8,128)(2,1)S(1)}, f32[128,1792]{1,0:T(8,128)}) custom-call(bf16[8,2,512,640]{3,2,1,0:T(8,128)(2,1)} %bitcast.51, bf16[3584,5120]{1,0:T(8,128)(2,1)} %pad_maximum_fusion.weight_ref, f32[1,1792]{1,0:T(1,128)S(1)} %broadcast_in_dim.2.bias_ref, bf16[128,1792]{1,0:T(8,128)(2,1)S(1)} %pad.16.up_ref, ...), custom_call_target="tpu_custom_call" | custom-call | flops 20000000000 | bytes 36000000 | tf_op jit(solution)/shard_map/pallas_call | solution.py:102
  253.9 1.1 fusion.15.refs_1_
  254.9 15.3 %shard_map.143 = bf16[8,512,640]{2,1,0:T(8,128)(2,1)} custom-call(s32[2]{0:T(128)S(1)} %pad_add_fusion.place_ref, bf16[512,1792]{1,0:T(8,128)(2,1)} %get-tuple-element.19.grad_ref, bf16[3584,5120]{1,0:T(8,128)(2,1)} %pad_maximum_fusion.weight_ref, bf16[512,128]{1,0:T(8,128)(2,1)S(1)} %pad_maximum_fusion.4.refs_0_, bf16[160,640]{1,0:T(8,128)(2,1)S(1)} %fusion.15.refs_1_), custom_call_target="tpu_custom_call" | custom-call | flops 20000000000 | bytes 36000000 | tf_op jit(solution)/shard_map/pallas_call | solution.py:167
  270.9 0.9 collective-permute-done.15
  271.8 1.3 collective-permute-start.16
  274.1 5.4 %collective-permute-done.16 = bf16[256,128]{1,0:T(8,128)(2,1)S(1)} collective-permute-done((bf16[256,128]{1,0:T(8,128)(2,1)S(1)}, bf16[256,128]{1,0:T(8,128)(2,1)S(1)}, u32[]{:S(2)}, u32[]{:S(2)}) %collective-permute-start.16) | collective-permute-done | bytes 65568 | tf_op jit(solution)/shard_map/ppermute | solution.py:201
  279.5 1.4 collective-permute-start.17
  281.0 1.5 collective-permute-start.26
  282.5 1.5 collective-permute-start.28
  284.0 1.3 collective-permute-done.17
  285.3 1.3 collective-permute-start.20
  287.6 7.2 %collective-permute-done.20 = bf16[256,128]{1,0:T(8,128)(2,1)S(1)} collective-permute-done((bf16[256,128]{1,0:T(8,128)(2,1)S(1)}, bf16[256,128]{1,0:T(8,128)(2,1)S(1)}, u32[]{:S(2)}, u32[]{:S(2)}) %collective-permute-start.20) | collective-permute-done | bytes 65568 | tf_op jit(solution)/shard_map/ppermute | solution.py:201
  294.8 1.3 collective-permute-start.21
  296.5 3.8 %collective-permute-done.21 = bf16[256,128]{1,0:T(8,128)(2,1)S(1)} collective-permute-done((bf16[256,128]{1,0:T(8,128)(2,1)S(1)}, bf16[256,128]{1,0:T(8,128)(2,1)S(1)}, u32[]{:S(2)}, u32[]{:S(2)}) %collective-permute-start.21) | collective-permute-done | bytes 65568 | tf_op jit(solution)/shard_map/ppermute | solution.py:201
  300.6 2.0 collective-permute-start.29
  302.6 1.4 collective-permute-start.27
  305.8 2.5 collective-permute-start.25
  310.0 1.1 collective-permute-done.27
  312.7 4.7 %collective-permute-done.24 = bf16[128,640]{1,0:T(8,128)(2,1)S(1)} collective-permute-done((bf16[128,640]{1,0:T(8,128)(2,1)S(1)}, bf16[128,640]{1,0:T(8,128)(2,1)S(1)}, u32[]{:S(2)}, u32[]{:S(2)}) %collective-permute-start.24) | collective-permute-done | bytes 163872 | tf_op jit(solution)/shard_map/ppermute | solution.py:290
  318.2 9.9 %reduce-scatter.5.cloned.1.call-done = bf16[1,512,640]{2,1,0:T(8,128)(2,1)} async-done(((bf16[8,512,640]{2,1,0:T(8,128)(2,1)}), bf16[1,512,640]{2,1,0:T(8,128)(2,1)}) %reduce-scatter.5.cloned.1.call-update) | async-done | bytes 655376 | tf_op jit(solution)/shard_map/reduce_scatter | solution.py:353
  328.1 2.4 pad_maximum_fusion.3
  (123 shorter events, 18.2 us)
Async XLA Ops:
  7.2 101.7 %all-gather.5.cloned.1.call-start = ((), (), s32[]{:S(2)}) async-start(), calls=%async_computation.4 | async-start | bytes 11796480 | tf_op jit(solution)/shard_map/all_gather | solution.py:321
  11.0 211.3 %all-gather.7.cloned.1.call-start = ((), (), s32[]{:S(2)}) async-start(), calls=%async_computation.5 | async-start | bytes 11796480 | tf_op jit(solution)/shard_map/all_gather | solution.py:321
  12.3 305.9 %reduce-scatter.3.cloned.1.call-start = ((), (), s32[]{:S(2)}) async-start(), calls=%async_computation.2 | async-start | bytes 4055040 | tf_op jit(solution)/shard_map/reduce_scatter | solution.py:353
  13.4 95.5 %copy-start.2 = (bf16[128,1792]{1,0:T(8,128)(2,1)}, bf16[128,1792]{1,0:T(8,128)(2,1)S(1)}, u32[]{:S(2)}) copy-start(bf16[128,1792]{1,0:T(8,128)(2,1)S(1)} %get-tuple-element.41.down_hi_ref) | copy-start | bytes 1376260
  154.2 3.2 collective-permute-start
  154.6 173.5 %reduce-scatter.5.cloned.1.call-start = ((), (), s32[]{:S(2)}) async-start(), calls=%async_computation.3 | async-start | bytes 5898240 | tf_op jit(solution)/shard_map/reduce_scatter | solution.py:353
  154.7 2.0 collective-permute-start.7
  156.6 2.9 copy-start.5
  156.7 2.9 copy-start.7
  156.7 4.3 %copy-start.17 = (bf16[256,128]{1,0:T(8,128)(2,1)}, bf16[256,128]{1,0:T(8,128)(2,1)S(1)}, u32[]{:S(2)}) copy-start(bf16[256,128]{1,0:T(8,128)(2,1)S(1)} %get-tuple-element.25.refs_0_) | copy-start | bytes 196612
  156.7 2.8 collective-permute-start.10
  158.2 2.8 copy-start.13
  158.2 5.5 %collective-permute-start.4 = (bf16[160,640]{1,0:T(8,128)(2,1)S(1)}, bf16[160,640]{1,0:T(8,128)(2,1)}, u32[]{:S(2)}, u32[]{:S(2)}) collective-permute-start(bf16[160,640]{1,0:T(8,128)(2,1)S(1)} %get-tuple-element.29.refs_2_), channel_id=1, source_target_pairs={{6,4},{7,5},{14,12},{15,13},{22,20},{23,21},{30,28},{31,29}} | collective-permute-start | bytes 614408 | tf_op jit(solution)/shard_map/ppermute | solution.py:201
  159.6 18.9 %copy-start.6 = (bf16[256,128]{1,0:T(8,128)(2,1)S(1)}, bf16[256,128]{1,0:T(8,128)(2,1)}, u32[]{:S(2)}) copy-start(bf16[256,128]{1,0:T(8,128)(2,1)} %copy-done.5) | copy-start | bytes 196612
  159.6 16.7 %collective-permute-start.11 = (bf16[256,128]{1,0:T(8,128)(2,1)S(1)}, bf16[256,128]{1,0:T(8,128)(2,1)S(1)}, u32[]{:S(2)}, u32[]{:S(2)}) collective-permute-start(bf16[256,128]{1,0:T(8,128)(2,1)S(1)} %fusion.19), channel_id=1, source_target_pairs={{4,2},{5,3},{12,10},{13,11},{20,18},{21,19},{28,26},{29,27}} | collective-permute-start | bytes 196616 | tf_op jit(solution)/shard_map/ppermute | solution.py:201
  161.0 17.4 %copy-start.8 = (bf16[256,128]{1,0:T(8,128)(2,1)S(1)}, bf16[256,128]{1,0:T(8,128)(2,1)}, u32[]{:S(2)}) copy-start(bf16[256,128]{1,0:T(8,128)(2,1)} %copy-done.7) | copy-start | bytes 196612
  161.0 18.1 %collective-permute-start.1 = (bf16[160,640]{1,0:T(8,128)(2,1)}, bf16[160,640]{1,0:T(8,128)(2,1)S(1)}, u32[]{:S(2)}, u32[]{:S(2)}) collective-permute-start(bf16[160,640]{1,0:T(8,128)(2,1)} %get-tuple-element.30.refs_1_), channel_id=1, source_target_pairs={{0,2},{1,3},{8,10},{9,11},{16,18},{17,19},{24,26},{25,27}} | collective-permute-start | bytes 614408 | tf_op jit(solution)/shard_map/ppermute | solution.py:201
  162.3 16.1 %collective-permute-start.8 = (bf16[256,128]{1,0:T(8,128)(2,1)}, bf16[256,128]{1,0:T(8,128)(2,1)S(1)}, u32[]{:S(2)}, u32[]{:S(2)}) collective-permute-start(bf16[256,128]{1,0:T(8,128)(2,1)} %shard_map.139), channel_id=1, source_target_pairs={{0,2},{1,3},{8,10},{9,11},{16,18},{17,19},{24,26},{25,27}} | collective-permute-start | bytes 196616 | tf_op jit(solution)/shard_map/ppermute | solution.py:201
  164.7 31.8 %copy-start.14 = (bf16[160,640]{1,0:T(8,128)(2,1)}, bf16[160,640]{1,0:T(8,128)(2,1)S(1)}, u32[]{:S(2)}) copy-start(bf16[160,640]{1,0:T(8,128)(2,1)S(1)} %fusion.12.refs_2_) | copy-start | bytes 614404
  164.7 30.9 %collective-permute-start.5 = (bf16[160,640]{1,0:T(8,128)(2,1)S(1)}, bf16[160,640]{1,0:T(8,128)(2,1)S(1)}, u32[]{:S(2)}, u32[]{:S(2)}) collective-permute-start(bf16[160,640]{1,0:T(8,128)(2,1)S(1)} %fusion.12.refs_2_), channel_id=1, source_target_pairs={{4,2},{5,3},{6,4},{7,5},{12,10},{13,11},{14,12},{15,13},{20,18},{2... | collective-permute-start | bytes 614408 | tf_op jit(solution)/shard_map/ppermute | solution.py:201
  196.5 18.3 %copy-start = (bf16[160,640]{1,0:T(8,128)(2,1)S(1)}, bf16[160,640]{1,0:T(8,128)(2,1)}, u32[]{:S(2)}) copy-start(bf16[160,640]{1,0:T(8,128)(2,1)} %get-tuple-element.27.refs_2_.refs_1_) | copy-start | bytes 614404
  196.5 7.6 %collective-permute-start.9 = (bf16[256,128]{1,0:T(8,128)(2,1)}, bf16[256,128]{1,0:T(8,128)(2,1)S(1)}, u32[]{:S(2)}, u32[]{:S(2)}) collective-permute-start(bf16[256,128]{1,0:T(8,128)(2,1)} %shard_map.140), channel_id=1, source_target_pairs={{2,4},{3,5},{10,12},{11,13},{18,20},{19,21},{26,28},{27,29}} | collective-permute-start | bytes 196616 | tf_op jit(solution)/shard_map/ppermute | solution.py:201
  197.9 22.7 %collective-permute-start.13 = (bf16[256,128]{1,0:T(8,128)(2,1)S(1)}, bf16[256,128]{1,0:T(8,128)(2,1)S(1)}, u32[]{:S(2)}, u32[]{:S(2)}) collective-permute-start(bf16[256,128]{1,0:T(8,128)(2,1)S(1)} %get-tuple-element.49.refs_3_), channel_id=1, source_target_pairs={{2,0},{3,1},{10,8},{11,9},{18,16},{19,17},{26,24},{27,25}} | collective-permute-start | bytes 196616 | tf_op jit(solution)/shard_map/ppermute | solution.py:201
  199.2 14.1 %collective-permute-start.2 = (bf16[160,640]{1,0:T(8,128)(2,1)}, bf16[160,640]{1,0:T(8,128)(2,1)S(1)}, u32[]{:S(2)}, u32[]{:S(2)}) collective-permute-start(bf16[160,640]{1,0:T(8,128)(2,1)} %get-tuple-element.28.refs_1_), channel_id=1, source_target_pairs={{0,2},{1,3},{2,4},{3,5},{8,10},{9,11},{10,12},{11,13},{16,18},{17,... | collective-permute-start | bytes 614408 | tf_op jit(solution)/shard_map/ppermute | solution.py:201
  214.1 7.2 %collective-permute-start.12 = (bf16[256,128]{1,0:T(8,128)(2,1)}, bf16[256,128]{1,0:T(8,128)(2,1)S(1)}, u32[]{:S(2)}, u32[]{:S(2)}) collective-permute-start(bf16[256,128]{1,0:T(8,128)(2,1)} %shard_map.141.refs_2_), channel_id=1, source_target_pairs={{4,6},{5,7},{12,14},{13,15},{20,22},{21,23},{28,30},{29,31}} | collective-permute-start | bytes 196616 | tf_op jit(solution)/shard_map/ppermute | solution.py:201
  214.8 39.1 %collective-permute-start.6 = (bf16[160,640]{1,0:T(8,128)(2,1)S(1)}, bf16[160,640]{1,0:T(8,128)(2,1)S(1)}, u32[]{:S(2)}, u32[]{:S(2)}) collective-permute-start(bf16[160,640]{1,0:T(8,128)(2,1)S(1)} %copy-done), channel_id=1, source_target_pairs={{2,0},{3,1},{4,2},{5,3},{6,4},{7,5},{10,8},{11,9},{12,10},{13,11},... | collective-permute-start | bytes 614408 | tf_op jit(solution)/shard_map/ppermute | solution.py:201
  216.7 37.2 %collective-permute-start.3 = (bf16[160,640]{1,0:T(8,128)(2,1)}, bf16[160,640]{1,0:T(8,128)(2,1)}, u32[]{:S(2)}, u32[]{:S(2)}) collective-permute-start(bf16[160,640]{1,0:T(8,128)(2,1)} %fusion.13.refs_1_.refs_0_), channel_id=1, source_target_pairs={{0,2},{1,3},{2,4},{3,5},{4,6},{5,7},{8,10},{9,11},{10,12},{11,13},... | collective-permute-start | bytes 614408 | tf_op jit(solution)/shard_map/ppermute | solution.py:201
  222.2 31.6 %collective-permute-start.14 = (bf16[256,128]{1,0:T(8,128)(2,1)S(1)}, bf16[256,128]{1,0:T(8,128)(2,1)S(1)}, u32[]{:S(2)}, u32[]{:S(2)}) collective-permute-start(bf16[256,128]{1,0:T(8,128)(2,1)S(1)} %add_convert_fusion.5), channel_id=1, source_target_pairs={{0,1},{1,0},{2,3},{3,2},{4,5},{5,4},{6,7},{7,6},{8,9},{9,8},{10,11... | collective-permute-start | bytes 196616 | tf_op jit(solution)/shard_map/ppermute | solution.py:205
  253.8 16.4 %copy-start.18 = (bf16[256,128]{1,0:T(8,128)(2,1)}, bf16[256,128]{1,0:T(8,128)(2,1)S(1)}, u32[]{:S(2)}) copy-start(bf16[256,128]{1,0:T(8,128)(2,1)S(1)} %get-tuple-element.48) | copy-start | bytes 196612
  270.3 2.8 copy-start.12
  270.3 1.4 collective-permute-start.15
  271.8 7.7 %collective-permute-start.16 = (bf16[256,128]{1,0:T(8,128)(2,1)S(1)}, bf16[256,128]{1,0:T(8,128)(2,1)S(1)}, u32[]{:S(2)}, u32[]{:S(2)}) collective-permute-start(bf16[256,128]{1,0:T(8,128)(2,1)S(1)} %get-tuple-element.23), channel_id=1, source_target_pairs={{0,2},{1,3},{8,10},{9,11},{16,18},{17,19},{24,26},{25,27}} | collective-permute-start | bytes 196616 | tf_op jit(solution)/shard_map/ppermute | solution.py:201
  273.2 13.4 %copy-start.10 = (bf16[1024,640]{1,0:T(8,128)(2,1)S(1)}, bf16[1024,640]{1,0:T(8,128)(2,1)}, u32[]{:S(2)}) copy-start(bf16[1024,640]{1,0:T(8,128)(2,1)} %param.11) | copy-start | bytes 3932164
  273.2 13.4 %copy-start.19 = (bf16[256,128]{1,0:T(8,128)(2,1)S(1)}, bf16[256,128]{1,0:T(8,128)(2,1)}, u32[]{:S(2)}) copy-start(bf16[256,128]{1,0:T(8,128)(2,1)} %copy-done.18) | copy-start | bytes 196612
  273.3 10.7 %collective-permute-start.19 = (bf16[256,128]{1,0:T(8,128)(2,1)S(1)}, bf16[256,128]{1,0:T(8,128)(2,1)S(1)}, u32[]{:S(2)}, u32[]{:S(2)}) collective-permute-start(bf16[256,128]{1,0:T(8,128)(2,1)S(1)} %get-tuple-element.23), channel_id=1, source_target_pairs={{6,4},{7,5},{14,12},{15,13},{22,20},{23,21},{30,28},{31,29}} | collective-permute-start | bytes 196616 | tf_op jit(solution)/shard_map/ppermute | solution.py:201
  279.5 16.6 %copy-start.4 = (bf16[1024,640]{1,0:T(8,128)(2,1)S(1)}, bf16[1024,640]{1,0:T(8,128)(2,1)}, u32[]{:S(2)}) copy-start(bf16[1024,640]{1,0:T(8,128)(2,1)} %param.10) | copy-start | bytes 3932164
  279.5 5.8 %collective-permute-start.17 = (bf16[256,128]{1,0:T(8,128)(2,1)S(1)}, bf16[256,128]{1,0:T(8,128)(2,1)S(1)}, u32[]{:S(2)}, u32[]{:S(2)}) collective-permute-start(bf16[256,128]{1,0:T(8,128)(2,1)S(1)} %fusion.20), channel_id=1, source_target_pairs={{2,4},{3,5},{10,12},{11,13},{18,20},{19,21},{26,28},{27,29}} | collective-permute-start | bytes 196616 | tf_op jit(solution)/shard_map/ppermute | solution.py:201
  281.0 19.5 %collective-permute-start.26 = (bf16[64,1728]{1,0:T(8,128)(2,1)S(1)}, bf16[64,1728]{1,0:T(8,128)(2,1)S(1)}, u32[]{:S(2)}, u32[]{:S(2)}) collective-permute-start(bf16[64,1728]{1,0:T(8,128)(2,1)S(1)} %get-tuple-element.38), channel_id=1, source_target_pairs={{0,8},{8,0},{16,24},{24,16},{1,9},{9,1},{17,25},{25,17},{2,10},{10... | collective-permute-start | bytes 663560 | tf_op jit(solution)/shard_map/ppermute | solution.py:279
  282.5 17.9 %collective-permute-start.28 = (bf16[64,1728]{1,0:T(8,128)(2,1)S(1)}, bf16[64,1728]{1,0:T(8,128)(2,1)S(1)}, u32[]{:S(2)}, u32[]{:S(2)}) collective-permute-start(bf16[64,1728]{1,0:T(8,128)(2,1)S(1)} %get-tuple-element.37), channel_id=1, source_target_pairs={{0,16},{8,24},{16,0},{24,8},{1,17},{9,25},{17,1},{25,9},{2,18},{10... | collective-permute-start | bytes 663560 | tf_op jit(solution)/shard_map/ppermute | solution.py:279
  285.3 9.4 %collective-permute-start.20 = (bf16[256,128]{1,0:T(8,128)(2,1)S(1)}, bf16[256,128]{1,0:T(8,128)(2,1)S(1)}, u32[]{:S(2)}, u32[]{:S(2)}) collective-permute-start(bf16[256,128]{1,0:T(8,128)(2,1)S(1)} %get-tuple-element.46), channel_id=1, source_target_pairs={{4,2},{5,3},{12,10},{13,11},{20,18},{21,19},{28,26},{29,27}} | collective-permute-start | bytes 196616 | tf_op jit(solution)/shard_map/ppermute | solution.py:201
  286.9 9.5 %collective-permute-start.18 = (bf16[256,128]{1,0:T(8,128)(2,1)S(1)}, bf16[256,128]{1,0:T(8,128)(2,1)S(1)}, u32[]{:S(2)}, u32[]{:S(2)}) collective-permute-start(bf16[256,128]{1,0:T(8,128)(2,1)S(1)} %get-tuple-element.45), channel_id=1, source_target_pairs={{4,6},{5,7},{12,14},{13,15},{20,22},{21,23},{28,30},{29,31}} | collective-permute-start | bytes 196616 | tf_op jit(solution)/shard_map/ppermute | solution.py:201
  294.8 5.5 %collective-permute-start.21 = (bf16[256,128]{1,0:T(8,128)(2,1)S(1)}, bf16[256,128]{1,0:T(8,128)(2,1)S(1)}, u32[]{:S(2)}, u32[]{:S(2)}) collective-permute-start(bf16[256,128]{1,0:T(8,128)(2,1)S(1)} %add_convert_fusion.3), channel_id=1, source_target_pairs={{2,0},{3,1},{10,8},{11,9},{18,16},{19,17},{26,24},{27,25}} | collective-permute-start | bytes 196616 | tf_op jit(solution)/shard_map/ppermute | solution.py:201
  300.4 3.7 %collective-permute-start.22 = (bf16[256,128]{1,0:T(8,128)(2,1)S(1)}, bf16[256,128]{1,0:T(8,128)(2,1)S(1)}, u32[]{:S(2)}, u32[]{:S(2)}) collective-permute-start(bf16[256,128]{1,0:T(8,128)(2,1)S(1)} %add_convert_fusion.2), channel_id=1, source_target_pairs={{0,1},{1,0},{2,3},{3,2},{4,5},{5,4},{6,7},{7,6},{8,9},{9,8},{10,11... | collective-permute-start | bytes 196616 | tf_op jit(solution)/shard_map/ppermute | solution.py:205
  300.6 8.5 %collective-permute-start.29 = (bf16[64,1728]{1,0:T(8,128)(2,1)S(1)}, bf16[64,1728]{1,0:T(8,128)(2,1)S(1)}, u32[]{:S(2)}, u32[]{:S(2)}) collective-permute-start(bf16[64,1728]{1,0:T(8,128)(2,1)S(1)} %get-tuple-element.35), channel_id=1, source_target_pairs={{0,8},{8,0},{16,24},{24,16},{1,9},{9,1},{17,25},{25,17},{2,10},{10... | collective-permute-start | bytes 663560 | tf_op jit(solution)/shard_map/ppermute | solution.py:279
  302.6 8.4 %collective-permute-start.27 = (bf16[64,1728]{1,0:T(8,128)(2,1)S(1)}, bf16[64,1728]{1,0:T(8,128)(2,1)S(1)}, u32[]{:S(2)}, u32[]{:S(2)}) collective-permute-start(bf16[64,1728]{1,0:T(8,128)(2,1)S(1)} %get-tuple-element.36), channel_id=1, source_target_pairs={{0,16},{8,24},{16,0},{24,8},{1,17},{9,25},{17,1},{25,9},{2,18},{10... | collective-permute-start | bytes 663560 | tf_op jit(solution)/shard_map/ppermute | solution.py:279
  304.7 8.0 %collective-permute-start.23 = (bf16[128,640]{1,0:T(8,128)(2,1)S(1)}, bf16[128,640]{1,0:T(8,128)(2,1)S(1)}, u32[]{:S(2)}, u32[]{:S(2)}) collective-permute-start(bf16[128,640]{1,0:T(8,128)(2,1)S(1)} %fusion.17), channel_id=1, source_target_pairs={{0,8},{8,0},{16,24},{24,16},{1,9},{9,1},{17,25},{25,17},{2,10},{10... | collective-permute-start | bytes 491528 | tf_op jit(solution)/shard_map/ppermute | solution.py:290
  305.3 12.1 %collective-permute-start.24 = (bf16[128,640]{1,0:T(8,128)(2,1)S(1)}, bf16[128,640]{1,0:T(8,128)(2,1)S(1)}, u32[]{:S(2)}, u32[]{:S(2)}) collective-permute-start(bf16[128,640]{1,0:T(8,128)(2,1)S(1)} %fusion.17), channel_id=1, source_target_pairs={{0,16},{8,24},{16,0},{24,8},{1,17},{9,25},{17,1},{25,9},{2,18},{10... | collective-permute-start | bytes 491528 | tf_op jit(solution)/shard_map/ppermute | solution.py:290
  305.8 11.6 %collective-permute-start.25 = (bf16[128,640]{1,0:T(8,128)(2,1)S(1)}, bf16[128,640]{1,0:T(8,128)(2,1)S(1)}, u32[]{:S(2)}, u32[]{:S(2)}) collective-permute-start(bf16[128,640]{1,0:T(8,128)(2,1)S(1)} %fusion.17), channel_id=1, source_target_pairs={{0,24},{8,16},{16,8},{24,0},{1,25},{9,17},{17,9},{25,1},{2,26},{10... | collective-permute-start | bytes 491528 | tf_op jit(solution)/shard_map/ppermute | solution.py:290
  (10 other events, 13.1 us)
Sparse Core Ops, SparseCore 0:
  11.1 97.7 all-gather.4
  111.1 107.8 all-gather.6
  221.4 41.8 reduce-scatter.2
  270.4 57.6 reduce-scatter.4

commit v6 on v5

--- a/solution.py
+++ b/solution.py
@@ -16,7 +16,7 @@
 COLS = 256
 VMEM_BYTES = 52 * 1024 * 1024
 COST = pl.CostEstimate(flops=20_000_000_000, bytes_accessed=36_000_000, transcendentals=0)
-SPLIT = ((512, 320), (512, 0))
+SPLIT = ((512, 384), (512, 0))
 
 
 def dot_nn(left, right):
@@ -335,30 +335,28 @@
     for index, (both, first) in enumerate(zip(gathered, firsts)):
         def advance(left):
             sent = []
-            while index and lows[-1].left() > left:
-                ready = moving[-1].hop() if moving[-1] else []
-                sent = ready + lows[-1].hop(ready)
+            while index and moving[-1] and moving[-1].left() > left:
+                sent = moving[-1].hop()
             return sent
 
         grad_pre, low, grad = hidden_call(
             both, weights, bias, up_hi, down_lo, down_hi, ff, advance(0)
         )
-        if index:
-            lows[-1] = lows[-1].result()
-            after = [lows[-1]]
-            if moving[-1]:
-                moving[-1] = moving[-1].result()
-                after.append(moving[-1])
-        share, *shares = share_call(place, grad_pre, weights, chips, first, after if index else ())
+        after = []
+        if index and moving[-1]:
+            moving[-1] = moving[-1].result()
+            after = moving[-1:]
+        share, *shares = share_call(place, grad_pre, weights, chips, first, after)
         far.append(lax.psum_scatter(share, "col", scatter_dimension=0))
         moving.append(Shares(*shares, chips) if first else None)
-        lows.append(LowSum(low, core, chips))
+        lows.append(low)
         grads = grad if grads is None else grads + grad
     hidden_part = (grads[:, :ff] * scale).astype(BF16)
-    while lows[-1].left():
+    summing = LowSum(jnp.concatenate(lows, axis=0), core, chips)
+    while summing.left():
         ready = moving[-1].hop() if moving[-1] else []
-        lows[-1].hop(ready)
-    lows[-1] = lows[-1].result()
+        summing.hop(ready)
+    low = summing.result()
     if moving[-1]:
         moving[-1] = moving[-1].result()
     outs = []
@@ -370,12 +368,8 @@
     inner_up_grad = hidden_sums[:rank]
     outer_down_grad = hidden_sums[rank:].T
 
-    feature_part = 0.0
-    for start, size, gated, low in zip(starts, sizes, gated_parts, lows):
-        tokens = tokens_in[start : start + size]
-        feature_part = feature_part + jnp.concatenate(
-            [dot_tn(low[:, :rank], gated), dot_tn(low[:, rank:], tokens)], axis=0
-        )
+    gated = jnp.concatenate(gated_parts, axis=0)
+    feature_part = jnp.concatenate([dot_tn(low[:, :rank], gated), dot_tn(low[:, rank:], tokens_in)], axis=0)
     feature_sums = sum_rows_at_once((feature_part * scale).astype(BF16))
     outer_up_grad = feature_sums[:rank]
     inner_down_grad = feature_sums[rank:].T

time: 341 us -> 346 us (1.015)
  waiting for transfers between devices: 148 us -> 163 us
  starting transfers between devices: 36.6 us -> 29.3 us
    ppermute x18 -> x12, waiting for transfers between devices: 58.2 us -> 68.1 us  [send(): return lax.ppermute(value, 'col', lane_pairs(pairs))]
    ppermute x18 -> x12, starting transfers between devices: 25.2 us -> 17.7 us  [send(): return lax.ppermute(value, 'col', lane_pairs(pairs))]
    all_gather x2, waiting for transfers between devices: 69.6 us -> 76.3 us  [local(): gathered.append(lax.all_gather(both, 'col', axis=0))]
  transfers between devices with their start and end apart: 34 -> 26, of which waited for: 17 -> 15; matrix products, arithmetic and copies ran while one was open for 11% -> 11% of each run, Pallas kernels for 27% -> 26%
where the time goes in v6:
time: 346 us; the launch traced here: 342 us
  waiting for transfers between devices  163 us (47%)
  Pallas kernels  90.4 us (26%)
  other arithmetic  39.2 us (11%)
  starting transfers between devices  29.3 us (8%)
  between operations  14.2 us (4%)
  local copies, waits for them, and re-layouts  5.02 us (1%)
    all_gather x2, waiting for transfers between devices, local(): gathered.append(lax.all_gather(both, 'col', axis=0))  76.3 us
    ppermute x12, waiting for transfers between devices, send(): return lax.ppermute(value, 'col', lane_pairs(pairs))  68.1 us
    pallas_call x2, Pallas kernels, hidden_call(): pl.pallas_call(functools.partial(hidden_kernel, ff), grid=(devices,), in_...  59.9 us
    pallas_call x2, Pallas kernels, share_call(): pl.pallas_call(functools.partial(share_kernel, first), grid_spec=pltpu.Pr...  30.5 us
    concatenate x1, other arithmetic, local(): jnp.concatenate([inner_weight.T, blank, inner_down.T, outer_weight.T, bla...  25.8 us
    ppermute x12, starting transfers between devices, send(): return lax.ppermute(value, 'col', lane_pairs(pairs))  17.7 us
    reduce_scatter x2, waiting for transfers between devices, local(): far.append(lax.psum_scatter(share, 'col', scatter_dimension=0))  7.45 us
    ppermute x4, starting transfers between devices, sum_rows(): lax.ppermute(piece.astype(BF16), 'row', [(i, i ^ bit) for i in range(rows)])  7.15 us
  transfers between devices with their start and end apart: 26, of which 15 were waited for; matrix products, arithmetic and copies ran while one was open for 11% of the time, Pallas kernels for 26%

profile of v6, /device:TPU:8, one launch (start us, length us, event | category | flops | bytes accessed | tf_op | source)
XLA Modules:
  0.0 341.7 jit_solution(5036774331797474205)
XLA Ops:
  7.2 1.5 slice_bitcast_fusion.1
  8.7 0.8 dynamic_slice.3
  9.8 0.8 copy-done.1
  10.6 1.2 pad_maximum_fusion.1
  11.9 1.2 pad_maximum_fusion.2
  13.4 0.8 copy-done.8
  14.4 25.8 %pad_maximum_fusion.weight_ref = bf16[3584,5120]{1,0:T(8,128)(2,1)} fusion(bf16[64,5120]{1,0:T(8,128)(2,1)S(1)} %copy-done.8, bf16[1728,5120]{1,0:T(8,128)(2,1)} %bitcast.44, bf16[64,5120]{1,0:T(8,128)(2,1)S(1)} %bitcast.48, bf16[1728,5120]{1,0:T(8,128)(2,1)} %bitcast.45), kind=kLoop, calls=%fused_computation | loop fusion | flops 146800640 | bytes 73400320 | tf_op jit(solution)/shard_map/concatenate | solution.py:326
  40.2 69.5 %all-gather.5.cloned.1.call-done = bf16[16,512,640]{2,1,0:T(8,128)(2,1)} async-done(((bf16[2,512,640]{2,1,0:T(8,128)(2,1)}), bf16[16,512,640]{2,1,0:T(8,128)(2,1)}) %all-gather.5.cloned.1.call-update) | async-done | bytes 10485776 | tf_op jit(solution)/shard_map/all_gather | solution.py:321
  109.7 30.3 %shard_map.137 = (bf16[512,1792]{1,0:T(8,128)(2,1)}, bf16[512,128]{1,0:T(8,128)(2,1)S(1)}, f32[128,1792]{1,0:T(8,128)}) custom-call(bf16[8,2,512,640]{3,2,1,0:T(8,128)(2,1)} %bitcast.53, bf16[3584,5120]{1,0:T(8,128)(2,1)} %pad_maximum_fusion.weight_ref, f32[1,1792]{1,0:T(1,128)S(1)} %broadcast_in_dim.2.bias_ref, bf16[128,1792]{1,0:T(8,128)(2,1)S(1)} %pad.16.up_ref, ...), custom_call_target="tpu_custom_call" | custom-call | flops 20000000000 | bytes 36000000 | tf_op jit(solution)/shard_map/pallas_call | solution.py:102
  140.0 15.2 %shard_map.138 = (bf16[8,320,640]{2,1,0:T(8,128)(2,1)}, bf16[4,192,640]{2,1,0:T(8,128)(2,1)S(1)}, bf16[4,192,640]{2,1,0:T(8,128)(2,1)}) custom-call(s32[2]{0:T(128)S(1)} %pad_add_fusion.place_ref, bf16[512,1792]{1,0:T(8,128)(2,1)} %get-tuple-element.14.grad_ref, bf16[3584,5120]{1,0:T(8,128)(2,1)} %pad_maximum_fusion.weight_ref), custom_call_target="tpu_custom_call" | custom-call | flops 20000000000 | bytes 36000000 | tf_op jit(solution)/shard_map/pallas_call | solution.py:167
  155.6 2.5 collective-permute-done
  158.1 1.2 bitcast_convert_fusion.1
  160.0 1.3 collective-permute-start.1
  161.3 1.0 fusion.8
  162.3 1.3 collective-permute-start.5
  163.6 13.1 %collective-permute-done.1 = bf16[192,640]{1,0:T(8,128)(2,1)S(1)} collective-permute-done((bf16[192,640]{1,0:T(8,128)(2,1)S(1)}, bf16[192,640]{1,0:T(8,128)(2,1)S(1)}, u32[]{:S(2)}, u32[]{:S(2)}) %collective-permute-start.1) | collective-permute-done | bytes 245792 | tf_op jit(solution)/shard_map/ppermute | solution.py:201
  176.8 20.9 %collective-permute-done.5 = bf16[192,640]{1,0:T(8,128)(2,1)S(1)} collective-permute-done((bf16[192,640]{1,0:T(8,128)(2,1)S(1)}, bf16[192,640]{1,0:T(8,128)(2,1)S(1)}, u32[]{:S(2)}, u32[]{:S(2)}) %collective-permute-start.5) | collective-permute-done | bytes 245792 | tf_op jit(solution)/shard_map/ppermute | solution.py:201
  197.7 1.2 fusion.6
  198.9 1.9 collective-permute-start.2
  200.9 3.9 %collective-permute-start.6 = (bf16[192,640]{1,0:T(8,128)(2,1)S(1)}, bf16[192,640]{1,0:T(8,128)(2,1)}, u32[]{:S(2)}, u32[]{:S(2)}) collective-permute-start(bf16[192,640]{1,0:T(8,128)(2,1)S(1)} %get-tuple-element.25.refs_1_), channel_id=1, source_target_pairs={{2,0},{3,1},{4,2},{5,3},{6,4},{7,5},{10,8},{11,9},{12,10},{13,11},... | collective-permute-start | bytes 737288 | tf_op jit(solution)/shard_map/ppermute | solution.py:201
  204.8 9.8 %collective-permute-done.2 = bf16[192,640]{1,0:T(8,128)(2,1)S(1)} collective-permute-done((bf16[192,640]{1,0:T(8,128)(2,1)S(1)}, bf16[192,640]{1,0:T(8,128)(2,1)S(1)}, u32[]{:S(2)}, u32[]{:S(2)}) %collective-permute-start.2) | collective-permute-done | bytes 245792 | tf_op jit(solution)/shard_map/ppermute | solution.py:201
  214.6 1.0 fusion.9.refs_0_
  215.7 1.9 collective-permute-start.3
  217.6 6.8 %all-gather.7.cloned.1.call-done = bf16[16,512,640]{2,1,0:T(8,128)(2,1)} async-done(((bf16[2,512,640]{2,1,0:T(8,128)(2,1)}), bf16[16,512,640]{2,1,0:T(8,128)(2,1)}) %all-gather.7.cloned.1.call-update) | async-done | bytes 10485776 | tf_op jit(solution)/shard_map/all_gather | solution.py:321
  224.4 29.6 %shard_map.139 = (bf16[512,1792]{1,0:T(8,128)(2,1)}, bf16[512,128]{1,0:T(8,128)(2,1)S(1)}, f32[128,1792]{1,0:T(8,128)}) custom-call(bf16[8,2,512,640]{3,2,1,0:T(8,128)(2,1)} %bitcast.52, bf16[3584,5120]{1,0:T(8,128)(2,1)} %pad_maximum_fusion.weight_ref, f32[1,1792]{1,0:T(1,128)S(1)} %broadcast_in_dim.2.bias_ref, bf16[128,1792]{1,0:T(8,128)(2,1)S(1)} %pad.16.up_ref, ...), custom_call_target="tpu_custom_call" | custom-call | flops 20000000000 | bytes 36000000 | tf_op jit(solution)/shard_map/pallas_call | solution.py:102
  254.0 1.3 fusion.11.refs_0_
  255.4 15.4 %shard_map.140 = bf16[8,512,640]{2,1,0:T(8,128)(2,1)} custom-call(s32[2]{0:T(128)S(1)} %pad_add_fusion.place_ref, bf16[512,1792]{1,0:T(8,128)(2,1)} %get-tuple-element.18.grad_ref, bf16[3584,5120]{1,0:T(8,128)(2,1)} %pad_maximum_fusion.weight_ref, bf16[192,640]{1,0:T(8,128)(2,1)S(1)} %fusion.11.refs_0_), custom_call_target="tpu_custom_call" | custom-call | flops 20000000000 | bytes 36000000 | tf_op jit(solution)/shard_map/pallas_call | solution.py:167
  271.1 1.1 collective-permute-done.7
  272.3 1.3 collective-permute-start.8
  274.2 5.6 %collective-permute-done.8 = bf16[512,128]{1,0:T(8,128)(2,1)S(1)} collective-permute-done((bf16[512,128]{1,0:T(8,128)(2,1)S(1)}, bf16[512,128]{1,0:T(8,128)(2,1)S(1)}, u32[]{:S(2)}, u32[]{:S(2)}) %collective-permute-start.8) | collective-permute-done | bytes 131104 | tf_op jit(solution)/shard_map/ppermute | solution.py:201
  279.9 1.3 collective-permute-start.9
  281.3 6.7 %collective-permute-done.9 = bf16[512,128]{1,0:T(8,128)(2,1)S(1)} collective-permute-done((bf16[512,128]{1,0:T(8,128)(2,1)S(1)}, bf16[512,128]{1,0:T(8,128)(2,1)S(1)}, u32[]{:S(2)}, u32[]{:S(2)}) %collective-permute-start.9) | collective-permute-done | bytes 131104 | tf_op jit(solution)/shard_map/ppermute | solution.py:201
  288.1 1.3 collective-permute-start.12
  289.4 2.1 collective-permute-start.18
  291.6 1.5 collective-permute-start.20
  293.7 7.4 %collective-permute-done.12 = bf16[512,128]{1,0:T(8,128)(2,1)S(1)} collective-permute-done((bf16[512,128]{1,0:T(8,128)(2,1)S(1)}, bf16[512,128]{1,0:T(8,128)(2,1)S(1)}, u32[]{:S(2)}, u32[]{:S(2)}) %collective-permute-start.12) | collective-permute-done | bytes 131104 | tf_op jit(solution)/shard_map/ppermute | solution.py:201
  301.2 1.4 collective-permute-start.13
  302.8 2.1 collective-permute-start.21
  304.9 1.4 collective-permute-start.19
  306.3 4.5 %collective-permute-done.13 = bf16[512,128]{1,0:T(8,128)(2,1)S(1)} collective-permute-done((bf16[512,128]{1,0:T(8,128)(2,1)S(1)}, bf16[512,128]{1,0:T(8,128)(2,1)S(1)}, u32[]{:S(2)}, u32[]{:S(2)}) %collective-permute-start.13) | collective-permute-done | bytes 131104 | tf_op jit(solution)/shard_map/ppermute | solution.py:201
  311.1 0.8 add_bitcast_fusion
  313.3 1.7 collective-permute-start.15
  315.0 1.5 collective-permute-start.16
  316.9 0.8 convert_add_fusion.3
  317.7 2.7 collective-permute-done.15
  320.4 4.1 %collective-permute-done.16 = bf16[128,640]{1,0:T(8,128)(2,1)S(1)} collective-permute-done((bf16[128,640]{1,0:T(8,128)(2,1)S(1)}, bf16[128,640]{1,0:T(8,128)(2,1)S(1)}, u32[]{:S(2)}, u32[]{:S(2)}) %collective-permute-start.16) | collective-permute-done | bytes 163872 | tf_op jit(solution)/shard_map/ppermute | solution.py:290
  325.3 7.5 %reduce-scatter.5.cloned.1.call-done = bf16[1,512,640]{2,1,0:T(8,128)(2,1)} async-done(((bf16[8,512,640]{2,1,0:T(8,128)(2,1)}), bf16[1,512,640]{2,1,0:T(8,128)(2,1)}) %reduce-scatter.5.cloned.1.call-update) | async-done | bytes 655376 | tf_op jit(solution)/shard_map/reduce_scatter | solution.py:350
  332.8 2.4 pad_maximum_fusion.3
  (72 shorter events, 7.0 us)
Async XLA Ops:
  7.2 2.3 copy-start.5
  7.2 102.5 %all-gather.5.cloned.1.call-start = ((), (), s32[]{:S(2)}) async-start(), calls=%async_computation.4 | async-start | bytes 11796480 | tf_op jit(solution)/shard_map/all_gather | solution.py:321
  9.8 0.9 copy-start.1
  9.8 2.1 copy-start.3
  11.8 212.6 %all-gather.7.cloned.1.call-start = ((), (), s32[]{:S(2)}) async-start(), calls=%async_computation.5 | async-start | bytes 11796480 | tf_op jit(solution)/shard_map/all_gather | solution.py:321
  11.9 1.3 copy-start.12
  11.9 1.3 copy-start.10
  11.9 1.5 copy-start.11
  13.1 1.1 copy-start.8
  13.1 1.3 copy-start.9
  13.2 312.2 %reduce-scatter.3.cloned.1.call-start = ((), (), s32[]{:S(2)}) async-start(), calls=%async_computation.2 | async-start | bytes 3686400 | tf_op jit(solution)/shard_map/reduce_scatter | solution.py:350
  155.2 2.9 collective-permute-start
  155.6 177.2 %reduce-scatter.5.cloned.1.call-start = ((), (), s32[]{:S(2)}) async-start(), calls=%async_computation.3 | async-start | bytes 5898240 | tf_op jit(solution)/shard_map/reduce_scatter | solution.py:350
  159.3 2.0 collective-permute-start.4
  160.0 16.8 %collective-permute-start.1 = (bf16[192,640]{1,0:T(8,128)(2,1)S(1)}, bf16[192,640]{1,0:T(8,128)(2,1)S(1)}, u32[]{:S(2)}, u32[]{:S(2)}) collective-permute-start(bf16[192,640]{1,0:T(8,128)(2,1)S(1)} %get-tuple-element.28), channel_id=1, source_target_pairs={{0,2},{1,3},{8,10},{9,11},{16,18},{17,19},{24,26},{25,27}} | collective-permute-start | bytes 737288 | tf_op jit(solution)/shard_map/ppermute | solution.py:201
  162.3 35.3 %collective-permute-start.5 = (bf16[192,640]{1,0:T(8,128)(2,1)S(1)}, bf16[192,640]{1,0:T(8,128)(2,1)S(1)}, u32[]{:S(2)}, u32[]{:S(2)}) collective-permute-start(bf16[192,640]{1,0:T(8,128)(2,1)S(1)} %fusion.8), channel_id=1, source_target_pairs={{4,2},{5,3},{6,4},{7,5},{12,10},{13,11},{14,12},{15,13},{20,18},{2... | collective-permute-start | bytes 737288 | tf_op jit(solution)/shard_map/ppermute | solution.py:201
  198.9 15.7 %collective-permute-start.2 = (bf16[192,640]{1,0:T(8,128)(2,1)S(1)}, bf16[192,640]{1,0:T(8,128)(2,1)S(1)}, u32[]{:S(2)}, u32[]{:S(2)}) collective-permute-start(bf16[192,640]{1,0:T(8,128)(2,1)S(1)} %get-tuple-element.26), channel_id=1, source_target_pairs={{0,2},{1,3},{2,4},{3,5},{8,10},{9,11},{10,12},{11,13},{16,18},{17,... | collective-permute-start | bytes 737288 | tf_op jit(solution)/shard_map/ppermute | solution.py:201
  200.9 53.2 %collective-permute-start.6 = (bf16[192,640]{1,0:T(8,128)(2,1)S(1)}, bf16[192,640]{1,0:T(8,128)(2,1)}, u32[]{:S(2)}, u32[]{:S(2)}) collective-permute-start(bf16[192,640]{1,0:T(8,128)(2,1)S(1)} %get-tuple-element.25.refs_1_), channel_id=1, source_target_pairs={{2,0},{3,1},{4,2},{5,3},{6,4},{7,5},{10,8},{11,9},{12,10},{13,11},... | collective-permute-start | bytes 737288 | tf_op jit(solution)/shard_map/ppermute | solution.py:201
  215.7 38.3 %collective-permute-start.3 = (bf16[192,640]{1,0:T(8,128)(2,1)S(1)}, bf16[192,640]{1,0:T(8,128)(2,1)}, u32[]{:S(2)}, u32[]{:S(2)}) collective-permute-start(bf16[192,640]{1,0:T(8,128)(2,1)S(1)} %fusion.9.refs_0_), channel_id=1, source_target_pairs={{0,2},{1,3},{2,4},{3,5},{4,6},{5,7},{8,10},{9,11},{10,12},{11,13},... | collective-permute-start | bytes 737288 | tf_op jit(solution)/shard_map/ppermute | solution.py:201
  270.7 10.5 %copy-start.7 = (f32[128,1792]{1,0:T(8,128)S(1)}, f32[128,1792]{1,0:T(8,128)}, u32[]{:S(2)}) copy-start(f32[128,1792]{1,0:T(8,128)} %get-tuple-element.22) | copy-start | bytes 2752516
  270.7 10.5 %copy-start.6 = (f32[128,1792]{1,0:T(8,128)S(1)}, f32[128,1792]{1,0:T(8,128)}, u32[]{:S(2)}) copy-start(f32[128,1792]{1,0:T(8,128)} %get-tuple-element.21) | copy-start | bytes 2752516
  270.8 1.4 collective-permute-start.7
  272.3 7.6 %collective-permute-start.8 = (bf16[512,128]{1,0:T(8,128)(2,1)S(1)}, bf16[512,128]{1,0:T(8,128)(2,1)S(1)}, u32[]{:S(2)}, u32[]{:S(2)}) collective-permute-start(bf16[512,128]{1,0:T(8,128)(2,1)S(1)} %get-tuple-element.23), channel_id=1, source_target_pairs={{0,2},{1,3},{8,10},{9,11},{16,18},{17,19},{24,26},{25,27}} | collective-permute-start | bytes 393224 | tf_op jit(solution)/shard_map/ppermute | solution.py:201
  273.6 7.7 %collective-permute-start.11 = (bf16[512,128]{1,0:T(8,128)(2,1)S(1)}, bf16[512,128]{1,0:T(8,128)(2,1)S(1)}, u32[]{:S(2)}, u32[]{:S(2)}) collective-permute-start(bf16[512,128]{1,0:T(8,128)(2,1)S(1)} %get-tuple-element.23), channel_id=1, source_target_pairs={{6,4},{7,5},{14,12},{15,13},{22,20},{23,21},{30,28},{31,29}} | collective-permute-start | bytes 393224 | tf_op jit(solution)/shard_map/ppermute | solution.py:201
  279.9 8.1 %collective-permute-start.9 = (bf16[512,128]{1,0:T(8,128)(2,1)S(1)}, bf16[512,128]{1,0:T(8,128)(2,1)S(1)}, u32[]{:S(2)}, u32[]{:S(2)}) collective-permute-start(bf16[512,128]{1,0:T(8,128)(2,1)S(1)} %fusion.13), channel_id=1, source_target_pairs={{2,4},{3,5},{10,12},{11,13},{18,20},{19,21},{26,28},{27,29}} | collective-permute-start | bytes 393224 | tf_op jit(solution)/shard_map/ppermute | solution.py:201
  288.1 13.1 %collective-permute-start.12 = (bf16[512,128]{1,0:T(8,128)(2,1)S(1)}, bf16[512,128]{1,0:T(8,128)(2,1)S(1)}, u32[]{:S(2)}, u32[]{:S(2)}) collective-permute-start(bf16[512,128]{1,0:T(8,128)(2,1)S(1)} %get-tuple-element.42), channel_id=1, source_target_pairs={{4,2},{5,3},{12,10},{13,11},{20,18},{21,19},{28,26},{29,27}} | collective-permute-start | bytes 393224 | tf_op jit(solution)/shard_map/ppermute | solution.py:201
  289.4 13.3 %collective-permute-start.18 = (bf16[64,1728]{1,0:T(8,128)(2,1)S(1)}, bf16[64,1728]{1,0:T(8,128)(2,1)S(1)}, u32[]{:S(2)}, u32[]{:S(2)}) collective-permute-start(bf16[64,1728]{1,0:T(8,128)(2,1)S(1)} %get-tuple-element.36), channel_id=1, source_target_pairs={{0,8},{8,0},{16,24},{24,16},{1,9},{9,1},{17,25},{25,17},{2,10},{10... | collective-permute-start | bytes 663560 | tf_op jit(solution)/shard_map/ppermute | solution.py:279
  291.6 11.1 %collective-permute-start.20 = (bf16[64,1728]{1,0:T(8,128)(2,1)S(1)}, bf16[64,1728]{1,0:T(8,128)(2,1)S(1)}, u32[]{:S(2)}, u32[]{:S(2)}) collective-permute-start(bf16[64,1728]{1,0:T(8,128)(2,1)S(1)} %get-tuple-element.35), channel_id=1, source_target_pairs={{0,16},{8,24},{16,0},{24,8},{1,17},{9,25},{17,1},{25,9},{2,18},{10... | collective-permute-start | bytes 663560 | tf_op jit(solution)/shard_map/ppermute | solution.py:279
  293.1 13.3 %collective-permute-start.10 = (bf16[512,128]{1,0:T(8,128)(2,1)S(1)}, bf16[512,128]{1,0:T(8,128)(2,1)S(1)}, u32[]{:S(2)}, u32[]{:S(2)}) collective-permute-start(bf16[512,128]{1,0:T(8,128)(2,1)S(1)} %get-tuple-element.41), channel_id=1, source_target_pairs={{4,6},{5,7},{12,14},{13,15},{20,22},{21,23},{28,30},{29,31}} | collective-permute-start | bytes 393224 | tf_op jit(solution)/shard_map/ppermute | solution.py:201
  301.2 11.2 %copy-start = (bf16[1024,640]{1,0:T(8,128)(2,1)S(1)}, bf16[1024,640]{1,0:T(8,128)(2,1)}, u32[]{:S(2)}) copy-start(bf16[1024,640]{1,0:T(8,128)(2,1)} %param.10) | copy-start | bytes 3932164
  301.2 9.6 %collective-permute-start.13 = (bf16[512,128]{1,0:T(8,128)(2,1)S(1)}, bf16[512,128]{1,0:T(8,128)(2,1)S(1)}, u32[]{:S(2)}, u32[]{:S(2)}) collective-permute-start(bf16[512,128]{1,0:T(8,128)(2,1)S(1)} %add_convert_fusion.3), channel_id=1, source_target_pairs={{2,0},{3,1},{10,8},{11,9},{18,16},{19,17},{26,24},{27,25}} | collective-permute-start | bytes 393224 | tf_op jit(solution)/shard_map/ppermute | solution.py:201
  302.8 8.3 %collective-permute-start.21 = (bf16[64,1728]{1,0:T(8,128)(2,1)S(1)}, bf16[64,1728]{1,0:T(8,128)(2,1)S(1)}, u32[]{:S(2)}, u32[]{:S(2)}) collective-permute-start(bf16[64,1728]{1,0:T(8,128)(2,1)S(1)} %get-tuple-element.33), channel_id=1, source_target_pairs={{0,8},{8,0},{16,24},{24,16},{1,9},{9,1},{17,25},{25,17},{2,10},{10... | collective-permute-start | bytes 663560 | tf_op jit(solution)/shard_map/ppermute | solution.py:279
  304.9 11.9 %collective-permute-start.19 = (bf16[64,1728]{1,0:T(8,128)(2,1)S(1)}, bf16[64,1728]{1,0:T(8,128)(2,1)S(1)}, u32[]{:S(2)}, u32[]{:S(2)}) collective-permute-start(bf16[64,1728]{1,0:T(8,128)(2,1)S(1)} %get-tuple-element.34), channel_id=1, source_target_pairs={{0,16},{8,24},{16,0},{24,8},{1,17},{9,25},{17,1},{25,9},{2,18},{10... | collective-permute-start | bytes 663560 | tf_op jit(solution)/shard_map/ppermute | solution.py:279
  311.0 1.9 copy-start.2
  311.0 1.9 copy-start.4
  311.0 1.4 collective-permute-start.14
  313.3 7.1 %collective-permute-start.15 = (bf16[128,640]{1,0:T(8,128)(2,1)S(1)}, bf16[128,640]{1,0:T(8,128)(2,1)S(1)}, u32[]{:S(2)}, u32[]{:S(2)}) collective-permute-start(bf16[128,640]{1,0:T(8,128)(2,1)S(1)} %fusion.12), channel_id=1, source_target_pairs={{0,8},{8,0},{16,24},{24,16},{1,9},{9,1},{17,25},{25,17},{2,10},{10... | collective-permute-start | bytes 491528 | tf_op jit(solution)/shard_map/ppermute | solution.py:290
  315.0 9.5 %collective-permute-start.16 = (bf16[128,640]{1,0:T(8,128)(2,1)S(1)}, bf16[128,640]{1,0:T(8,128)(2,1)S(1)}, u32[]{:S(2)}, u32[]{:S(2)}) collective-permute-start(bf16[128,640]{1,0:T(8,128)(2,1)S(1)} %fusion.12), channel_id=1, source_target_pairs={{0,16},{8,24},{16,0},{24,8},{1,17},{9,25},{17,1},{25,9},{2,18},{10... | collective-permute-start | bytes 491528 | tf_op jit(solution)/shard_map/ppermute | solution.py:290
  316.5 8.0 %collective-permute-start.17 = (bf16[128,640]{1,0:T(8,128)(2,1)S(1)}, bf16[128,640]{1,0:T(8,128)(2,1)S(1)}, u32[]{:S(2)}, u32[]{:S(2)}) collective-permute-start(bf16[128,640]{1,0:T(8,128)(2,1)S(1)} %fusion.12), channel_id=1, source_target_pairs={{0,24},{8,16},{16,8},{24,0},{1,25},{9,17},{17,9},{25,1},{2,26},{10... | collective-permute-start | bytes 491528 | tf_op jit(solution)/shard_map/ppermute | solution.py:290
Sparse Core Ops, SparseCore 0:
  12.0 97.7 all-gather.4
  111.9 112.4 all-gather.6
  226.7 39.2 reduce-scatter.2
  270.9 61.8 reduce-scatter.4

commit v7 on v5

--- a/solution.py
+++ b/solution.py
@@ -16,7 +16,7 @@
 COLS = 256
 VMEM_BYTES = 52 * 1024 * 1024
 COST = pl.CostEstimate(flops=20_000_000_000, bytes_accessed=36_000_000, transcendentals=0)
-SPLIT = ((512, 320), (512, 0))
+SPLIT = ((512, 288), (512, 0))
 
 
 def dot_nn(left, right):
@@ -364,7 +364,9 @@
     outs = []
     for near, rest in zip(moving, far):
         outs += [rest] if near is None else [near, rest]
-    tokens_grad = jnp.concatenate(outs, axis=0)
+    ending = outs.pop()
+    placed = jnp.concatenate(outs + [jnp.zeros_like(ending)], axis=0)
+    tokens_grad = lax.dynamic_update_slice_in_dim(placed, ending, tok_rows - ending.shape[0], 0)
 
     hidden_sums = sum_rows(hidden_part)
     inner_up_grad = hidden_sums[:rank]

time: 341 us -> 339 us (level)
  waiting for transfers between devices: 148 us -> 141 us
    ppermute x18, waiting for transfers between devices: 58.2 us -> 49.3 us  [send(): return lax.ppermute(value, 'col', lane_pairs(pairs))]
  transfers between devices with their start and end apart: 34 -> 34, of which waited for: 17 -> 17; matrix products, arithmetic and copies ran while one was open for 11% -> 12% of each run, Pallas kernels for 27% -> 27%
where the time goes in v7:
time: 339 us; the launch traced here: 335 us
  waiting for transfers between devices  141 us (42%)
  Pallas kernels  91.1 us (27%)
  other arithmetic  40.1 us (12%)
  starting transfers between devices  38.4 us (11%)
  between operations  14.4 us (4%)
  local copies, waits for them, and re-layouts  8.47 us (2%)
    all_gather x2, waiting for transfers between devices, local(): gathered.append(lax.all_gather(both, 'col', axis=0))  69.6 us
    pallas_call x2, Pallas kernels, hidden_call(): pl.pallas_call(functools.partial(hidden_kernel, ff), grid=(devices,), in_...  60.6 us
    ppermute x18, waiting for transfers between devices, send(): return lax.ppermute(value, 'col', lane_pairs(pairs))  49.3 us
    pallas_call x2, Pallas kernels, share_call(): pl.pallas_call(functools.partial(share_kernel, first), grid_spec=pltpu.Pr...  30.5 us
    ppermute x18, starting transfers between devices, send(): return lax.ppermute(value, 'col', lane_pairs(pairs))  27.7 us
    concatenate x1, other arithmetic, local(): jnp.concatenate([inner_weight.T, blank, inner_down.T, outer_weight.T, bla...  25.5 us
    reduce_scatter x2, waiting for transfers between devices, local(): far.append(lax.psum_scatter(share, 'col', scatter_dimension=0))  12.2 us
  transfers between devices with their start and end apart: 34, of which 17 were waited for; matrix products, arithmetic and copies ran while one was open for 12% of the time, Pallas kernels for 27%

profile of v7, /device:TPU:8, one launch (start us, length us, event | category | flops | bytes accessed | tf_op | source)
XLA Modules:
  0.0 334.9 jit_solution(3074153685373638516)
XLA Ops:
  7.2 1.5 slice_bitcast_fusion
  9.8 1.2 pad_maximum_fusion.1
  11.0 1.2 pad_maximum_fusion.2
  13.8 25.5 %pad_maximum_fusion.weight_ref = bf16[3584,5120]{1,0:T(8,128)(2,1)} fusion(bf16[64,5120]{1,0:T(8,128)(2,1)S(1)} %copy-done.12, bf16[1728,5120]{1,0:T(8,128)(2,1)} %bitcast.46, bf16[64,5120]{1,0:T(8,128)(2,1)S(1)} %bitcast.48, bf16[1728,5120]{1,0:T(8,128)(2,1)} %bitcast.47), kind=kLoop, calls=%fused_computation | loop fusion | flops 146800640 | bytes 73400320 | tf_op jit(solution)/shard_map/concatenate | solution.py:326
  39.3 69.6 %all-gather.5.cloned.1.call-done = bf16[16,512,640]{2,1,0:T(8,128)(2,1)} async-done(((bf16[2,512,640]{2,1,0:T(8,128)(2,1)}), bf16[16,512,640]{2,1,0:T(8,128)(2,1)}) %all-gather.5.cloned.1.call-update) | async-done | bytes 10485776 | tf_op jit(solution)/shard_map/all_gather | solution.py:321
  108.9 30.5 %shard_map.137 = (bf16[512,1792]{1,0:T(8,128)(2,1)}, bf16[512,128]{1,0:T(8,128)(2,1)S(1)}, f32[128,1792]{1,0:T(8,128)}) custom-call(bf16[8,2,512,640]{3,2,1,0:T(8,128)(2,1)} %bitcast.52, bf16[3584,5120]{1,0:T(8,128)(2,1)} %pad_maximum_fusion.weight_ref, f32[1,1792]{1,0:T(1,128)S(1)} %broadcast_in_dim.8.bias_ref, bf16[128,1792]{1,0:T(8,128)(2,1)S(1)} %pad.16.up_ref, ...), custom_call_target="tpu_custom_call" | custom-call | flops 20000000000 | bytes 36000000 | tf_op jit(solution)/shard_map/pallas_call | solution.py:102
  139.4 15.1 %shard_map.138 = (bf16[8,368,640]{2,1,0:T(8,128)(2,1)}, bf16[4,144,640]{2,1,0:T(8,128)(2,1)S(1)}, bf16[4,144,640]{2,1,0:T(8,128)(2,1)S(1)}) custom-call(s32[2]{0:T(128)S(1)} %pad_add_fusion.place_ref, bf16[512,1792]{1,0:T(8,128)(2,1)} %get-tuple-element.14.grad_ref, bf16[3584,5120]{1,0:T(8,128)(2,1)} %pad_maximum_fusion.weight_ref), custom_call_target="tpu_custom_call" | custom-call | flops 20000000000 | bytes 36000000 | tf_op jit(solution)/shard_map/pallas_call | solution.py:167
  155.2 1.8 collective-permute-done.7
  157.8 1.2 bitcast_convert_fusion
  159.0 1.3 collective-permute-start.1
  160.3 1.3 collective-permute-start.11
  162.3 1.3 collective-permute-start.8
  163.6 9.6 %collective-permute-done.1 = bf16[144,640]{1,0:T(8,128)(2,1)} collective-permute-done((bf16[144,640]{1,0:T(8,128)(2,1)S(1)}, bf16[144,640]{1,0:T(8,128)(2,1)}, u32[]{:S(2)}, u32[]{:S(2)}) %collective-permute-start.1) | collective-permute-done | bytes 184352 | tf_op jit(solution)/shard_map/ppermute | solution.py:201
  173.2 1.1 fusion.11.refs_1_
  174.4 1.9 collective-permute-start.2
  177.0 13.5 %collective-permute-done.2 = bf16[144,640]{1,0:T(8,128)(2,1)S(1)} collective-permute-done((bf16[144,640]{1,0:T(8,128)(2,1)S(1)}, bf16[144,640]{1,0:T(8,128)(2,1)S(1)}, u32[]{:S(2)}, u32[]{:S(2)}) %collective-permute-start.2) | collective-permute-done | bytes 184352 | tf_op jit(solution)/shard_map/ppermute | solution.py:201
  190.5 1.9 fusion.13
  192.4 4.7 %collective-permute-start.9 = (bf16[256,128]{1,0:T(8,128)(2,1)}, bf16[256,128]{1,0:T(8,128)(2,1)S(1)}, u32[]{:S(2)}, u32[]{:S(2)}) collective-permute-start(bf16[256,128]{1,0:T(8,128)(2,1)} %shard_map.140), channel_id=1, source_target_pairs={{2,4},{3,5},{10,12},{11,13},{18,20},{19,21},{26,28},{27,29}} | collective-permute-start | bytes 196616 | tf_op jit(solution)/shard_map/ppermute | solution.py:201
  197.0 1.3 collective-permute-start.13
  198.3 1.3 collective-permute-start.5
  199.6 1.4 collective-permute-done.9
  201.7 8.6 %collective-permute-done.5 = bf16[144,640]{1,0:T(8,128)(2,1)S(1)} collective-permute-done((bf16[144,640]{1,0:T(8,128)(2,1)}, bf16[144,640]{1,0:T(8,128)(2,1)S(1)}, u32[]{:S(2)}, u32[]{:S(2)}) %collective-permute-start.5) | collective-permute-done | bytes 184352 | tf_op jit(solution)/shard_map/ppermute | solution.py:201
  210.3 1.7 fusion.10.refs_2_.refs_1_
  212.7 2.9 collective-permute-start.3
  215.5 3.0 collective-permute-start.6
  220.5 30.1 %shard_map.142 = (bf16[512,1792]{1,0:T(8,128)(2,1)}, bf16[512,128]{1,0:T(8,128)(2,1)S(1)}, f32[128,1792]{1,0:T(8,128)}) custom-call(bf16[8,2,512,640]{3,2,1,0:T(8,128)(2,1)} %bitcast.51, bf16[3584,5120]{1,0:T(8,128)(2,1)} %pad_maximum_fusion.weight_ref, f32[1,1792]{1,0:T(1,128)S(1)} %broadcast_in_dim.8.bias_ref, bf16[128,1792]{1,0:T(8,128)(2,1)S(1)} %pad.16.up_ref, ...), custom_call_target="tpu_custom_call" | custom-call | flops 20000000000 | bytes 36000000 | tf_op jit(solution)/shard_map/pallas_call | solution.py:102
  251.7 15.4 %shard_map.143 = bf16[8,512,640]{2,1,0:T(8,128)(2,1)} custom-call(s32[2]{0:T(128)S(1)} %pad_add_fusion.place_ref, bf16[512,1792]{1,0:T(8,128)(2,1)} %get-tuple-element.19.grad_ref, bf16[3584,5120]{1,0:T(8,128)(2,1)} %pad_maximum_fusion.weight_ref, bf16[512,128]{1,0:T(8,128)(2,1)S(1)} %pad_maximum_fusion.3.refs_0_, bf16[144,640]{1,0:T(8,128)(2,1)S(1)} %fusion.15.refs_1_), custom_call_target="tpu_custom_call" | custom-call | flops 20000000000 | bytes 36000000 | tf_op jit(solution)/shard_map/pallas_call | solution.py:167
  268.6 1.3 collective-permute-start.16
  270.8 4.5 %collective-permute-done.16 = bf16[256,128]{1,0:T(8,128)(2,1)S(1)} collective-permute-done((bf16[256,128]{1,0:T(8,128)(2,1)S(1)}, bf16[256,128]{1,0:T(8,128)(2,1)S(1)}, u32[]{:S(2)}, u32[]{:S(2)}) %collective-permute-start.16) | collective-permute-done | bytes 65568 | tf_op jit(solution)/shard_map/ppermute | solution.py:201
  275.4 1.4 collective-permute-start.17
  277.9 1.5 collective-permute-start.26
  279.4 1.4 collective-permute-done.17
  280.8 1.3 collective-permute-start.20
  283.1 6.9 %collective-permute-done.20 = bf16[256,128]{1,0:T(8,128)(2,1)S(1)} collective-permute-done((bf16[256,128]{1,0:T(8,128)(2,1)S(1)}, bf16[256,128]{1,0:T(8,128)(2,1)S(1)}, u32[]{:S(2)}, u32[]{:S(2)}) %collective-permute-start.20) | collective-permute-done | bytes 65568 | tf_op jit(solution)/shard_map/ppermute | solution.py:201
  290.0 1.3 collective-permute-start.21
  291.6 3.4 %collective-permute-done.21 = bf16[256,128]{1,0:T(8,128)(2,1)S(1)} collective-permute-done((bf16[256,128]{1,0:T(8,128)(2,1)S(1)}, bf16[256,128]{1,0:T(8,128)(2,1)S(1)}, u32[]{:S(2)}, u32[]{:S(2)}) %collective-permute-start.21) | collective-permute-done | bytes 65568 | tf_op jit(solution)/shard_map/ppermute | solution.py:201
  295.4 1.7 collective-permute-start.27
  297.0 1.5 collective-permute-start.29
  299.7 1.5 collective-permute-start.24
  301.3 1.5 collective-permute-start.23
  302.7 1.1 collective-permute-done.27
  306.3 2.6 collective-permute-done.25
  308.9 1.5 collective-permute-done.24
  310.4 1.4 collective-permute-done.23
  312.6 1.3 maximum_maximum_fusion
  313.9 12.2 %reduce-scatter.5.cloned.1.call-done = bf16[1,512,640]{2,1,0:T(8,128)(2,1)} async-done(((bf16[8,512,640]{2,1,0:T(8,128)(2,1)}), bf16[1,512,640]{2,1,0:T(8,128)(2,1)}) %reduce-scatter.5.cloned.1.call-update) | async-done | bytes 655376 | tf_op jit(solution)/shard_map/reduce_scatter | solution.py:353
  326.1 1.2 bitcast_dynamic-update-slice_fusion
  327.3 1.0 copy-done.6
  (114 shorter events, 19.3 us)
Async XLA Ops:
  7.2 101.7 %all-gather.5.cloned.1.call-start = ((), (), s32[]{:S(2)}) async-start(), calls=%async_computation.4 | async-start | bytes 11796480 | tf_op jit(solution)/shard_map/all_gather | solution.py:321
  7.2 2.3 copy-start.4
  11.0 207.7 %all-gather.7.cloned.1.call-start = ((), (), s32[]{:S(2)}) async-start(), calls=%async_computation.5 | async-start | bytes 11796480 | tf_op jit(solution)/shard_map/all_gather | solution.py:321
  12.2 1.1 copy-start.16
  12.2 1.3 copy-start.12
  12.2 1.5 copy-start.13
  12.3 300.4 %reduce-scatter.3.cloned.1.call-start = ((), (), s32[]{:S(2)}) async-start(), calls=%async_computation.2 | async-start | bytes 4239360 | tf_op jit(solution)/shard_map/reduce_scatter | solution.py:353
  154.5 171.6 %reduce-scatter.5.cloned.1.call-start = ((), (), s32[]{:S(2)}) async-start(), calls=%async_computation.3 | async-start | bytes 5898240 | tf_op jit(solution)/shard_map/reduce_scatter | solution.py:353
  154.6 3.2 collective-permute-start
  155.0 2.0 collective-permute-start.7
  157.1 5.2 %copy-start.14 = (bf16[256,128]{1,0:T(8,128)(2,1)}, bf16[256,128]{1,0:T(8,128)(2,1)S(1)}, u32[]{:S(2)}) copy-start(bf16[256,128]{1,0:T(8,128)(2,1)S(1)} %get-tuple-element.25.refs_0_) | copy-start | bytes 196612
  157.1 3.2 collective-permute-start.10
  158.9 3.4 %copy-start.9 = (bf16[144,640]{1,0:T(8,128)(2,1)}, bf16[144,640]{1,0:T(8,128)(2,1)S(1)}, u32[]{:S(2)}) copy-start(bf16[144,640]{1,0:T(8,128)(2,1)S(1)} %get-tuple-element.30.refs_2_) | copy-start | bytes 552964
  158.9 3.4 %copy-start.11 = (bf16[144,640]{1,0:T(8,128)(2,1)}, bf16[144,640]{1,0:T(8,128)(2,1)S(1)}, u32[]{:S(2)}) copy-start(bf16[144,640]{1,0:T(8,128)(2,1)S(1)} %get-tuple-element.29.refs_1_) | copy-start | bytes 552964
  159.0 14.3 %collective-permute-start.1 = (bf16[144,640]{1,0:T(8,128)(2,1)S(1)}, bf16[144,640]{1,0:T(8,128)(2,1)}, u32[]{:S(2)}, u32[]{:S(2)}) collective-permute-start(bf16[144,640]{1,0:T(8,128)(2,1)S(1)} %get-tuple-element.29.refs_1_), channel_id=1, source_target_pairs={{0,2},{1,3},{8,10},{9,11},{16,18},{17,19},{24,26},{25,27}} | collective-permute-start | bytes 552968 | tf_op jit(solution)/shard_map/ppermute | solution.py:201
  160.3 16.0 %collective-permute-start.11 = (bf16[256,128]{1,0:T(8,128)(2,1)S(1)}, bf16[256,128]{1,0:T(8,128)(2,1)S(1)}, u32[]{:S(2)}, u32[]{:S(2)}) collective-permute-start(bf16[256,128]{1,0:T(8,128)(2,1)S(1)} %fusion.19), channel_id=1, source_target_pairs={{4,2},{5,3},{12,10},{13,11},{20,18},{21,19},{28,26},{29,27}} | collective-permute-start | bytes 196616 | tf_op jit(solution)/shard_map/ppermute | solution.py:201
  161.6 15.4 %collective-permute-start.4 = (bf16[144,640]{1,0:T(8,128)(2,1)S(1)}, bf16[144,640]{1,0:T(8,128)(2,1)S(1)}, u32[]{:S(2)}, u32[]{:S(2)}) collective-permute-start(bf16[144,640]{1,0:T(8,128)(2,1)S(1)} %get-tuple-element.30.refs_2_), channel_id=1, source_target_pairs={{6,4},{7,5},{14,12},{15,13},{22,20},{23,21},{30,28},{31,29}} | collective-permute-start | bytes 552968 | tf_op jit(solution)/shard_map/ppermute | solution.py:201
  162.3 14.0 %collective-permute-start.8 = (bf16[256,128]{1,0:T(8,128)(2,1)}, bf16[256,128]{1,0:T(8,128)(2,1)S(1)}, u32[]{:S(2)}, u32[]{:S(2)}) collective-permute-start(bf16[256,128]{1,0:T(8,128)(2,1)} %shard_map.139), channel_id=1, source_target_pairs={{0,2},{1,3},{8,10},{9,11},{16,18},{17,19},{24,26},{25,27}} | collective-permute-start | bytes 196616 | tf_op jit(solution)/shard_map/ppermute | solution.py:201
  174.3 18.0 %copy-start.10 = (bf16[144,640]{1,0:T(8,128)(2,1)}, bf16[144,640]{1,0:T(8,128)(2,1)S(1)}, u32[]{:S(2)}) copy-start(bf16[144,640]{1,0:T(8,128)(2,1)S(1)} %fusion.11.refs_1_) | copy-start | bytes 552964
  174.4 16.1 %collective-permute-start.2 = (bf16[144,640]{1,0:T(8,128)(2,1)S(1)}, bf16[144,640]{1,0:T(8,128)(2,1)S(1)}, u32[]{:S(2)}, u32[]{:S(2)}) collective-permute-start(bf16[144,640]{1,0:T(8,128)(2,1)S(1)} %fusion.11.refs_1_), channel_id=1, source_target_pairs={{0,2},{1,3},{2,4},{3,5},{8,10},{9,11},{10,12},{11,13},{16,18},{17,... | collective-permute-start | bytes 552968 | tf_op jit(solution)/shard_map/ppermute | solution.py:201
  192.3 20.3 %copy-start = (bf16[144,640]{1,0:T(8,128)(2,1)S(1)}, bf16[144,640]{1,0:T(8,128)(2,1)}, u32[]{:S(2)}) copy-start(bf16[144,640]{1,0:T(8,128)(2,1)} %get-tuple-element.27.refs_1_.refs_0_) | copy-start | bytes 552964
  192.4 8.7 %collective-permute-start.9 = (bf16[256,128]{1,0:T(8,128)(2,1)}, bf16[256,128]{1,0:T(8,128)(2,1)S(1)}, u32[]{:S(2)}, u32[]{:S(2)}) collective-permute-start(bf16[256,128]{1,0:T(8,128)(2,1)} %shard_map.140), channel_id=1, source_target_pairs={{2,4},{3,5},{10,12},{11,13},{18,20},{19,21},{26,28},{27,29}} | collective-permute-start | bytes 196616 | tf_op jit(solution)/shard_map/ppermute | solution.py:201
  197.0 21.5 %collective-permute-start.13 = (bf16[256,128]{1,0:T(8,128)(2,1)S(1)}, bf16[256,128]{1,0:T(8,128)(2,1)S(1)}, u32[]{:S(2)}, u32[]{:S(2)}) collective-permute-start(bf16[256,128]{1,0:T(8,128)(2,1)S(1)} %get-tuple-element.49.refs_3_), channel_id=1, source_target_pairs={{2,0},{3,1},{10,8},{11,9},{18,16},{19,17},{26,24},{27,25}} | collective-permute-start | bytes 196616 | tf_op jit(solution)/shard_map/ppermute | solution.py:201
  198.3 12.0 %collective-permute-start.5 = (bf16[144,640]{1,0:T(8,128)(2,1)}, bf16[144,640]{1,0:T(8,128)(2,1)S(1)}, u32[]{:S(2)}, u32[]{:S(2)}) collective-permute-start(bf16[144,640]{1,0:T(8,128)(2,1)} %get-tuple-element.28.refs_2_), channel_id=1, source_target_pairs={{4,2},{5,3},{6,4},{7,5},{12,10},{13,11},{14,12},{15,13},{20,18},{2... | collective-permute-start | bytes 552968 | tf_op jit(solution)/shard_map/ppermute | solution.py:201
  212.0 6.5 %collective-permute-start.12 = (bf16[256,128]{1,0:T(8,128)(2,1)}, bf16[256,128]{1,0:T(8,128)(2,1)S(1)}, u32[]{:S(2)}, u32[]{:S(2)}) collective-permute-start(bf16[256,128]{1,0:T(8,128)(2,1)} %shard_map.141.refs_2_), channel_id=1, source_target_pairs={{4,6},{5,7},{12,14},{13,15},{20,22},{21,23},{28,30},{29,31}} | collective-permute-start | bytes 196616 | tf_op jit(solution)/shard_map/ppermute | solution.py:201
  212.7 38.0 %collective-permute-start.3 = (bf16[144,640]{1,0:T(8,128)(2,1)S(1)}, bf16[144,640]{1,0:T(8,128)(2,1)S(1)}, u32[]{:S(2)}, u32[]{:S(2)}) collective-permute-start(bf16[144,640]{1,0:T(8,128)(2,1)S(1)} %copy-done), channel_id=1, source_target_pairs={{0,2},{1,3},{2,4},{3,5},{4,6},{5,7},{8,10},{9,11},{10,12},{11,13},... | collective-permute-start | bytes 552968 | tf_op jit(solution)/shard_map/ppermute | solution.py:201
  215.5 35.1 %collective-permute-start.6 = (bf16[144,640]{1,0:T(8,128)(2,1)}, bf16[144,640]{1,0:T(8,128)(2,1)S(1)}, u32[]{:S(2)}, u32[]{:S(2)}) collective-permute-start(bf16[144,640]{1,0:T(8,128)(2,1)} %fusion.10.refs_2_.refs_1_), channel_id=1, source_target_pairs={{2,0},{3,1},{4,2},{5,3},{6,4},{7,5},{10,8},{11,9},{12,10},{13,11},... | collective-permute-start | bytes 552968 | tf_op jit(solution)/shard_map/ppermute | solution.py:201
  218.6 32.0 %collective-permute-start.14 = (bf16[256,128]{1,0:T(8,128)(2,1)S(1)}, bf16[256,128]{1,0:T(8,128)(2,1)S(1)}, u32[]{:S(2)}, u32[]{:S(2)}) collective-permute-start(bf16[256,128]{1,0:T(8,128)(2,1)S(1)} %add_convert_fusion.5), channel_id=1, source_target_pairs={{0,1},{1,0},{2,3},{3,2},{4,5},{5,4},{6,7},{7,6},{8,9},{9,8},{10,11... | collective-permute-start | bytes 196616 | tf_op jit(solution)/shard_map/ppermute | solution.py:205
  267.1 2.8 copy-start.7
  267.1 2.8 copy-start.8
  267.1 1.4 collective-permute-start.15
  268.6 6.8 %collective-permute-start.16 = (bf16[256,128]{1,0:T(8,128)(2,1)S(1)}, bf16[256,128]{1,0:T(8,128)(2,1)S(1)}, u32[]{:S(2)}, u32[]{:S(2)}) collective-permute-start(bf16[256,128]{1,0:T(8,128)(2,1)S(1)} %get-tuple-element.23), channel_id=1, source_target_pairs={{0,2},{1,3},{8,10},{9,11},{16,18},{17,19},{24,26},{25,27}} | collective-permute-start | bytes 196616 | tf_op jit(solution)/shard_map/ppermute | solution.py:201
  270.0 12.1 %copy-start.5 = (bf16[1024,640]{1,0:T(8,128)(2,1)S(1)}, bf16[1024,640]{1,0:T(8,128)(2,1)}, u32[]{:S(2)}) copy-start(bf16[1024,640]{1,0:T(8,128)(2,1)} %param.11) | copy-start | bytes 3932164
  270.0 9.3 %collective-permute-start.19 = (bf16[256,128]{1,0:T(8,128)(2,1)S(1)}, bf16[256,128]{1,0:T(8,128)(2,1)S(1)}, u32[]{:S(2)}, u32[]{:S(2)}) collective-permute-start(bf16[256,128]{1,0:T(8,128)(2,1)S(1)} %get-tuple-element.23), channel_id=1, source_target_pairs={{6,4},{7,5},{14,12},{15,13},{22,20},{23,21},{30,28},{31,29}} | collective-permute-start | bytes 196616 | tf_op jit(solution)/shard_map/ppermute | solution.py:201
  275.4 15.9 %copy-start.3 = (bf16[1024,640]{1,0:T(8,128)(2,1)S(1)}, bf16[1024,640]{1,0:T(8,128)(2,1)}, u32[]{:S(2)}) copy-start(bf16[1024,640]{1,0:T(8,128)(2,1)} %param.10) | copy-start | bytes 3932164
  275.4 5.3 %collective-permute-start.17 = (bf16[256,128]{1,0:T(8,128)(2,1)S(1)}, bf16[256,128]{1,0:T(8,128)(2,1)S(1)}, u32[]{:S(2)}, u32[]{:S(2)}) collective-permute-start(bf16[256,128]{1,0:T(8,128)(2,1)S(1)} %fusion.20), channel_id=1, source_target_pairs={{2,4},{3,5},{10,12},{11,13},{18,20},{19,21},{26,28},{27,29}} | collective-permute-start | bytes 196616 | tf_op jit(solution)/shard_map/ppermute | solution.py:201
  276.9 18.3 %collective-permute-start.28 = (bf16[64,1728]{1,0:T(8,128)(2,1)S(1)}, bf16[64,1728]{1,0:T(8,128)(2,1)S(1)}, u32[]{:S(2)}, u32[]{:S(2)}) collective-permute-start(bf16[64,1728]{1,0:T(8,128)(2,1)S(1)} %get-tuple-element.37), channel_id=1, source_target_pairs={{0,16},{8,24},{16,0},{24,8},{1,17},{9,25},{17,1},{25,9},{2,18},{10... | collective-permute-start | bytes 663560 | tf_op jit(solution)/shard_map/ppermute | solution.py:279
  277.9 17.3 %collective-permute-start.26 = (bf16[64,1728]{1,0:T(8,128)(2,1)S(1)}, bf16[64,1728]{1,0:T(8,128)(2,1)S(1)}, u32[]{:S(2)}, u32[]{:S(2)}) collective-permute-start(bf16[64,1728]{1,0:T(8,128)(2,1)S(1)} %get-tuple-element.38), channel_id=1, source_target_pairs={{0,8},{8,0},{16,24},{24,16},{1,9},{9,1},{17,25},{25,17},{2,10},{10... | collective-permute-start | bytes 663560 | tf_op jit(solution)/shard_map/ppermute | solution.py:279
  280.8 9.2 %collective-permute-start.20 = (bf16[256,128]{1,0:T(8,128)(2,1)S(1)}, bf16[256,128]{1,0:T(8,128)(2,1)S(1)}, u32[]{:S(2)}, u32[]{:S(2)}) collective-permute-start(bf16[256,128]{1,0:T(8,128)(2,1)S(1)} %get-tuple-element.46), channel_id=1, source_target_pairs={{4,2},{5,3},{12,10},{13,11},{20,18},{21,19},{28,26},{29,27}} | collective-permute-start | bytes 196616 | tf_op jit(solution)/shard_map/ppermute | solution.py:201
  282.4 9.3 %collective-permute-start.18 = (bf16[256,128]{1,0:T(8,128)(2,1)S(1)}, bf16[256,128]{1,0:T(8,128)(2,1)S(1)}, u32[]{:S(2)}, u32[]{:S(2)}) collective-permute-start(bf16[256,128]{1,0:T(8,128)(2,1)S(1)} %get-tuple-element.45), channel_id=1, source_target_pairs={{4,6},{5,7},{12,14},{13,15},{20,22},{21,23},{28,30},{29,31}} | collective-permute-start | bytes 196616 | tf_op jit(solution)/shard_map/ppermute | solution.py:201
  290.0 5.1 %collective-permute-start.21 = (bf16[256,128]{1,0:T(8,128)(2,1)S(1)}, bf16[256,128]{1,0:T(8,128)(2,1)S(1)}, u32[]{:S(2)}, u32[]{:S(2)}) collective-permute-start(bf16[256,128]{1,0:T(8,128)(2,1)S(1)} %add_convert_fusion.3), channel_id=1, source_target_pairs={{2,0},{3,1},{10,8},{11,9},{18,16},{19,17},{26,24},{27,25}} | collective-permute-start | bytes 196616 | tf_op jit(solution)/shard_map/ppermute | solution.py:201
  295.1 3.4 %collective-permute-start.22 = (bf16[256,128]{1,0:T(8,128)(2,1)S(1)}, bf16[256,128]{1,0:T(8,128)(2,1)S(1)}, u32[]{:S(2)}, u32[]{:S(2)}) collective-permute-start(bf16[256,128]{1,0:T(8,128)(2,1)S(1)} %add_convert_fusion.2), channel_id=1, source_target_pairs={{0,1},{1,0},{2,3},{3,2},{4,5},{5,4},{6,7},{7,6},{8,9},{9,8},{10,11... | collective-permute-start | bytes 196616 | tf_op jit(solution)/shard_map/ppermute | solution.py:205
  295.4 8.5 %collective-permute-start.27 = (bf16[64,1728]{1,0:T(8,128)(2,1)S(1)}, bf16[64,1728]{1,0:T(8,128)(2,1)S(1)}, u32[]{:S(2)}, u32[]{:S(2)}) collective-permute-start(bf16[64,1728]{1,0:T(8,128)(2,1)S(1)} %get-tuple-element.36), channel_id=1, source_target_pairs={{0,16},{8,24},{16,0},{24,8},{1,17},{9,25},{17,1},{25,9},{2,18},{10... | collective-permute-start | bytes 663560 | tf_op jit(solution)/shard_map/ppermute | solution.py:279
  297.0 8.4 %collective-permute-start.29 = (bf16[64,1728]{1,0:T(8,128)(2,1)S(1)}, bf16[64,1728]{1,0:T(8,128)(2,1)S(1)}, u32[]{:S(2)}, u32[]{:S(2)}) collective-permute-start(bf16[64,1728]{1,0:T(8,128)(2,1)S(1)} %get-tuple-element.35), channel_id=1, source_target_pairs={{0,8},{8,0},{16,24},{24,16},{1,9},{9,1},{17,25},{25,17},{2,10},{10... | collective-permute-start | bytes 663560 | tf_op jit(solution)/shard_map/ppermute | solution.py:279
  299.2 9.7 %collective-permute-start.25 = (bf16[128,640]{1,0:T(8,128)(2,1)S(1)}, bf16[128,640]{1,0:T(8,128)(2,1)S(1)}, u32[]{:S(2)}, u32[]{:S(2)}) collective-permute-start(bf16[128,640]{1,0:T(8,128)(2,1)S(1)} %fusion.17), channel_id=1, source_target_pairs={{0,24},{8,16},{16,8},{24,0},{1,25},{9,17},{17,9},{25,1},{2,26},{10... | collective-permute-start | bytes 491528 | tf_op jit(solution)/shard_map/ppermute | solution.py:290
  299.7 10.7 %collective-permute-start.24 = (bf16[128,640]{1,0:T(8,128)(2,1)S(1)}, bf16[128,640]{1,0:T(8,128)(2,1)S(1)}, u32[]{:S(2)}, u32[]{:S(2)}) collective-permute-start(bf16[128,640]{1,0:T(8,128)(2,1)S(1)} %fusion.17), channel_id=1, source_target_pairs={{0,16},{8,24},{16,0},{24,8},{1,17},{9,25},{17,1},{25,9},{2,18},{10... | collective-permute-start | bytes 491528 | tf_op jit(solution)/shard_map/ppermute | solution.py:290
  301.3 10.6 %collective-permute-start.23 = (bf16[128,640]{1,0:T(8,128)(2,1)S(1)}, bf16[128,640]{1,0:T(8,128)(2,1)S(1)}, u32[]{:S(2)}, u32[]{:S(2)}) collective-permute-start(bf16[128,640]{1,0:T(8,128)(2,1)S(1)} %fusion.17), channel_id=1, source_target_pairs={{0,8},{8,0},{16,24},{24,16},{1,9},{9,1},{17,25},{25,17},{2,10},{10... | collective-permute-start | bytes 491528 | tf_op jit(solution)/shard_map/ppermute | solution.py:290
  327.3 1.1 copy-start.6
  (4 other events, 3.4 us)
Sparse Core Ops, SparseCore 0:
  11.1 97.7 all-gather.4
  110.5 107.0 all-gather.6
  219.9 43.0 reduce-scatter.2
  267.2 58.8 reduce-scatter.4

commit v8 on v7

--- a/solution.py
+++ b/solution.py
@@ -16,7 +16,7 @@
 COLS = 256
 VMEM_BYTES = 52 * 1024 * 1024
 COST = pl.CostEstimate(flops=20_000_000_000, bytes_accessed=36_000_000, transcendentals=0)
-SPLIT = ((512, 288), (512, 0))
+SPLIT = ((480, 308), (544, 0))
 
 
 def dot_nn(left, right):

time: 339 us -> 348 us (1.027)
  waiting for transfers between devices: 141 us -> 146 us
    ppermute x18, waiting for transfers between devices: 49.3 us -> 57.8 us  [send(): return lax.ppermute(value, 'col', lane_pairs(pairs))]
    all_gather x2, waiting for transfers between devices: 69.6 us -> 62.7 us  [local(): gathered.append(lax.all_gather(both, 'col', axis=0))]
    ppermute x4, waiting for transfers between devices: 1.96 us -> 6.4 us  [sum_rows(): lax.ppermute(piece.astype(BF16), 'row', [(i, i ^ bit) for i in range(rows)])]
    ppermute x3, waiting for transfers between devices: 5.52 us -> 2.01 us  [sum_rows_at_once(): lax.ppermute(value, 'row', [(i, i ^ other) for i in range(rows)])]
  transfers between devices with their start and end apart: 34 -> 34, of which waited for: 17 -> 21; matrix products, arithmetic and copies ran while one was open for 12% -> 12% of each run, Pallas kernels for 27% -> 26%
where the time goes in v8:
time: 348 us; the launch traced here: 342 us
  waiting for transfers between devices  146 us (42%)
  Pallas kernels  90.5 us (26%)
  other arithmetic  41.3 us (12%)
  starting transfers between devices  40.4 us (12%)
  between operations  14.3 us (4%)
  local copies, waits for them, and re-layouts  7.77 us (2%)
    all_gather x2, waiting for transfers between devices, local(): gathered.append(lax.all_gather(both, 'col', axis=0))  62.7 us
    pallas_call x2, Pallas kernels, hidden_call(): pl.pallas_call(functools.partial(hidden_kernel, ff), grid=(devices,), in_...  60.3 us
    ppermute x18, waiting for transfers between devices, send(): return lax.ppermute(value, 'col', lane_pairs(pairs))  57.8 us
    ppermute x18, starting transfers between devices, send(): return lax.ppermute(value, 'col', lane_pairs(pairs))  30.8 us
    pallas_call x2, Pallas kernels, share_call(): pl.pallas_call(functools.partial(share_kernel, first), grid_spec=pltpu.Pr...  30.2 us
    concatenate x1, other arithmetic, local(): jnp.concatenate([inner_weight.T, blank, inner_down.T, outer_weight.T, bla...  25.6 us
    reduce_scatter x2, waiting for transfers between devices, local(): far.append(lax.psum_scatter(share, 'col', scatter_dimension=0))  14.7 us
  transfers between devices with their start and end apart: 34, of which 21 were waited for; matrix products, arithmetic and copies ran while one was open for 12% of the time, Pallas kernels for 26%

profile of v8, /device:TPU:8, one launch (start us, length us, event | category | flops | bytes accessed | tf_op | source)
XLA Modules:
  0.0 342.0 jit_solution(4650059829950987137)
XLA Ops:
  9.1 1.2 fusion.9
  10.3 1.2 pad_maximum_fusion.2
  13.0 1.2 pad_maximum_fusion.1
  15.8 25.6 %pad_maximum_fusion.weight_ref = bf16[3584,5120]{1,0:T(8,128)(2,1)} fusion(bf16[64,5120]{1,0:T(8,128)(2,1)S(1)} %copy-done.14, bf16[1728,5120]{1,0:T(8,128)(2,1)} %bitcast.46, bf16[64,5120]{1,0:T(8,128)(2,1)S(1)} %bitcast.48, bf16[1728,5120]{1,0:T(8,128)(2,1)} %bitcast.47), kind=kLoop, calls=%fused_computation | loop fusion | flops 146800640 | bytes 73400320 | tf_op jit(solution)/shard_map/concatenate | solution.py:326
  41.4 62.7 %all-gather.5.cloned.1.call-done = bf16[16,480,640]{2,1,0:T(8,128)(2,1)} async-done(((bf16[2,480,640]{2,1,0:T(8,128)(2,1)}), bf16[16,480,640]{2,1,0:T(8,128)(2,1)}) %all-gather.5.cloned.1.call-update) | async-done | bytes 9830416 | tf_op jit(solution)/shard_map/all_gather | solution.py:321
  104.0 29.3 %shard_map.137 = (bf16[480,1792]{1,0:T(8,128)(2,1)}, bf16[480,128]{1,0:T(8,128)(2,1)S(1)}, f32[128,1792]{1,0:T(8,128)}) custom-call(bf16[8,2,480,640]{3,2,1,0:T(8,128)(2,1)} %bitcast.52, bf16[3584,5120]{1,0:T(8,128)(2,1)} %pad_maximum_fusion.weight_ref, f32[1,1792]{1,0:T(1,128)S(1)} %broadcast_in_dim.8.bias_ref, bf16[128,1792]{1,0:T(8,128)(2,1)S(1)} %pad.16.up_ref, ...), custom_call_target="tpu_custom_call" | custom-call | flops 20000000000 | bytes 36000000 | tf_op jit(solution)/shard_map/pallas_call | solution.py:102
  133.3 14.6 %shard_map.138 = (bf16[8,336,640]{2,1,0:T(8,128)(2,1)}, bf16[4,144,640]{2,1,0:T(8,128)(2,1)S(1)}, bf16[4,144,640]{2,1,0:T(8,128)(2,1)}) custom-call(s32[2]{0:T(128)S(1)} %pad_add_fusion.place_ref, bf16[480,1792]{1,0:T(8,128)(2,1)} %get-tuple-element.14.grad_ref, bf16[3584,5120]{1,0:T(8,128)(2,1)} %pad_maximum_fusion.weight_ref), custom_call_target="tpu_custom_call" | custom-call | flops 20000000000 | bytes 36000000 | tf_op jit(solution)/shard_map/pallas_call | solution.py:167
  148.5 1.6 collective-permute-done.7
  151.0 1.3 collective-permute-start.1
  153.0 1.3 collective-permute-start.11
  154.3 1.3 collective-permute-start.4
  155.6 1.3 collective-permute-start.8
  156.9 8.6 %collective-permute-done.1 = bf16[144,640]{1,0:T(8,128)(2,1)} collective-permute-done((bf16[144,640]{1,0:T(8,128)(2,1)S(1)}, bf16[144,640]{1,0:T(8,128)(2,1)}, u32[]{:S(2)}, u32[]{:S(2)}) %collective-permute-start.1) | collective-permute-done | bytes 184352 | tf_op jit(solution)/shard_map/ppermute | solution.py:201
  166.6 2.2 collective-permute-start.2
  168.8 2.1 collective-permute-done.11
  170.8 1.5 add_convert_fusion.6
  172.3 7.0 %collective-permute-done.2 = bf16[144,640]{1,0:T(8,128)(2,1)S(1)} collective-permute-done((bf16[144,640]{1,0:T(8,128)(2,1)S(1)}, bf16[144,640]{1,0:T(8,128)(2,1)S(1)}, u32[]{:S(2)}, u32[]{:S(2)}) %collective-permute-start.2) | collective-permute-done | bytes 184352 | tf_op jit(solution)/shard_map/ppermute | solution.py:201
  179.4 1.8 fusion.13
  181.2 6.9 %collective-permute-start.9 = (bf16[240,128]{1,0:T(8,128)(2,1)}, bf16[240,128]{1,0:T(8,128)(2,1)S(1)}, u32[]{:S(2)}, u32[]{:S(2)}) collective-permute-start(bf16[240,128]{1,0:T(8,128)(2,1)} %shard_map.140), channel_id=1, source_target_pairs={{2,4},{3,5},{10,12},{11,13},{18,20},{19,21},{26,28},{27,29}} | collective-permute-start | bytes 184328 | tf_op jit(solution)/shard_map/ppermute | solution.py:201
  188.1 1.3 collective-permute-start.13
  189.4 1.3 collective-permute-start.5
  190.7 1.3 collective-permute-done.9
  192.6 15.7 %collective-permute-done.5 = bf16[144,640]{1,0:T(8,128)(2,1)S(1)} collective-permute-done((bf16[144,640]{1,0:T(8,128)(2,1)}, bf16[144,640]{1,0:T(8,128)(2,1)S(1)}, u32[]{:S(2)}, u32[]{:S(2)}) %collective-permute-start.5) | collective-permute-done | bytes 184352 | tf_op jit(solution)/shard_map/ppermute | solution.py:201
  210.9 4.0 %collective-permute-start.3 = (bf16[144,640]{1,0:T(8,128)(2,1)S(1)}, bf16[144,640]{1,0:T(8,128)(2,1)S(1)}, u32[]{:S(2)}, u32[]{:S(2)}) collective-permute-start(bf16[144,640]{1,0:T(8,128)(2,1)S(1)} %copy-done), channel_id=1, source_target_pairs={{0,2},{1,3},{2,4},{3,5},{4,6},{5,7},{8,10},{9,11},{10,12},{11,13},... | collective-permute-start | bytes 552968 | tf_op jit(solution)/shard_map/ppermute | solution.py:201
  214.9 1.9 collective-permute-start.6
  216.9 3.3 collective-permute-done.3
  220.2 4.1 %collective-permute-done.6 = bf16[144,640]{1,0:T(8,128)(2,1)S(1)} collective-permute-done((bf16[144,640]{1,0:T(8,128)(2,1)}, bf16[144,640]{1,0:T(8,128)(2,1)S(1)}, u32[]{:S(2)}, u32[]{:S(2)}) %collective-permute-start.6) | collective-permute-done | bytes 184352 | tf_op jit(solution)/shard_map/ppermute | solution.py:201
  225.3 31.0 %shard_map.142 = (bf16[544,1792]{1,0:T(8,128)(2,1)}, bf16[544,128]{1,0:T(8,128)(2,1)S(1)}, f32[128,1792]{1,0:T(8,128)}) custom-call(bf16[8,2,544,640]{3,2,1,0:T(8,128)(2,1)} %bitcast.51, bf16[3584,5120]{1,0:T(8,128)(2,1)} %pad_maximum_fusion.weight_ref, f32[1,1792]{1,0:T(1,128)S(1)} %broadcast_in_dim.8.bias_ref, bf16[128,1792]{1,0:T(8,128)(2,1)S(1)} %pad.16.up_ref, ...), custom_call_target="tpu_custom_call" | custom-call | flops 20000000000 | bytes 36000000 | tf_op jit(solution)/shard_map/pallas_call | solution.py:102
  256.3 15.6 %shard_map.143 = bf16[8,544,640]{2,1,0:T(8,128)(2,1)} custom-call(s32[2]{0:T(128)S(1)} %pad_add_fusion.place_ref, bf16[544,1792]{1,0:T(8,128)(2,1)} %get-tuple-element.19.grad_ref, bf16[3584,5120]{1,0:T(8,128)(2,1)} %pad_maximum_fusion.weight_ref, bf16[480,128]{1,0:T(8,128)(2,1)S(1)} %pad_maximum_fusion.3.refs_0_, bf16[144,640]{1,0:T(8,128)(2,1)S(1)} %fusion.15.refs_1_), custom_call_target="tpu_custom_call" | custom-call | flops 20000000000 | bytes 36000000 | tf_op jit(solution)/shard_map/pallas_call | solution.py:167
  272.2 1.2 collective-permute-done.15
  273.4 1.4 collective-permute-start.16
  275.8 4.9 %collective-permute-done.16 = bf16[272,128]{1,0:T(8,128)(2,1)S(1)} collective-permute-done((bf16[272,128]{1,0:T(8,128)(2,1)S(1)}, bf16[272,128]{1,0:T(8,128)(2,1)S(1)}, u32[]{:S(2)}, u32[]{:S(2)}) %collective-permute-start.16) | collective-permute-done | bytes 69664 | tf_op jit(solution)/shard_map/ppermute | solution.py:201
  280.7 1.3 collective-permute-start.17
  282.3 3.4 collective-permute-done.17
  285.7 1.3 collective-permute-start.20
  287.8 6.8 %collective-permute-done.20 = bf16[272,128]{1,0:T(8,128)(2,1)S(1)} collective-permute-done((bf16[272,128]{1,0:T(8,128)(2,1)S(1)}, bf16[272,128]{1,0:T(8,128)(2,1)S(1)}, u32[]{:S(2)}, u32[]{:S(2)}) %collective-permute-start.20) | collective-permute-done | bytes 69664 | tf_op jit(solution)/shard_map/ppermute | solution.py:201
  294.7 1.3 collective-permute-start.21
  296.1 1.6 collective-permute-start.28
  297.6 1.5 collective-permute-start.26
  299.9 2.2 collective-permute-done.28
  302.2 1.5 collective-permute-done.26
  304.4 1.5 collective-permute-start.29
  306.6 1.6 collective-permute-start.25
  308.6 1.5 collective-permute-start.23
  310.1 2.6 collective-permute-done.27
  317.3 1.3 maximum_maximum_fusion
  318.5 14.7 %reduce-scatter.5.cloned.1.call-done = bf16[1,544,640]{2,1,0:T(8,128)(2,1)} async-done(((bf16[8,544,640]{2,1,0:T(8,128)(2,1)}), bf16[1,544,640]{2,1,0:T(8,128)(2,1)}) %reduce-scatter.5.cloned.1.call-update) | async-done | bytes 696336 | tf_op jit(solution)/shard_map/reduce_scatter | solution.py:353
  333.2 1.2 bitcast_dynamic-update-slice_fusion
  (120 shorter events, 23.0 us)
Async XLA Ops:
  7.2 96.9 %all-gather.5.cloned.1.call-start = ((), (), s32[]{:S(2)}) async-start(), calls=%async_computation.4 | async-start | bytes 11059200 | tf_op jit(solution)/shard_map/all_gather | solution.py:321
  10.3 1.8 copy-start.3
  11.5 213.8 %all-gather.7.cloned.1.call-start = ((), (), s32[]{:S(2)}) async-start(), calls=%async_computation.5 | async-start | bytes 12533760 | tf_op jit(solution)/shard_map/all_gather | solution.py:321
  14.3 1.5 copy-start.15
  14.3 302.9 %reduce-scatter.3.cloned.1.call-start = ((), (), s32[]{:S(2)}) async-start(), calls=%async_computation.2 | async-start | bytes 3870720 | tf_op jit(solution)/shard_map/reduce_scatter | solution.py:353
  147.9 3.0 collective-permute-start
  148.2 185.1 %reduce-scatter.5.cloned.1.call-start = ((), (), s32[]{:S(2)}) async-start(), calls=%async_computation.3 | async-start | bytes 6266880 | tf_op jit(solution)/shard_map/reduce_scatter | solution.py:353
  148.2 1.9 collective-permute-start.7
  150.2 5.4 %copy-start.16 = (bf16[240,128]{1,0:T(8,128)(2,1)}, bf16[240,128]{1,0:T(8,128)(2,1)S(1)}, u32[]{:S(2)}) copy-start(bf16[240,128]{1,0:T(8,128)(2,1)S(1)} %get-tuple-element.25.refs_0_) | copy-start | bytes 184324
  150.2 2.1 collective-permute-start.10
  150.9 57.4 %copy-start.5 = (bf16[4,144,640]{2,1,0:T(8,128)(2,1)}, bf16[4,144,640]{2,1,0:T(8,128)(2,1)S(1)}, u32[]{:S(2)}) copy-start(bf16[4,144,640]{2,1,0:T(8,128)(2,1)S(1)} %collective-permute-done) | copy-start | bytes 2211844
  151.0 4.6 %copy-start.11 = (bf16[144,640]{1,0:T(8,128)(2,1)}, bf16[144,640]{1,0:T(8,128)(2,1)S(1)}, u32[]{:S(2)}) copy-start(bf16[144,640]{1,0:T(8,128)(2,1)S(1)} %get-tuple-element.30.refs_2_) | copy-start | bytes 552964
  151.0 4.6 %copy-start.13 = (bf16[144,640]{1,0:T(8,128)(2,1)}, bf16[144,640]{1,0:T(8,128)(2,1)S(1)}, u32[]{:S(2)}) copy-start(bf16[144,640]{1,0:T(8,128)(2,1)S(1)} %get-tuple-element.29.refs_1_) | copy-start | bytes 552964
  151.0 14.5 %collective-permute-start.1 = (bf16[144,640]{1,0:T(8,128)(2,1)S(1)}, bf16[144,640]{1,0:T(8,128)(2,1)}, u32[]{:S(2)}, u32[]{:S(2)}) collective-permute-start(bf16[144,640]{1,0:T(8,128)(2,1)S(1)} %get-tuple-element.29.refs_1_), channel_id=1, source_target_pairs={{0,2},{1,3},{8,10},{9,11},{16,18},{17,19},{24,26},{25,27}} | collective-permute-start | bytes 552968 | tf_op jit(solution)/shard_map/ppermute | solution.py:201
  153.0 17.8 %collective-permute-start.11 = (bf16[240,128]{1,0:T(8,128)(2,1)}, bf16[240,128]{1,0:T(8,128)(2,1)}, u32[]{:S(2)}, u32[]{:S(2)}) collective-permute-start(bf16[240,128]{1,0:T(8,128)(2,1)} %fusion.27), channel_id=1, source_target_pairs={{4,2},{5,3},{12,10},{13,11},{20,18},{21,19},{28,26},{29,27}} | collective-permute-start | bytes 184328 | tf_op jit(solution)/shard_map/ppermute | solution.py:201
  154.3 18.0 %collective-permute-start.4 = (bf16[144,640]{1,0:T(8,128)(2,1)S(1)}, bf16[144,640]{1,0:T(8,128)(2,1)}, u32[]{:S(2)}, u32[]{:S(2)}) collective-permute-start(bf16[144,640]{1,0:T(8,128)(2,1)S(1)} %get-tuple-element.30.refs_2_), channel_id=1, source_target_pairs={{6,4},{7,5},{14,12},{15,13},{22,20},{23,21},{30,28},{31,29}} | collective-permute-start | bytes 552968 | tf_op jit(solution)/shard_map/ppermute | solution.py:201
  155.6 15.2 %collective-permute-start.8 = (bf16[240,128]{1,0:T(8,128)(2,1)}, bf16[240,128]{1,0:T(8,128)(2,1)S(1)}, u32[]{:S(2)}, u32[]{:S(2)}) collective-permute-start(bf16[240,128]{1,0:T(8,128)(2,1)} %shard_map.139), channel_id=1, source_target_pairs={{0,2},{1,3},{8,10},{9,11},{16,18},{17,19},{24,26},{25,27}} | collective-permute-start | bytes 184328 | tf_op jit(solution)/shard_map/ppermute | solution.py:201
  166.6 14.6 %copy-start.12 = (bf16[144,640]{1,0:T(8,128)(2,1)}, bf16[144,640]{1,0:T(8,128)(2,1)S(1)}, u32[]{:S(2)}) copy-start(bf16[144,640]{1,0:T(8,128)(2,1)S(1)} %fusion.11.refs_1_) | copy-start | bytes 552964
  166.6 12.8 %collective-permute-start.2 = (bf16[144,640]{1,0:T(8,128)(2,1)S(1)}, bf16[144,640]{1,0:T(8,128)(2,1)S(1)}, u32[]{:S(2)}, u32[]{:S(2)}) collective-permute-start(bf16[144,640]{1,0:T(8,128)(2,1)S(1)} %fusion.11.refs_1_), channel_id=1, source_target_pairs={{0,2},{1,3},{2,4},{3,5},{8,10},{9,11},{10,12},{11,13},{16,18},{17,... | collective-permute-start | bytes 552968 | tf_op jit(solution)/shard_map/ppermute | solution.py:201
  181.2 29.7 %copy-start = (bf16[144,640]{1,0:T(8,128)(2,1)S(1)}, bf16[144,640]{1,0:T(8,128)(2,1)}, u32[]{:S(2)}) copy-start(bf16[144,640]{1,0:T(8,128)(2,1)} %get-tuple-element.27.refs_1_.refs_0_) | copy-start | bytes 552964
  181.2 10.8 %collective-permute-start.9 = (bf16[240,128]{1,0:T(8,128)(2,1)}, bf16[240,128]{1,0:T(8,128)(2,1)S(1)}, u32[]{:S(2)}, u32[]{:S(2)}) collective-permute-start(bf16[240,128]{1,0:T(8,128)(2,1)} %shard_map.140), channel_id=1, source_target_pairs={{2,4},{3,5},{10,12},{11,13},{18,20},{19,21},{26,28},{27,29}} | collective-permute-start | bytes 184328 | tf_op jit(solution)/shard_map/ppermute | solution.py:201
  188.1 21.8 %collective-permute-start.13 = (bf16[240,128]{1,0:T(8,128)(2,1)S(1)}, bf16[240,128]{1,0:T(8,128)(2,1)S(1)}, u32[]{:S(2)}, u32[]{:S(2)}) collective-permute-start(bf16[240,128]{1,0:T(8,128)(2,1)S(1)} %get-tuple-element.45.refs_3_), channel_id=1, source_target_pairs={{2,0},{3,1},{10,8},{11,9},{18,16},{19,17},{26,24},{27,25}} | collective-permute-start | bytes 184328 | tf_op jit(solution)/shard_map/ppermute | solution.py:201
  189.4 18.9 %collective-permute-start.5 = (bf16[144,640]{1,0:T(8,128)(2,1)}, bf16[144,640]{1,0:T(8,128)(2,1)S(1)}, u32[]{:S(2)}, u32[]{:S(2)}) collective-permute-start(bf16[144,640]{1,0:T(8,128)(2,1)} %get-tuple-element.28.refs_2_), channel_id=1, source_target_pairs={{4,2},{5,3},{6,4},{7,5},{12,10},{13,11},{14,12},{15,13},{20,18},{2... | collective-permute-start | bytes 552968 | tf_op jit(solution)/shard_map/ppermute | solution.py:201
  209.1 16.3 %copy-start.1 = (bf16[144,640]{1,0:T(8,128)(2,1)S(1)}, bf16[144,640]{1,0:T(8,128)(2,1)}, u32[]{:S(2)}) copy-start(bf16[144,640]{1,0:T(8,128)(2,1)} %fusion.10.refs_2_.refs_1_) | copy-start | bytes 552964
  209.1 16.3 %copy-start.2 = (bf16[240,128]{1,0:T(8,128)(2,1)S(1)}, bf16[240,128]{1,0:T(8,128)(2,1)}, u32[]{:S(2)}) copy-start(bf16[240,128]{1,0:T(8,128)(2,1)} %shard_map.141.refs_2_) | copy-start | bytes 184324
  209.1 0.8 collective-permute-start.12
  210.8 6.0 %collective-permute-start.14 = (bf16[240,128]{1,0:T(8,128)(2,1)S(1)}, bf16[240,128]{1,0:T(8,128)(2,1)S(1)}, u32[]{:S(2)}, u32[]{:S(2)}) collective-permute-start(bf16[240,128]{1,0:T(8,128)(2,1)S(1)} %add_convert_fusion.5), channel_id=1, source_target_pairs={{0,1},{1,0},{2,3},{3,2},{4,5},{5,4},{6,7},{7,6},{8,9},{9,8},{10,11... | collective-permute-start | bytes 184328 | tf_op jit(solution)/shard_map/ppermute | solution.py:205
  210.9 9.3 %collective-permute-start.3 = (bf16[144,640]{1,0:T(8,128)(2,1)S(1)}, bf16[144,640]{1,0:T(8,128)(2,1)S(1)}, u32[]{:S(2)}, u32[]{:S(2)}) collective-permute-start(bf16[144,640]{1,0:T(8,128)(2,1)S(1)} %copy-done), channel_id=1, source_target_pairs={{0,2},{1,3},{2,4},{3,5},{4,6},{5,7},{8,10},{9,11},{10,12},{11,13},... | collective-permute-start | bytes 552968 | tf_op jit(solution)/shard_map/ppermute | solution.py:201
  214.9 9.4 %collective-permute-start.6 = (bf16[144,640]{1,0:T(8,128)(2,1)}, bf16[144,640]{1,0:T(8,128)(2,1)S(1)}, u32[]{:S(2)}, u32[]{:S(2)}) collective-permute-start(bf16[144,640]{1,0:T(8,128)(2,1)} %fusion.10.refs_2_.refs_1_), channel_id=1, source_target_pairs={{2,0},{3,1},{4,2},{5,3},{6,4},{7,5},{10,8},{11,9},{12,10},{13,11},... | collective-permute-start | bytes 552968 | tf_op jit(solution)/shard_map/ppermute | solution.py:201
  272.0 2.9 copy-start.8
  272.0 10.0 %copy-start.4 = (bf16[1024,640]{1,0:T(8,128)(2,1)S(1)}, bf16[1024,640]{1,0:T(8,128)(2,1)}, u32[]{:S(2)}) copy-start(bf16[1024,640]{1,0:T(8,128)(2,1)} %param.10) | copy-start | bytes 3932164
  272.0 1.3 collective-permute-start.15
  273.4 13.7 %copy-start.9 = (f32[128,1792]{1,0:T(8,128)S(1)}, f32[128,1792]{1,0:T(8,128)}, u32[]{:S(2)}) copy-start(f32[128,1792]{1,0:T(8,128)} %get-tuple-element.21) | copy-start | bytes 2752516
  273.4 13.7 %copy-start.10 = (f32[128,1792]{1,0:T(8,128)S(1)}, f32[128,1792]{1,0:T(8,128)}, u32[]{:S(2)}) copy-start(f32[128,1792]{1,0:T(8,128)} %get-tuple-element.22) | copy-start | bytes 2752516
  273.4 7.2 %collective-permute-start.16 = (bf16[272,128]{1,0:T(8,128)(2,1)S(1)}, bf16[272,128]{1,0:T(8,128)(2,1)S(1)}, u32[]{:S(2)}, u32[]{:S(2)}) collective-permute-start(bf16[272,128]{1,0:T(8,128)(2,1)S(1)} %get-tuple-element.23), channel_id=1, source_target_pairs={{0,2},{1,3},{8,10},{9,11},{16,18},{17,19},{24,26},{25,27}} | collective-permute-start | bytes 208904 | tf_op jit(solution)/shard_map/ppermute | solution.py:201
  275.1 7.2 %collective-permute-start.19 = (bf16[272,128]{1,0:T(8,128)(2,1)S(1)}, bf16[272,128]{1,0:T(8,128)(2,1)S(1)}, u32[]{:S(2)}, u32[]{:S(2)}) collective-permute-start(bf16[272,128]{1,0:T(8,128)(2,1)S(1)} %get-tuple-element.23), channel_id=1, source_target_pairs={{6,4},{7,5},{14,12},{15,13},{22,20},{23,21},{30,28},{31,29}} | collective-permute-start | bytes 208904 | tf_op jit(solution)/shard_map/ppermute | solution.py:201
  280.7 5.0 %collective-permute-start.17 = (bf16[272,128]{1,0:T(8,128)(2,1)S(1)}, bf16[272,128]{1,0:T(8,128)(2,1)S(1)}, u32[]{:S(2)}, u32[]{:S(2)}) collective-permute-start(bf16[272,128]{1,0:T(8,128)(2,1)S(1)} %fusion.18), channel_id=1, source_target_pairs={{2,4},{3,5},{10,12},{11,13},{18,20},{19,21},{26,28},{27,29}} | collective-permute-start | bytes 208904 | tf_op jit(solution)/shard_map/ppermute | solution.py:201
  285.7 8.9 %collective-permute-start.20 = (bf16[272,128]{1,0:T(8,128)(2,1)S(1)}, bf16[272,128]{1,0:T(8,128)(2,1)S(1)}, u32[]{:S(2)}, u32[]{:S(2)}) collective-permute-start(bf16[272,128]{1,0:T(8,128)(2,1)S(1)} %get-tuple-element.42), channel_id=1, source_target_pairs={{4,2},{5,3},{12,10},{13,11},{20,18},{21,19},{28,26},{29,27}} | collective-permute-start | bytes 208904 | tf_op jit(solution)/shard_map/ppermute | solution.py:201
  287.2 11.9 %collective-permute-start.18 = (bf16[272,128]{1,0:T(8,128)(2,1)S(1)}, bf16[272,128]{1,0:T(8,128)(2,1)S(1)}, u32[]{:S(2)}, u32[]{:S(2)}) collective-permute-start(bf16[272,128]{1,0:T(8,128)(2,1)S(1)} %get-tuple-element.41), channel_id=1, source_target_pairs={{4,6},{5,7},{12,14},{13,15},{20,22},{21,23},{28,30},{29,31}} | collective-permute-start | bytes 208904 | tf_op jit(solution)/shard_map/ppermute | solution.py:201
  294.7 5.0 %collective-permute-start.21 = (bf16[272,128]{1,0:T(8,128)(2,1)S(1)}, bf16[272,128]{1,0:T(8,128)(2,1)S(1)}, u32[]{:S(2)}, u32[]{:S(2)}) collective-permute-start(bf16[272,128]{1,0:T(8,128)(2,1)S(1)} %add_convert_fusion.3), channel_id=1, source_target_pairs={{2,0},{3,1},{10,8},{11,9},{18,16},{19,17},{26,24},{27,25}} | collective-permute-start | bytes 208904 | tf_op jit(solution)/shard_map/ppermute | solution.py:201
  296.1 6.1 %collective-permute-start.28 = (bf16[64,1728]{1,0:T(8,128)(2,1)S(1)}, bf16[64,1728]{1,0:T(8,128)(2,1)S(1)}, u32[]{:S(2)}, u32[]{:S(2)}) collective-permute-start(bf16[64,1728]{1,0:T(8,128)(2,1)S(1)} %get-tuple-element.33), channel_id=1, source_target_pairs={{0,16},{8,24},{16,0},{24,8},{1,17},{9,25},{17,1},{25,9},{2,18},{10... | collective-permute-start | bytes 663560 | tf_op jit(solution)/shard_map/ppermute | solution.py:279
  297.6 6.0 %collective-permute-start.26 = (bf16[64,1728]{1,0:T(8,128)(2,1)S(1)}, bf16[64,1728]{1,0:T(8,128)(2,1)S(1)}, u32[]{:S(2)}, u32[]{:S(2)}) collective-permute-start(bf16[64,1728]{1,0:T(8,128)(2,1)S(1)} %get-tuple-element.34), channel_id=1, source_target_pairs={{0,8},{8,0},{16,24},{24,16},{1,9},{9,1},{17,25},{25,17},{2,10},{10... | collective-permute-start | bytes 663560 | tf_op jit(solution)/shard_map/ppermute | solution.py:279
  299.8 6.0 %collective-permute-start.22 = (bf16[272,128]{1,0:T(8,128)(2,1)S(1)}, bf16[272,128]{1,0:T(8,128)(2,1)S(1)}, u32[]{:S(2)}, u32[]{:S(2)}) collective-permute-start(bf16[272,128]{1,0:T(8,128)(2,1)S(1)} %add_convert_fusion.2), channel_id=1, source_target_pairs={{0,1},{1,0},{2,3},{3,2},{4,5},{5,4},{6,7},{7,6},{8,9},{9,8},{10,11... | collective-permute-start | bytes 208904 | tf_op jit(solution)/shard_map/ppermute | solution.py:205
  303.8 9.0 %collective-permute-start.27 = (bf16[64,1728]{1,0:T(8,128)(2,1)S(1)}, bf16[64,1728]{1,0:T(8,128)(2,1)S(1)}, u32[]{:S(2)}, u32[]{:S(2)}) collective-permute-start(bf16[64,1728]{1,0:T(8,128)(2,1)S(1)} %get-tuple-element.32), channel_id=1, source_target_pairs={{0,16},{8,24},{16,0},{24,8},{1,17},{9,25},{17,1},{25,9},{2,18},{10... | collective-permute-start | bytes 663560 | tf_op jit(solution)/shard_map/ppermute | solution.py:279
  304.4 9.2 %collective-permute-start.29 = (bf16[64,1728]{1,0:T(8,128)(2,1)S(1)}, bf16[64,1728]{1,0:T(8,128)(2,1)S(1)}, u32[]{:S(2)}, u32[]{:S(2)}) collective-permute-start(bf16[64,1728]{1,0:T(8,128)(2,1)S(1)} %get-tuple-element.31), channel_id=1, source_target_pairs={{0,8},{8,0},{16,24},{24,16},{1,9},{9,1},{17,25},{25,17},{2,10},{10... | collective-permute-start | bytes 663560 | tf_op jit(solution)/shard_map/ppermute | solution.py:279
  306.6 8.6 %collective-permute-start.25 = (bf16[128,640]{1,0:T(8,128)(2,1)S(1)}, bf16[128,640]{1,0:T(8,128)(2,1)S(1)}, u32[]{:S(2)}, u32[]{:S(2)}) collective-permute-start(bf16[128,640]{1,0:T(8,128)(2,1)S(1)} %fusion.17), channel_id=1, source_target_pairs={{0,24},{8,16},{16,8},{24,0},{1,25},{9,17},{17,9},{25,1},{2,26},{10... | collective-permute-start | bytes 491528 | tf_op jit(solution)/shard_map/ppermute | solution.py:290
  308.1 8.1 %collective-permute-start.24 = (bf16[128,640]{1,0:T(8,128)(2,1)S(1)}, bf16[128,640]{1,0:T(8,128)(2,1)S(1)}, u32[]{:S(2)}, u32[]{:S(2)}) collective-permute-start(bf16[128,640]{1,0:T(8,128)(2,1)S(1)} %fusion.17), channel_id=1, source_target_pairs={{0,16},{8,24},{16,0},{24,8},{1,17},{9,25},{17,1},{25,9},{2,18},{10... | collective-permute-start | bytes 491528 | tf_op jit(solution)/shard_map/ppermute | solution.py:290
  308.6 7.8 %collective-permute-start.23 = (bf16[128,640]{1,0:T(8,128)(2,1)S(1)}, bf16[128,640]{1,0:T(8,128)(2,1)S(1)}, u32[]{:S(2)}, u32[]{:S(2)}) collective-permute-start(bf16[128,640]{1,0:T(8,128)(2,1)S(1)} %fusion.17), channel_id=1, source_target_pairs={{0,8},{8,0},{16,24},{24,16},{1,9},{9,1},{17,25},{25,17},{2,10},{10... | collective-permute-start | bytes 491528 | tf_op jit(solution)/shard_map/ppermute | solution.py:290
  (6 other events, 6.5 us)
Sparse Core Ops, SparseCore 0:
  11.6 92.3 all-gather.4
  105.7 112.5 all-gather.6
  220.6 39.5 reduce-scatter.2
  272.1 61.0 reduce-scatter.4
